TPU v7x, 32 devices: a whole 2x2x4 slice. The times are simulated.
32 devices in a mesh: seq: 4 (over y, x), head: 8 (over z, core).
Axes of the slice: x: 2, y: 2, z: 4, core: 2. Of those that a mesh axis runs over, the one named last changes fastest.
Arguments:
- hidden: bfloat16 [8, 2048, 2048], P('head', 'seq'), may hold values from -6 to 6
- lengths: int32 [8], P('head'), may hold values from 512 to 2048, as said below
- out_grad: bfloat16 [8, 2048, 2048], P('head', 'seq'), may hold values from -6 to 6
- norm_gain: bfloat16 [2048], P('head'), may hold values from 0.5 to 1.5
- w_in: bfloat16 [2048, 8448], P('head'), may hold values from -0.125 to 0.125
- w_dt: bfloat16 [2048, 64], P('head'), may hold values from -0.125 to 0.125
- conv_weight: bfloat16 [4, 4352], P(None, 'head'), may hold values from -3 to 3
- conv_bias: bfloat16 [4352], P('head'), may hold values from -0.5 to 0.5
- dt_bias: bfloat16 [64], P('head'), may hold values from -4 to -2
- a_log: bfloat16 [64], P('head'), may hold values from -6 to 0
- skip_gain: bfloat16 [64], P('head'), may hold values from 0.5 to 1.5
- gate_gain: bfloat16 [4096], P('head'), may hold values from 0.5 to 1.5
- w_out: bfloat16 [4096, 2048], P('head'), may hold values from -0.09375 to 0.09375
Outputs:
- block_out: bfloat16 [8, 2048, 2048], P('head', 'seq')
- hidden_grad: float32 [8, 2048, 2048], P('head', 'seq')
- norm_gain_grad: float32 [2048], P('head')
- w_in_grad: float32 [2048, 8448], P('head')
- w_dt_grad: float32 [2048, 64], P('head')
- conv_weight_grad: float32 [4, 4352], P(None, 'head')
- conv_bias_grad: float32 [4352], P('head')
- dt_bias_grad: float32 [64], P('head')
- a_log_grad: float32 [64], P('head')
- skip_grad: float32 [64], P('head')
- gate_gain_grad: float32 [4096], P('head')
- w_out_grad: float32 [4096, 2048], P('head')
Inputs may be any that keep to these rules, and one draw needn't show every extreme that they name: lengths of the buckets; some bucket has exactly 2048.
All inputs are finite; a program needn't handle non-finite values.
Results may differ from a plain program's by a relative error of at most 0.02.
Values may be sent and summed in bfloat16 or wider, within the bound.
A program may use at most 512 MiB of HBM per device.

v0:
```python
import jax
import jax.numpy as jnp
from jax import lax
from jax.sharding import PartitionSpec as P

HEADS = 64
HEAD_DIM = 64
STATE = 128
KERNEL = 4
SPAN = 256
DI = 4096
CHANNELS = 4352


EPS = 1e-05
SCAN_PREC = lax.Precision.HIGH


def shifted(array, axis, by):
    peers = lax.axis_size(axis)
    pairs = [(i, i + by) for i in range(peers) if 0 <= i + by < peers]
    return lax.ppermute(array, axis, pairs)


def prefix(array, axis, combine, identity, reverse):
    peers, index = (lax.axis_size(axis), lax.axis_index(axis))
    everything = jax.tree.map(
        lambda part, kind: lax.all_gather(part.astype(kind), axis),
        array,
        jax.tree.map(lambda a: jnp.bfloat16 if a.dtype == jnp.float32 else a.dtype, array),
    )
    start = jax.tree.map(
        lambda part, zero: jnp.broadcast_to(jnp.asarray(zero, part.dtype), part.shape),
        array,
        identity,
    )

    def turn(k, before):
        at = peers - 1 - k if reverse else k
        reached = at > index if reverse else at < index
        new = combine(
            before, jax.tree.map(lambda part, own: part[at].astype(own.dtype), everything, array)
        )
        return jax.tree.map(lambda a, b: jnp.where(reached, a, b), new, before)

    return lax.fori_loop(0, peers, turn, start)


def rms_scale(values, gain):
    return values * lax.rsqrt(jnp.mean(values * values, axis=-1, keepdims=True) + EPS) * gain


def silu_slope(values):
    logistic = jax.nn.sigmoid(values)
    return logistic * (1.0 + values * (1.0 - logistic))


def span_step(decay_rate, causal):

    def advance(state_in, pieces):
        x_block, dt_block, b_block, c_block = pieces
        cumulate = jnp.cumsum(dt_block * decay_rate, axis=0)
        spread = cumulate[:, None, :] - cumulate[None, :, :]
        weights = jnp.exp(jnp.where(causal[:, :, None], spread, -jnp.inf))
        scores = jnp.einsum("tn,sn->ts", c_block, b_block, precision=SCAN_PREC)
        scaled = x_block * dt_block[:, :, None]
        inner_part = jnp.einsum(
            "tsh,shp->thp", scores[:, :, None] * weights, scaled, precision=SCAN_PREC
        )
        cross_part = (
            jnp.einsum("tn,hnp->thp", c_block, state_in, precision=SCAN_PREC)
            * jnp.exp(cumulate)[:, :, None]
        )
        tail_decay = jnp.exp(cumulate[-1:, :] - cumulate)
        state_add = jnp.einsum(
            "sn,shp->hnp", b_block, scaled * tail_decay[:, :, None], precision=SCAN_PREC
        )
        renewed = jnp.exp(cumulate[-1, :])[:, None, None] * state_in + state_add
        return (renewed, inner_part + cross_part)

    return advance


def local_scan(x_seq, dt_seq, b_seq, c_seq, a_vals, skip_vals):
    seq_len, head_count, head_width = x_seq.shape
    span_count = seq_len // SPAN
    decay_rate = -jnp.exp(a_vals)
    causal = jnp.tril(jnp.ones((SPAN, SPAN), dtype=jnp.bool_))
    blocks = (
        x_seq.reshape(span_count, SPAN, head_count, head_width),
        dt_seq.reshape(span_count, SPAN, head_count),
        b_seq.reshape(span_count, SPAN, b_seq.shape[1]),
        c_seq.reshape(span_count, SPAN, c_seq.shape[1]),
    )
    zero_state = jnp.zeros((head_count, b_seq.shape[1], head_width), jnp.float32)
    last_state, outputs = lax.scan(span_step(decay_rate, causal), zero_state, blocks)
    results = outputs.reshape(seq_len, head_count, head_width) + skip_vals[None, :, None] * x_seq
    profile = jnp.exp(jnp.cumsum(dt_seq * decay_rate, axis=0))
    return (results, profile[-1], last_state, profile)


def join_states(earlier, later):
    return (earlier[0] * later[0], later[0][..., None, None] * earlier[1] + later[1])


def fetch_weights(shards):
    return (
        lax.all_gather(shards[0], "head", axis=0, tiled=True),
        lax.all_gather(shards[1], "head", axis=0, tiled=True),
        lax.all_gather(shards[2], "head", axis=0, tiled=True),
        lax.all_gather(shards[3], "head", axis=1, tiled=True),
        lax.all_gather(shards[4], "head", axis=0, tiled=True),
        lax.all_gather(shards[5], "head", axis=0, tiled=True),
        lax.all_gather(shards[6], "head", axis=0, tiled=True),
        lax.all_gather(shards[7], "head", axis=0, tiled=True),
        lax.all_gather(shards[8], "head", axis=0, tiled=True),
        lax.all_gather(shards[9], "head", axis=0, tiled=True),
    )


def map_scan(inputs, a_vals, skip_vals):

    def one_seq(pieces):
        x_seq, dt_seq, bc_seq = pieces
        return local_scan(
            x_seq.astype(jnp.float32),
            dt_seq.astype(jnp.float32),
            bc_seq[:, :STATE].astype(jnp.float32),
            bc_seq[:, STATE:].astype(jnp.float32),
            a_vals,
            skip_vals,
        )

    return lax.map(one_seq, inputs, batch_size=8)


def run_forward(hidden, lengths, shards):
    gathered = fetch_weights(shards)
    norm_gain, w_in, w_dt, conv_weight, conv_bias, dt_bias, a_log, skip_gain, gate_gain, w_out = (
        gathered
    )
    seq_dev, local_len, model_width = hidden.shape
    row_count = seq_dev * local_len
    hidden32 = hidden.astype(jnp.float32).reshape(row_count, model_width)
    normed = rms_scale(hidden32, norm_gain.astype(jnp.float32)).astype(jnp.bfloat16)
    projected = jnp.dot(normed, w_in, preferred_element_type=jnp.float32)
    dt_raw = jnp.dot(normed, w_dt, preferred_element_type=jnp.float32)
    conv_in = projected[:, DI:].astype(jnp.bfloat16).reshape(seq_dev, local_len, CHANNELS)
    rim_rows = conv_in[:, local_len - (KERNEL - 1) :, :]
    before = shifted(rim_rows, "seq", 1)
    padded = jnp.concatenate([before, conv_in], axis=1)
    kernel32 = conv_weight.astype(jnp.float32)
    conv_pre = jnp.zeros((seq_dev, local_len, CHANNELS), jnp.float32) + conv_bias.astype(
        jnp.float32
    )
    for shift_by in range(KERNEL):
        conv_pre = conv_pre + kernel32[shift_by] * padded[:, shift_by : shift_by + local_len]
    activated = jax.nn.silu(conv_pre)
    x_tok = activated[..., :DI].astype(jnp.bfloat16).reshape(seq_dev, local_len, HEADS, HEAD_DIM)
    bc_tok = activated[..., DI:].astype(jnp.bfloat16)
    dt_tok = (
        jax.nn.softplus(dt_raw + dt_bias.astype(jnp.float32))
        .astype(jnp.bfloat16)
        .reshape(seq_dev, local_len, HEADS)
    )
    x_heads, dt_heads = (
        lax.all_to_all(x_tok, "head", split_axis=2, concat_axis=0, tiled=True),
        lax.all_to_all(dt_tok, "head", split_axis=2, concat_axis=0, tiled=True),
    )
    bc_heads = lax.all_gather(bc_tok, "head", axis=0, tiled=True)
    head_share = HEADS // lax.axis_size("head")
    offset = lax.axis_index("head") * head_share
    a_vals = lax.dynamic_slice_in_dim(a_log.astype(jnp.float32), offset, head_share)
    skip_vals = lax.dynamic_slice_in_dim(skip_gain.astype(jnp.float32), offset, head_share)
    scanned, totals, finals, profile = map_scan((x_heads, dt_heads, bc_heads), a_vals, skip_vals)
    identity_pair = (jnp.ones_like(totals), jnp.zeros_like(finals))
    _, incoming = prefix((totals, finals), "seq", join_states, identity_pair, False)
    c_heads = bc_heads[..., STATE:].astype(jnp.float32)
    carried = (
        jnp.einsum("stn,shnp->sthp", c_heads, incoming, precision=SCAN_PREC) * profile[..., None]
    )
    ssd_out = (scanned + carried).astype(jnp.bfloat16)
    ssd_tok = lax.all_to_all(ssd_out, "head", split_axis=0, concat_axis=2, tiled=True)
    ssd32 = ssd_tok.astype(jnp.float32).reshape(row_count, DI)
    gate_in = projected[:, :DI]
    gated_out = ssd32 * jax.nn.silu(gate_in)
    gate_normed = rms_scale(gated_out, gate_gain.astype(jnp.float32)).astype(jnp.bfloat16)
    branch = jnp.dot(gate_normed, w_out, preferred_element_type=jnp.float32)
    positions = lax.axis_index("seq") * local_len + jnp.arange(local_len, dtype=jnp.int32)
    token_mask = (positions[None, :] < lengths[:, None]).astype(jnp.float32).reshape(row_count, 1)
    block32 = hidden32 + token_mask * branch
    kept_values = (
        gathered,
        hidden32,
        normed,
        projected,
        dt_raw,
        padded,
        conv_pre,
        x_heads,
        dt_heads,
        bc_heads,
        a_vals,
        skip_vals,
        incoming,
        profile,
        totals,
        ssd32,
        gated_out,
        gate_normed,
        token_mask,
    )
    return (block32, kept_values)


def run_backward(out_grad, kept_values):
    (
        gathered,
        hidden32,
        normed,
        projected,
        dt_raw,
        padded,
        conv_pre,
        x_heads,
        dt_heads,
        bc_heads,
        a_vals,
        skip_vals,
        incoming,
        profile,
        totals,
        ssd32,
        gated_out,
        gate_normed,
        token_mask,
    ) = kept_values
    norm_gain, w_in, w_dt, conv_weight, conv_bias, dt_bias, a_log, skip_gain, gate_gain, w_out = (
        gathered
    )
    seq_dev, local_len, model_width = out_grad.shape
    row_count = seq_dev * local_len
    grad32 = out_grad.astype(jnp.float32).reshape(row_count, model_width)
    d_branch = (token_mask * grad32).astype(jnp.bfloat16)
    w_out_grad = jnp.einsum("rk,rd->kd", gate_normed, d_branch, preferred_element_type=jnp.float32)
    d_gnorm = jnp.einsum("rd,kd->rk", d_branch, w_out, preferred_element_type=jnp.float32)
    _, norm_pull = jax.vjp(rms_scale, gated_out, gate_gain.astype(jnp.float32))
    d_gated, gate_gain_grad = norm_pull(d_gnorm)
    gate_in = projected[:, :DI]
    _, gate_pull = jax.vjp(
        lambda ssd_vals, gate_vals: ssd_vals * jax.nn.silu(gate_vals), ssd32, gate_in
    )
    d_ssd, d_gate = gate_pull(d_gated)
    d_ssd_tok = d_ssd.astype(jnp.bfloat16).reshape(seq_dev, local_len, HEADS, HEAD_DIM)
    d_ssd_heads = lax.all_to_all(d_ssd_tok, "head", split_axis=2, concat_axis=0, tiled=True)
    dy32 = d_ssd_heads.astype(jnp.float32)
    c_heads = bc_heads[..., STATE:].astype(jnp.float32)
    d_incoming = jnp.einsum("stn,sth,sthp->shnp", c_heads, profile, dy32, precision=SCAN_PREC)
    identity_pair = (jnp.ones_like(totals), jnp.zeros_like(d_incoming))
    _, adjoint = prefix((totals, d_incoming), "seq", join_states, identity_pair, True)
    d_totals = jnp.sum(adjoint * incoming, axis=(2, 3))
    d_profile = jnp.einsum("stn,shnp,sthp->sth", c_heads, incoming, dy32, precision=SCAN_PREC)
    d_c_extra = jnp.einsum("sth,shnp,sthp->stn", profile, incoming, dy32, precision=SCAN_PREC)

    def seq_back(pieces):
        x_seq, dt_seq, bc_seq, dy_seq, dtot_seq, dfin_seq, dprof_seq = pieces
        _, pull = jax.vjp(
            local_scan,
            x_seq.astype(jnp.float32),
            dt_seq.astype(jnp.float32),
            bc_seq[:, :STATE].astype(jnp.float32),
            bc_seq[:, STATE:].astype(jnp.float32),
            a_vals,
            skip_vals,
        )
        return pull((dy_seq, dtot_seq, dfin_seq, dprof_seq))

    d_x, d_dt, d_b, d_c, d_a, d_skip = lax.map(
        seq_back, (x_heads, dt_heads, bc_heads, dy32, d_totals, adjoint, d_profile), batch_size=8
    )
    d_bc = jnp.concatenate([d_b, d_c + d_c_extra], axis=-1)
    d_a = jnp.sum(d_a, axis=0)
    d_skip = jnp.sum(d_skip, axis=0)
    d_bc_tok = lax.psum_scatter(d_bc, "head", scatter_dimension=0, tiled=True)
    d_x_tok, d_dt_tok = (
        lax.all_to_all(d_x.astype(jnp.bfloat16), "head", split_axis=0, concat_axis=2, tiled=True),
        lax.all_to_all(d_dt.astype(jnp.bfloat16), "head", split_axis=0, concat_axis=2, tiled=True),
    )
    head_share = HEADS // lax.axis_size("head")
    offset = lax.axis_index("head") * head_share
    a_log_grad = lax.dynamic_update_slice_in_dim(jnp.zeros((HEADS,), jnp.float32), d_a, offset, 0)
    skip_grad = lax.dynamic_update_slice_in_dim(jnp.zeros((HEADS,), jnp.float32), d_skip, offset, 0)
    d_act = jnp.concatenate(
        [d_x_tok.astype(jnp.float32).reshape(seq_dev, local_len, DI), d_bc_tok], axis=-1
    )
    d_conv = d_act * silu_slope(conv_pre)
    conv_bias_grad = jnp.sum(d_conv, axis=(0, 1))
    kernel32 = conv_weight.astype(jnp.float32)
    conv_weight_grad = jnp.stack(
        [
            jnp.sum(d_conv * padded[:, shift_by : shift_by + local_len], axis=(0, 1))
            for shift_by in range(KERNEL)
        ]
    )
    d_padded = jnp.zeros((seq_dev, local_len + KERNEL - 1, CHANNELS), jnp.float32)
    for shift_by in range(KERNEL):
        d_padded = d_padded + jnp.pad(
            kernel32[shift_by] * d_conv, ((0, 0), (shift_by, KERNEL - 1 - shift_by), (0, 0))
        )
    d_rim = shifted(d_padded[:, : KERNEL - 1].astype(jnp.bfloat16), "seq", -1).astype(jnp.float32)
    d_conv_in = d_padded[:, KERNEL - 1 :] + jnp.pad(
        d_rim, ((0, 0), (local_len - (KERNEL - 1), 0), (0, 0))
    )
    d_dt_pre = d_dt_tok.astype(jnp.float32).reshape(row_count, HEADS) * jax.nn.sigmoid(
        dt_raw + dt_bias.astype(jnp.float32)
    )
    dt_bias_grad = jnp.sum(d_dt_pre, axis=0)
    d_proj = jnp.concatenate([d_gate, d_conv_in.reshape(row_count, CHANNELS)], axis=-1).astype(
        jnp.bfloat16
    )
    d_dt_raw = d_dt_pre.astype(jnp.bfloat16)
    w_in_grad = jnp.einsum("rd,re->de", normed, d_proj, preferred_element_type=jnp.float32)
    w_dt_grad = jnp.einsum("rd,rh->dh", normed, d_dt_raw, preferred_element_type=jnp.float32)
    d_normed = jnp.einsum(
        "re,de->rd", d_proj, w_in, preferred_element_type=jnp.float32
    ) + jnp.einsum("rh,dh->rd", d_dt_raw, w_dt, preferred_element_type=jnp.float32)
    _, first_pull = jax.vjp(rms_scale, hidden32, norm_gain.astype(jnp.float32))
    d_hidden, norm_gain_grad = first_pull(d_normed)
    hidden_grad = (grad32 + d_hidden).reshape(seq_dev, local_len, model_width)
    summed = (
        lax.psum_scatter(norm_gain_grad, "head", scatter_dimension=0, tiled=True),
        lax.psum_scatter(w_in_grad, "head", scatter_dimension=0, tiled=True),
        lax.psum_scatter(w_dt_grad, "head", scatter_dimension=0, tiled=True),
        lax.psum_scatter(conv_weight_grad, "head", scatter_dimension=1, tiled=True),
        lax.psum_scatter(conv_bias_grad, "head", scatter_dimension=0, tiled=True),
        lax.psum_scatter(dt_bias_grad, "head", scatter_dimension=0, tiled=True),
        lax.psum_scatter(a_log_grad, "head", scatter_dimension=0, tiled=True),
        lax.psum_scatter(skip_grad, "head", scatter_dimension=0, tiled=True),
        lax.psum_scatter(gate_gain_grad, "head", scatter_dimension=0, tiled=True),
        lax.psum_scatter(w_out_grad, "head", scatter_dimension=0, tiled=True),
    )
    shared = (
        lax.psum(summed[0].astype(jnp.bfloat16), "seq").astype(jnp.float32),
        lax.psum(summed[1].astype(jnp.bfloat16), "seq").astype(jnp.float32),
        lax.psum(summed[2].astype(jnp.bfloat16), "seq").astype(jnp.float32),
        lax.psum(summed[3].astype(jnp.bfloat16), "seq").astype(jnp.float32),
        lax.psum(summed[4].astype(jnp.bfloat16), "seq").astype(jnp.float32),
        lax.psum(summed[5].astype(jnp.bfloat16), "seq").astype(jnp.float32),
        lax.psum(summed[6].astype(jnp.bfloat16), "seq").astype(jnp.float32),
        lax.psum(summed[7].astype(jnp.bfloat16), "seq").astype(jnp.float32),
        lax.psum(summed[8].astype(jnp.bfloat16), "seq").astype(jnp.float32),
        lax.psum(summed[9].astype(jnp.bfloat16), "seq").astype(jnp.float32),
    )
    return (hidden_grad, shared)


def local(
    hidden,
    lengths,
    out_grad,
    norm_gain,
    w_in,
    w_dt,
    conv_weight,
    conv_bias,
    dt_bias,
    a_log,
    skip_gain,
    gate_gain,
    w_out,
):
    shards = (
        norm_gain,
        w_in,
        w_dt,
        conv_weight,
        conv_bias,
        dt_bias,
        a_log,
        skip_gain,
        gate_gain,
        w_out,
    )
    block32, kept_values = run_forward(hidden, lengths, shards)
    fenced = lax.optimization_barrier((hidden, lengths, block32) + shards)
    _, kept_values = run_forward(fenced[0], fenced[1], fenced[3:])
    hidden_grad, shared = run_backward(out_grad, kept_values)
    block_out = block32.astype(jnp.bfloat16).reshape(hidden.shape)
    return (
        block_out,
        hidden_grad,
        shared[0],
        shared[1],
        shared[2],
        shared[3],
        shared[4],
        shared[5],
        shared[6],
        shared[7],
        shared[8],
        shared[9],
    )


def solution(mesh):
    return jax.shard_map(
        local,
        mesh=mesh,
        in_specs=(
            P("head", "seq", None),
            P("head"),
            P("head", "seq", None),
            P("head"),
            P("head", None),
            P("head", None),
            P(None, "head"),
            P("head"),
            P("head"),
            P("head"),
            P("head"),
            P("head"),
            P("head", None),
        ),
        out_specs=(
            P("head", "seq", None),
            P("head", "seq", None),
            P("head"),
            P("head", None),
            P("head", None),
            P(None, "head"),
            P("head"),
            P("head"),
            P("head"),
            P("head"),
            P("head"),
            P("head", None),
        ),
        check_vma=False,
    )
```

profile of v0, /device:TPU:8, one launch (start us, length us, event | category | flops | bytes accessed | tf_op | source)
XLA Modules:
  0.0 3775.4 jit_solution(3067362241057240136)
XLA Ops:
  20.0 35.2 all-reduce.24
  55.2 26.8 all_gather.91
  91.0 23.8 all-gather.6
  114.9 196.7 %all-gather.21.cloned.1.call-done = bf16[2048,8448]{1,0:T(8,128)(2,1)} async-done(((bf16[256,8448]{1,0:T(8,128)(2,1)}), bf16[2048,8448]{1,0:T(8,128)(2,1)}) %all-gather.21.cloned.1.call-update) | async-done | bytes 34603024 | tf_op jit(solution)/shard_map/all_gather | solution.py:109
  311.6 25.4 fusion.243
  374.9 49.1 %all-gather.23.cloned.1.call-done = bf16[8,512,256]{2,1,0:T(8,128)(2,1)} async-done(((bf16[1,512,256]{2,1,0:T(8,128)(2,1)}), bf16[8,512,256]{2,1,0:T(8,128)(2,1)}) %all-gather.23.cloned.1.call-update) | async-done | bytes 2097168 | tf_op jit(solution)/shard_map/all_gather | solution.py:170
  427.5 52.7 %all-to-all-done.1 = bf16[1,512,64,64]{1,3,0,2:T(8,128)(2,1)} async-done(((bf16[1,512,64,64]{1,3,0,2:T(8,128)(2,1)}), bf16[1,512,64,64]{1,3,0,2:T(8,128)(2,1)}, u32[]{:S(2)}, u32[]{:S(2)}) %all-to-all-start.1) | async-done | bytes 4194336 | tf_op jit(solution)/shard_map/all_to_all | solution.py:167
  509.9 51.1 %while.189 = (s32[]{:T(128)}, f32[8,8,128,64]{2,3,1,0:T(8,128)}, f32[2,8,256,8,64]{2,4,3,1,0:T(8,128)}, f32[2,8,256,8]{2,3,0,1:T(8,128)S(1)}, f32[8]{0:T(128)S(1...) while((s32[]{:T(128)}, f32[8,8,128,64]{2,3,1,0:T(8,128)}, ...), condition=%wide.region_4.5_spmd.clone, body=%wide.region_1.4_spmd.clone.sunk | while | flops 3645473024 | bytes 74594544 | solution.py:96
  592.6 27.0 all-gather.33.cloned.1.call-done
  619.6 30.1 while.190
  669.9 187.1 %all-gather.7 = bf16[8,1,512]{2,1,0:T(2,128)(2,1)S(1)} all-gather(bf16[1,1,512]{2,1,0:T(2,128)(2,1)S(1)} %reshape.851), channel_id=1, replica_groups=mesh['seq'=4,'head'=8] {'head'}, dimensions={0}, use_global_device_ids=true | all-gather | bytes 9216 | tf_op jit(solution)/shard_map/all_gather | solution.py:116
  880.1 19.4 convert_add_fusion.3
  911.6 21.1 all-gather.9
  933.9 39.7 %all-reduce.23 = (bf16[64]{0:T(256)(128)(2,1)S(1)}, bf16[64]{0:T(256)(128)(2,1)S(1)}, bf16[4352]{0:T(1024)(128)(2,1)S(1)}, bf16[64]{0:T(256)(128)(2,1)S(1)}) all-reduce(bf16[64]{0:T(256)(128)(2,1)S(1)} %dynamic-update-slice.4, bf16[64]{0:T(256)(128)(2,1)S(1)} %dynamic-update-slice.5, ...), channel_id=1, replica_groups=mesh['seq'=4,'head'=8] {'head'}, use_global_device_ids=true, to_apply=%add.12 | all-reduce | flops 4544 | bytes 18176
  973.5 30.5 all_gather.104
  1006.7 194.2 %all-gather.27.cloned.1.call-done = bf16[2048,8448]{1,0:T(8,128)(2,1)} async-done(((bf16[256,8448]{1,0:T(8,128)(2,1)}), bf16[2048,8448]{1,0:T(8,128)(2,1)}) %all-gather.27.cloned.1.call-update) | async-done | bytes 34603024 | tf_op jit(solution)/shard_map/all_gather | solution.py:109
  1200.9 25.5 fusion.287
  1276.3 44.5 %all-gather.29.cloned.1.call-done = bf16[8,512,256]{2,1,0:T(8,128)(2,1)} async-done(((bf16[1,512,256]{2,1,0:T(8,128)(2,1)}), bf16[8,512,256]{2,1,0:T(8,128)(2,1)}) %all-gather.29.cloned.1.call-update) | async-done | bytes 2097168 | tf_op jit(solution)/shard_map/all_gather | solution.py:170
  1324.3 56.7 %all-to-all-done.4 = bf16[1,512,64,64]{1,3,0,2:T(8,128)(2,1)} async-done(((bf16[1,512,64,64]{1,3,0,2:T(8,128)(2,1)}), bf16[1,512,64,64]{1,3,0,2:T(8,128)(2,1)}, u32[]{:S(2)}, u32[]{:S(2)}) %all-to-all-start.4) | async-done | bytes 4194336 | tf_op jit(solution)/shard_map/all_to_all | solution.py:167
  1410.8 51.1 %while.191 = (s32[]{:T(128)}, f32[8,8,128,64]{2,3,1,0:T(8,128)}, f32[2,8,256,8,64]{2,4,3,1,0:T(8,128)}, f32[2,8,256,8]{2,3,1,0:T(8,128)S(1)}, f32[8]{0:T(128)S(1...) while((s32[]{:T(128)}, f32[8,8,128,64]{2,3,1,0:T(8,128)}, ...), condition=%wide.region_14.15_spmd.clone, body=%wide.region_11.14_spmd.clone.sunk | while | flops 3645473024 | bytes 74594544 | solution.py:96
  1491.8 26.9 all-gather.35.cloned.1.call-done
  1518.7 36.4 while.192
  1576.3 185.4 %all-gather.10 = bf16[8,1,512]{2,1,0:T(2,128)(2,1)S(1)} all-gather(bf16[1,1,512]{2,1,0:T(2,128)(2,1)S(1)} %reshape.857), channel_id=1, replica_groups=mesh['seq'=4,'head'=8] {'head'}, dimensions={0}, use_global_device_ids=true | all-gather | bytes 9216 | tf_op jit(solution)/shard_map/all_gather | solution.py:116
  1786.8 17.3 multiply_reduce_fusion
  1804.2 17.1 fusion.201
  1835.4 90.4 %all-to-all-done.6 = bf16[1,512,64,64]{1,3,0,2:T(8,128)(2,1)} async-done(((bf16[1,512,64,64]{1,3,0,2:T(8,128)(2,1)}), bf16[1,512,64,64]{1,3,0,2:T(8,128)(2,1)}, u32[]{:S(2)}, u32[]{:S(2)}) %all-to-all-start.6) | async-done | bytes 4194336 | tf_op jit(solution)/shard_map/all_to_all | solution.py:255
  1944.8 99.2 %while.194 = (s32[]{:T(128)}, f32[8,8,128,64]{2,3,1,0:T(8,128)}, f32[2,8,256,256,8]{3,4,2,1,0:T(8,128)}, f32[2,8,256,8,1]{2,3,1,4,0:T(8,128)}, f32[2,8,256,256,1...) while((s32[]{:T(128)}, f32[8,8,128,64]{2,3,1,0:T(8,128)}, ...), condition=%wide.region_26.27_spmd.clone, body=%wide.region_23.26_spmd.clone.sunk | while | flops 2033746176 | bytes 301630016 | solution.py:96
  1954.9 16.3 multiply_dynamic-update-slice_fusion.5
  2003.5 16.2 multiply_dynamic-update-slice_fusion.5
  2061.8 31.8 while.193
  2104.6 302.7 %while.195 = (s32[]{:T(128)}, f32[8,8]{1,0:T(8,128)S(1)}, f32[8,8,128,64]{2,3,1,0:T(8,128)S(1)}, f32[2,8,256,8,64]{2,4,3,1,0:T(8,128)}, f32[2,8,256,8]{2,3,0,1:T...) while((s32[]{:T(128)}, f32[8,8]{1,0:T(8,128)S(1)}, ...), condition=%wide.region_39.40_spmd.clone, body=%wide.region_27.39_spmd.clone.sunk | while | flops 7293026816 | bytes 306080832 | solution.py:96
  2124.2 21.1 bitcast_dynamic-update-slice_fusion.29
  2168.8 25.6 fusion.422
  2208.8 19.8 reduce-window.122
  2272.9 21.0 bitcast_dynamic-update-slice_fusion.29
  2317.1 25.6 fusion.422
  2357.2 19.8 reduce-window.122
  2429.4 19.6 fusion.226
  2459.0 159.2 %all_to_all.90 = bf16[8,512,8,64]{1,3,2,0:T(8,128)(2,1)S(1)} all-to-all(bf16[8,512,8,64]{1,3,2,0:T(8,128)(2,1)S(1)} %get-tuple-element.2230), channel_id=1, replica_groups=mesh['seq'=4,'head'=8] {'head'}, dimensions={0} | all-to-all | bytes 8388608 | tf_op jit(solution)/shard_map/all_to_all | solution.py:286
  2681.8 30.5 fusion.207
  2722.2 39.6 %reduce-window.90 = f32[8,8,4,128]{3,1,2,0:T(8,128)S(1)} reduce-window(f32[8,8,4,128]{3,1,2,0:T(8,128)S(1)} %multiply_bitcast_fusion.3, f32[]{:T(128)} %constant.379.clone.1), window={size=1x1x1x128 pad=0_0x0_0x0_0x0_127}, to_apply=%region_42.43 | reduce-window | flops 4161536 | bytes 262148 | tf_op jit(solution)/shard_map/reduce-window.12
  2778.7 101.8 %reduce-scatter.14.cloned.1.call-done = f32[512,2048]{1,0:T(8,128)} async-done(((f32[4096,2048]{1,0:T(8,128)}), f32[512,2048]{1,0:T(8,128)}) %reduce-scatter.14.cloned.1.call-update) | async-done | bytes 4194320 | tf_op jit(solution)/shard_map/reduce_scatter | solution.py:340
  2884.4 658.7 %reduce-scatter.10.cloned.1.call-done = f32[256,8448]{1,0:T(8,128)} async-done(((f32[2048,8448]{1,0:T(8,128)}), f32[256,8448]{1,0:T(8,128)}) %reduce-scatter.10.cloned.1.call-update) | async-done | bytes 8650768 | tf_op jit(solution)/shard_map/reduce_scatter | solution.py:332
  3555.1 19.0 reduce-scatter.12.cloned.1.call-done
  3574.9 27.1 fusion.217
  3602.0 26.6 all-reduce.22
  3636.7 18.0 all-reduce.25
  3659.3 100.2 %all-reduce.29.cloned.1.call-done = (bf16[256,8448]{1,0:T(8,128)(2,1)}, bf16[512,2048]{1,0:T(8,128)(2,1)}) async-done(((bf16[256,8448]{1,0:T(8,128)(2,1)}, bf16[512,2048]{1,0:T(8,128)(2,1)}), (bf16[256,8448]{1,0:T(8,128)(2,1)}, bf16[512,2048]{1,0:T(8,128)(2,1)})) %all-reduce.29.cloned.1.call-update) | async-done | bytes 6422544 | tf_op jit(solution)/shard_map/psum | solution.py:344
  (830 shorter events, 988.3 us)
Async XLA Ops:
  7.2 48.0 %copy-start.66 = (bf16[256,64]{0,1:T(8,128)(2,1)S(1)}, bf16[256,64]{0,1:T(8,128)(2,1)}, u32[]{:S(2)}) copy-start(bf16[256,64]{0,1:T(8,128)(2,1)} %param.32) | copy-start | bytes 98308
  7.3 74.8 %copy-start.14 = (bf16[1,512,2048]{2,1,0:T(8,128)(2,1)S(1)}, bf16[1,512,2048]{2,1,0:T(8,128)(2,1)}, u32[]{:S(2)}) copy-start(bf16[1,512,2048]{2,1,0:T(8,128)(2,1)} %param.27) | copy-start | bytes 6291460
  7.3 304.3 %all-gather.21.cloned.1.call-start = ((), (), s32[]{:S(2)}) async-start(), calls=%async_computation.14 | async-start | bytes 38928384 | tf_op jit(solution)/shard_map/all_gather | solution.py:109
  8.0 83.0 %copy-start.74 = (bf16[4,544]{1,0:T(4,128)(2,1)S(1)}, bf16[4,544]{1,0:T(4,128)(2,1)}, u32[]{:S(2)}) copy-start(bf16[4,544]{1,0:T(4,128)(2,1)} %param.33) | copy-start | bytes 13060
  85.7 279.8 %all-to-all-start = ((bf16[8,2,2048]{2,1,0:T(2,128)(2,1)}), bf16[8,2,2048]{2,1,0:T(2,128)(2,1)S(1)}, u32[]{:S(2)}, u32[]{:S(2)}) async-start(bf16[8,2,2048]{2,1,0:T(2,128)(2,1)} %reshape.939), calls=%async_computation | async-start | bytes 131072 | tf_op jit(solution)/shard_map/all_to_all | solution.py:168
  341.0 5.2 collective-permute-start
  365.5 114.7 %all-to-all-start.1 = ((bf16[1,512,64,64]{1,3,0,2:T(8,128)(2,1)}), bf16[1,512,64,64]{1,3,0,2:T(8,128)(2,1)}, u32[]{:S(2)}, u32[]{:S(2)}) async-start(bf16[1,512,64,64]{1,3,0,2:T(8,128)(2,1)} %bitcast.947), calls=%async_computation.1 | async-start | bytes 8388608 | tf_op jit(solution)/shard_map/all_to_all | solution.py:167
  372.8 51.2 %all-gather.23.cloned.1.call-start = ((), (), s32[]{:S(2)}) async-start(), calls=%async_computation.15 | async-start | bytes 2359296 | tf_op jit(solution)/shard_map/all_gather | solution.py:170
  374.5 245.1 %all-gather.33.cloned.1.call-start = ((), (), s32[]{:S(2)}) async-start(), calls=%async_computation.24 | async-start | bytes 5242880 | tf_op jit(solution)/shard_map/all_gather | solution.py:28
  563.9 316.2 %all-gather.25.cloned.1.call-start = ((), (), s32[]{:S(2)}) async-start(), calls=%async_computation.16 | async-start | bytes 18874368 | tf_op jit(solution)/shard_map/all_gather | solution.py:117
  663.7 193.3 %all-to-all-start.2 = ((bf16[8,512,8,64]{1,3,2,0:T(8,128)(2,1)}), bf16[8,512,8,64]{1,3,2,0:T(8,128)(2,1)}, u32[]{:S(2)}, u32[]{:S(2)}) async-start(bf16[8,512,8,64]{1,3,2,0:T(8,128)(2,1)} %fusion.195), calls=%async_computation.2 | async-start | bytes 8388608 | tf_op jit(solution)/shard_map/all_to_all | solution.py:183
  669.2 531.7 %all-gather.27.cloned.1.call-start = ((), (), s32[]{:S(2)}) async-start(), calls=%async_computation.17 | async-start | bytes 38928384 | tf_op jit(solution)/shard_map/all_gather | solution.py:109
  899.5 33.4 copy-start.82
  899.5 33.6 copy-start.94
  899.5 33.9 copy-start.96
  899.5 34.1 copy-start.98
  899.5 74.0 %copy-start.67 = (bf16[256,64]{0,1:T(8,128)(2,1)S(1)}, bf16[256,64]{0,1:T(8,128)(2,1)}, u32[]{:S(2)}) copy-start(bf16[256,64]{0,1:T(8,128)(2,1)} %param.32) | copy-start | bytes 98308
  911.6 314.8 %copy-start.46 = (f32[8,1,256]{2,1,0:T(1,128)}, f32[8,1,256]{2,1,0:T(1,128)S(1)}, u32[]{:S(2)}) copy-start(f32[8,1,256]{2,1,0:T(1,128)S(1)} %convert_element_type.650) | copy-start | bytes 24580
  1004.6 221.8 %copy-start.48 = (f32[512]{0:T(512)}, f32[512]{0:T(512)S(1)}, u32[]{:S(2)}) copy-start(f32[512]{0:T(512)S(1)} %fusion.273) | copy-start | bytes 6148
  1232.4 11.3 collective-permute-start.1
  1238.0 30.5 all-to-all-start.3
  1268.5 112.5 %all-to-all-start.4 = ((bf16[1,512,64,64]{1,3,0,2:T(8,128)(2,1)}), bf16[1,512,64,64]{1,3,0,2:T(8,128)(2,1)}, u32[]{:S(2)}, u32[]{:S(2)}) async-start(bf16[1,512,64,64]{1,3,0,2:T(8,128)(2,1)} %bitcast.948), calls=%async_computation.4 | async-start | bytes 8388608 | tf_op jit(solution)/shard_map/all_to_all | solution.py:167
  1273.6 47.2 %all-gather.29.cloned.1.call-start = ((), (), s32[]{:S(2)}) async-start(), calls=%async_computation.18 | async-start | bytes 2359296 | tf_op jit(solution)/shard_map/all_gather | solution.py:170
  1275.3 243.3 %all-gather.35.cloned.1.call-start = ((), (), s32[]{:S(2)}) async-start(), calls=%async_computation.25 | async-start | bytes 5242880 | tf_op jit(solution)/shard_map/all_gather | solution.py:28
  1464.7 322.1 %all-gather.31.cloned.1.call-start = ((), (), s32[]{:S(2)}) async-start(), calls=%async_computation.19 | async-start | bytes 18874368 | tf_op jit(solution)/shard_map/all_gather | solution.py:117
  1465.5 97.6 %copy-start.85 = (f32[8]{0:T(128)}, f32[8]{0:T(128)S(1)}, u32[]{:S(2)}) copy-start(f32[8]{0:T(128)S(1)} %dynamic_slice.320) | copy-start | bytes 100
  1465.7 26.1 copy-start.34
  1475.4 87.8 %copy-start.27 = (f32[8,512,8]{1,2,0:T(8,128)}, f32[8,512,8]{1,2,0:T(8,128)S(1)}, u32[]{:S(2)}) copy-start(f32[8,512,8]{1,2,0:T(8,128)S(1)} %exponential_bitcast_fusion) | copy-start | bytes 393220
  1570.9 190.8 %all-to-all-start.5 = ((bf16[8,512,8,64]{1,3,2,0:T(8,128)(2,1)}), bf16[8,512,8,64]{1,3,2,0:T(8,128)(2,1)}, u32[]{:S(2)}, u32[]{:S(2)}) async-start(bf16[8,512,8,64]{1,3,2,0:T(8,128)(2,1)} %fusion.198), calls=%async_computation.5 | async-start | bytes 8388608 | tf_op jit(solution)/shard_map/all_to_all | solution.py:183
  1576.3 210.5 %copy-start.88 = (f32[512]{0:T(512)}, f32[512]{0:T(512)S(1)}, u32[]{:S(2)}) copy-start(f32[512]{0:T(512)S(1)} %fusion.272) | copy-start | bytes 6148
  1761.7 42.5 %copy-start.69 = (f32[8,1,512]{2,1,0:T(1,128)}, f32[8,1,512]{2,1,0:T(1,128)S(1)}, u32[]{:S(2)}) copy-start(f32[8,1,512]{2,1,0:T(1,128)S(1)} %convert_element_type.652) | copy-start | bytes 49156
  1827.7 98.1 %copy-start.28 = (f32[8,512,8]{1,2,0:T(8,128)S(1)}, f32[8,512,8]{1,2,0:T(8,128)}, u32[]{:S(2)}) copy-start(f32[8,512,8]{1,2,0:T(8,128)} %copy-done.27) | copy-start | bytes 393220
  1827.7 98.1 %all-to-all-start.6 = ((bf16[1,512,64,64]{1,3,0,2:T(8,128)(2,1)}), bf16[1,512,64,64]{1,3,0,2:T(8,128)(2,1)}, u32[]{:S(2)}, u32[]{:S(2)}) async-start(bf16[1,512,64,64]{1,3,0,2:T(8,128)(2,1)} %bitcast.949), calls=%async_computation.6 | async-start | bytes 8388608 | tf_op jit(solution)/shard_map/all_to_all | solution.py:255
  1835.3 226.6 %all-gather.37.cloned.1.call-start = ((), (), s32[]{:S(2)}) async-start(), calls=%async_computation.26 | async-start | bytes 5242880 | tf_op jit(solution)/shard_map/all_gather | solution.py:28
  1931.7 700.1 %reduce-scatter.8.cloned.1.call-start = ((), (), s32[]{:S(2)}) async-start(), calls=%async_computation.20 | async-start | bytes 4718592 | tf_op jit(solution)/shard_map/reduce_scatter | solution.py:284
  2104.7 64.0 %copy-start.25 = (pred[256,256]{1,0:T(8,128)(4,1)}, pred[256,256]{1,0:T(8,128)(4,1)S(1)}, u32[]{:S(2)}) copy-start(pred[256,256]{1,0:T(8,128)(4,1)S(1)} %get-tuple-element.3107) | copy-start | bytes 196612 | tf_op jit(solution)/shard_map/while/body/eval_jaxpr/vmap(transpose(jvp()))/while
  2253.4 63.7 %copy-start.25 = (pred[256,256]{1,0:T(8,128)(4,1)}, pred[256,256]{1,0:T(8,128)(4,1)S(1)}, u32[]{:S(2)}) copy-start(pred[256,256]{1,0:T(8,128)(4,1)S(1)} %get-tuple-element.3107) | copy-start | bytes 196612 | tf_op jit(solution)/shard_map/while/body/eval_jaxpr/vmap(transpose(jvp()))/while
  2427.8 452.7 %reduce-scatter.14.cloned.1.call-start = ((), (), s32[]{:S(2)}) async-start(), calls=%async_computation.23 | async-start | bytes 37748736 | tf_op jit(solution)/shard_map/reduce_scatter | solution.py:340
  2449.0 1094.0 %reduce-scatter.10.cloned.1.call-start = ((), (), s32[]{:S(2)}) async-start(), calls=%async_computation.21 | async-start | bytes 77856768 | tf_op jit(solution)/shard_map/reduce_scatter | solution.py:332
  2672.9 6.0 collective-permute-start.2
  2712.3 861.7 %reduce-scatter.12.cloned.1.call-start = ((), (), s32[]{:S(2)}) async-start(), calls=%async_computation.22 | async-start | bytes 589824 | tf_op jit(solution)/shard_map/reduce_scatter | solution.py:333
  2721.2 41.0 %copy-start.35 = (f32[1,512,64]{1,0,2:T(1,128)S(1)}, f32[1,512,64]{1,0,2:T(1,128)}, u32[]{:S(2)}) copy-start(f32[1,512,64]{1,0,2:T(1,128)} %copy-done.34) | copy-start | bytes 393220
  2721.2 41.0 %copy-start.50 = (f32[2,8,256,8]{2,3,0,1:T(8,128)S(1)}, f32[2,8,256,8]{2,3,0,1:T(8,128)}, u32[]{:S(2)}) copy-start(f32[2,8,256,8]{2,3,0,1:T(8,128)} %get-tuple-element.1324) | copy-start | bytes 393220
  2721.2 53.3 %copy-start.33 = (f32[512,64]{0,1:T(8,128)S(1)}, f32[512,64]{0,1:T(8,128)}, u32[]{:S(2)}) copy-start(f32[512,64]{0,1:T(8,128)} %copy-done.32) | copy-start | bytes 393220
  2776.1 859.6 %reduce-scatter.16.cloned.1.call-start = ((), (), s32[]{:S(2)}) async-start(), calls=%async_computation.27 | async-start | bytes 2506752
  2778.4 981.0 %all-reduce.29.cloned.1.call-start = ((), (), s32[]{:S(2)}) async-start(), calls=%async_computation.28 | async-start | bytes 12845056 | tf_op jit(solution)/shard_map/psum | solution.py:344
  3574.9 27.1 copy-start.78
  3574.9 54.2 %copy-start.77 = (f32[512]{0:T(512)S(1)}, f32[512]{0:T(512)}, u32[]{:S(2)}) copy-start(f32[512]{0:T(512)} %copy-done.76) | copy-start | bytes 6148
  (133 other events, 1052.5 us)
Sparse Core Ops, SparseCore 0:
  9.8 301.7 all-gather.20
  375.8 48.1 all-gather.22
  564.0 55.5 all-gather.32
  621.0 235.0 all-gather.24
  899.7 301.1 all-gather.26
  1275.7 45.0 all-gather.28
  1464.8 53.8 all-gather.34
  1520.3 234.8 all-gather.30
  1931.8 54.7 all-gather.36
  2428.0 64.1 reduce-scatter.7
  2494.6 385.9 reduce-scatter.13
  2882.9 660.1 reduce-scatter.9
  3545.4 28.5 reduce-scatter.11
  3576.2 34.5 reduce-scatter.15
  3614.6 144.7 all-reduce.28
where the time goes:
time: 3790 us; the launch traced here: 3780 us
  waiting for transfers between devices  1630 us (43%)
  blocking collectives  805 us (21%)
  other arithmetic  473 us (12%)
  matrix products  447 us (12%)
  local copies, waits for them, and re-layouts  344 us (9%)
  starting transfers between devices  51.7 us (1%)
    reduce_scatter x1, waiting for transfers between devices, run_backward(): lax.psum_scatter(w_in_grad, 'head', scatter_dimension=0, tiled=True)  659 us
    all_gather x2, waiting for transfers between devices, fetch_weights(): lax.all_gather(shards[1], 'head', axis=0, tiled=True)  391 us
    all_gather x2, blocking collectives, fetch_weights(): lax.all_gather(shards[8], 'head', axis=0, tiled=True)  372 us
    another operation x45, other arithmetic  165 us
    all_to_all x1, blocking collectives, run_backward(): lax.all_to_all(d_x.astype(jnp.bfloat16), 'head', split_axis=0, concat_axi...  159 us
    dot_general x8, matrix products, advance(): jnp.einsum('tsh,shp->thp', scores[:, :, None] * weights, scaled, precisio...  141 us
    all_to_all x2, waiting for transfers between devices, run_forward(): lax.all_to_all(x_tok, 'head', split_axis=2, concat_axis=0, tiled=True)  109 us
    reduce_scatter x1, waiting for transfers between devices, run_backward(): lax.psum_scatter(w_out_grad, 'head', scatter_dimension=0, tiled=True)  102 us
  transfers between devices with their start and end apart: 25, of which 15 were waited for; matrix products, arithmetic and copies ran while one was open for 16% of the time, Pallas kernels for 0%

commit v1 on v0

v1 whole, which is shorter than its diff:
```python
import functools

import jax
import jax.numpy as jnp
from jax import lax
from jax.experimental import pallas as pl
from jax.experimental.pallas import tpu as pltpu
from jax.sharding import PartitionSpec as P

HEADS = 64
HEAD_DIM = 64
STATE = 128
KERNEL = 4
CHUNK = 256
DI = 4096
CHANNELS = 4352
PROJ = DI + CHANNELS
EPS = 1e-05
LANES = 128
EVERY = ("seq", "head")
F32 = jnp.float32
BF16 = jnp.bfloat16


def dot(a, b):
    return jnp.dot(a, b, preferred_element_type=F32)


def dot_t(a, b):
    return lax.dot_general(a, b, (((1,), (1,)), ((), ())), preferred_element_type=F32)


def t_dot(a, b):
    return lax.dot_general(a, b, (((0,), (0,)), ((), ())), preferred_element_type=F32)


def sigmoid(v):
    return 1.0 / (1.0 + jnp.exp(-v))


def project_kernel(h_ref, w_ref, cw_ref, cb_ref, dtb_ref, z_ref, u_ref, act_ref, slope_ref, aux_ref, ext, *, heads, wide):
    step = pl.program_id(0)
    rows = h_ref.shape[0]
    chans = u_ref.shape[1]
    h = h_ref[...]
    h32 = h.astype(F32)
    r0 = lax.rsqrt(jnp.mean(h32 * h32, axis=1, keepdims=True) + EPS)
    z_ref[...] = (dot(h, w_ref[:, :wide]) * r0).astype(BF16)
    u = (dot(h, w_ref[:, wide : wide + chans]) * r0).astype(BF16)
    dt_raw = dot(h, w_ref[:, wide + chans :]) * r0

    @pl.when(step == 0)
    def _():
        ext[0:8, :] = jnp.zeros((8, chans), F32)

    @pl.when(step > 0)
    def _():
        ext[0:8, :] = ext[rows : rows + 8, :]

    u_ref[...] = u
    ext[8 : rows + 8, :] = u.astype(F32)
    pre = cb_ref[0:1, :]
    for k in range(KERNEL):
        pre = pre + cw_ref[k : k + 1, :] * ext[pl.ds(8 - (KERNEL - 1) + k, rows), :]
    sig = sigmoid(pre)
    act_ref[...] = (pre * sig).astype(BF16)
    slope_ref[...] = (sig * (1.0 + pre * (1.0 - sig))).astype(BF16)
    v = dt_raw + dtb_ref[0:1, :]
    soft = jnp.maximum(v, 0.0) + jnp.log1p(jnp.exp(-jnp.abs(v)))
    soft = soft.astype(BF16).astype(F32)
    lane = lax.broadcasted_iota(jnp.int32, v.shape, 1)
    aux = jnp.where(lane < heads, soft, 0.0)
    sig_v = pltpu.roll(sigmoid(v), heads, 1)
    aux = jnp.where((lane >= heads) & (lane < 2 * heads), sig_v, aux)
    aux_ref[...] = jnp.where(lane == 2 * heads, r0, aux)


def decays(aux, heads, expand, rate_e, rate_row, rate_col):
    rows = aux.shape[0]
    lane = lax.broadcasted_iota(jnp.int32, aux.shape, 1)
    dt = jnp.where(lane < heads, aux, 0.0).astype(BF16)
    r = lax.broadcasted_iota(jnp.int32, (rows, rows), 0)
    c = lax.broadcasted_iota(jnp.int32, (rows, rows), 1)
    causal = c <= r
    lower = jnp.where(causal, 1.0, 0.0).astype(BF16)
    dt_e = dot(dt, expand)
    cum_e = dot(lower, dt_e.astype(BF16)) * rate_e
    cum_c = dot(lower, dt) * rate_row
    cum_t = lax.dot_general(dt, lower, (((0,), (1,)), ((), ())), preferred_element_type=F32) * rate_col
    return causal, dt_e, cum_e, cum_c, cum_t


def scan_kernel(act_ref, aux_ref, z_ref, d0_ref, exp_ref, rowp_ref, colp_ref, y_ref, gg_ref, st_ref, stat_ref, state, *, heads, wide):
    step = pl.program_id(0)

    @pl.when(step == 0)
    def _():
        state[...] = jnp.zeros_like(state)

    rows = act_ref.shape[0]
    x = act_ref[:, :wide]
    x32 = x.astype(F32)
    b = act_ref[:, wide : wide + STATE]
    c = act_ref[:, wide + STATE :]
    causal, dt_e, cum_e, cum_c, cum_t = decays(
        aux_ref[...], heads, exp_ref[...], rowp_ref[0:1, :], rowp_ref[3:4, :LANES], colp_ref[:, 0:1]
    )
    xdt = x32 * dt_e
    xdt16 = xdt.astype(BF16)
    scores = dot_t(c, b)
    st = state[...]
    st_ref[0] = st
    half = lax.broadcasted_iota(jnp.int32, (rows, LANES), 1) < HEAD_DIM
    parts = []
    for pair in range(heads // 2):
        x2 = xdt16[:, LANES * pair : LANES * (pair + 1)]
        got = []
        for h in (2 * pair, 2 * pair + 1):
            spread = cum_c[:, h : h + 1] - cum_t[h : h + 1, :]
            m = (scores * jnp.exp(jnp.where(causal, spread, -1e30))).astype(BF16)
            got.append(dot(m, x2))
        parts.append(jnp.where(half, got[0], got[1]))
    y = jnp.concatenate(parts, axis=1) + dot(c, st.astype(BF16)) * jnp.exp(cum_e)
    last = cum_e[rows - 1 : rows, :]
    tail = jnp.exp(last - cum_e)
    state[...] = jnp.exp(last) * st + t_dot(b, (xdt * tail).astype(BF16))
    y_ref[...] = y
    ssd = (y + rowp_ref[1:2, :] * x32).astype(BF16).astype(F32)
    z = z_ref[...].astype(F32)
    g = ssd * (z * sigmoid(z))
    gain = rowp_ref[2:3, :]
    gg = g * gain
    gg_ref[...] = gg.astype(BF16)
    ssq = jnp.sum(g * g, axis=1, keepdims=True)
    cross = jnp.sum(gg * d0_ref[...].astype(F32), axis=1, keepdims=True)
    lane = lax.broadcasted_iota(jnp.int32, (rows, LANES), 1)
    stat_ref[...] = jnp.where(lane == 0, ssq, jnp.where(lane == 1, cross, 0.0))


def seg_dot(v, seg):
    hi = v.astype(BF16)
    rest = v - hi.astype(F32)
    mid = rest.astype(BF16)
    low = (rest - mid.astype(F32)).astype(BF16)
    return dot(hi, seg) + dot(mid, seg) + dot(low, seg)


def back_kernel(
    act_ref, aux_ref, z_ref, d0_ref, y_ref, st_ref, slope_ref, u_ref, stat_ref,
    exp_ref, seg_ref, rowp_ref, colp_ref, cw_ref,
    dp_ref, sm_ref, adj, ext, *, heads, wide,
):
    step = pl.program_id(0)
    rows = act_ref.shape[0]
    chans = u_ref.shape[1]

    @pl.when(step == 0)
    def _():
        sm_ref[...] = jnp.zeros_like(sm_ref)
        adj[...] = jnp.zeros_like(adj)
        ext[rows : rows + 8, :] = jnp.zeros((8, chans), F32)

    @pl.when(step > 0)
    def _():
        ext[rows : rows + 8, :] = ext[0:8, :]

    x = act_ref[:, :wide]
    x32 = x.astype(F32)
    b = act_ref[:, wide : wide + STATE]
    c = act_ref[:, wide + STATE :]
    aux = aux_ref[...]
    stat = stat_ref[...]
    r1m = stat[:, 0:1]
    coef = stat[:, 1:2]
    r0 = aux[:, 2 * heads : 2 * heads + 1]
    skip_e = rowp_ref[1:2, :]
    gain = rowp_ref[2:3, :]

    y = y_ref[...]
    ssd = (y + skip_e * x32).astype(BF16).astype(F32)
    z = z_ref[...].astype(F32)
    sig = sigmoid(z)
    sz = z * sig
    d_gated = (r1m * gain) * d0_ref[...].astype(F32) - (ssd * sz) * coef
    dy16 = (d_gated * sz).astype(BF16)
    dy = dy16.astype(F32)
    dp_ref[:, :wide] = (r0 * (d_gated * ssd * (sig * (1.0 + z * (1.0 - sig))))).astype(BF16)

    causal, dt_e, cum_e, cum_c, cum_t = decays(
        aux, heads, exp_ref[...], rowp_ref[0:1, :], rowp_ref[3:4, :LANES], colp_ref[:, 0:1]
    )
    xdt = x32 * dt_e
    xdt16 = xdt.astype(BF16)
    scores = dot_t(c, b)
    st = st_ref[0]
    st16 = st.astype(BF16)
    q_in = adj[...]
    q16 = q_in.astype(BF16)
    last = cum_e[rows - 1 : rows, :]
    ecum = jnp.exp(cum_e)
    tail = jnp.exp(last - cum_e)
    half = lax.broadcasted_iota(jnp.int32, (rows, LANES), 1) < HEAD_DIM
    zero = jnp.zeros((rows, LANES), BF16)
    n_sum = None
    parts = []
    for pair in range(heads // 2):
        cut = slice(LANES * pair, LANES * (pair + 1))
        x2 = xdt16[:, cut]
        dy2 = dy16[:, cut]
        got = []
        for side in range(2):
            h = 2 * pair + side
            spread = cum_c[:, h : h + 1] - cum_t[h : h + 1, :]
            ell = jnp.exp(jnp.where(causal, spread, -1e30))
            m = (scores * ell).astype(BF16)
            got.append(t_dot(m, dy2))
            own = half if side == 0 else jnp.logical_not(half)
            n = dot_t(jnp.where(own, dy2, zero), x2) * ell
            n_sum = n if n_sum is None else n_sum + n
        parts.append(jnp.where(half, got[0], got[1]))
    out_part = dot(b, q16) * tail
    v = jnp.concatenate(parts, axis=1) + out_part
    n16 = n_sum.astype(BF16)
    dy_e = (dy * ecum).astype(BF16)
    x_tail = (xdt * tail).astype(BF16)
    d_b = t_dot(n16, c) + dot_t(x_tail, q16)
    d_c = dot(n16, b) + dot_t(dy_e, st16)
    elast = jnp.exp(last)
    adj[...] = elast * q_in + t_dot(c, dy_e)

    seg = seg_ref[...]
    flow = dy * y - xdt16.astype(F32) * v
    passed = jnp.sum(xdt16.astype(F32) * out_part, axis=0, keepdims=True)
    passed = passed + elast * jnp.sum(q_in * st, axis=0, keepdims=True)
    flow_h = seg_dot(flow, seg)
    passed_h = seg_dot(jnp.broadcast_to(passed, (8, wide)), seg)[0:1, :]
    upper = jnp.where(
        lax.broadcasted_iota(jnp.int32, (rows, rows), 1) >= lax.broadcasted_iota(jnp.int32, (rows, rows), 0), 1.0, 0.0
    ).astype(BF16)
    hi = flow_h.astype(BF16)
    rest = flow_h - hi.astype(F32)
    mid = rest.astype(BF16)
    low = (rest - mid.astype(F32)).astype(BF16)
    crossing = dot(upper, hi) + dot(upper, mid) + dot(upper, low) + passed_h
    rate_row = rowp_ref[3:4, :LANES]
    decay_grad = rate_row * crossing
    d_dt = seg_dot(x32 * v, seg) + decay_grad
    lane = lax.broadcasted_iota(jnp.int32, (rows, LANES), 1)
    sig_v = pltpu.roll(aux, LANES - heads, 1)
    d_pre = jnp.where(lane < heads, d_dt * sig_v, 0.0)
    dt = jnp.where(lane < heads, aux, 0.0)
    dp_ref[:, wide + chans :] = (r0 * d_pre).astype(BF16)

    d_act = jnp.concatenate([skip_e * dy + dt_e * v, d_b, d_c], axis=1)
    d_conv = d_act * slope_ref[...].astype(F32)
    ext[0:rows, :] = d_conv
    u = u_ref[...].astype(F32)
    d_u = None
    for k in range(KERNEL):
        moved = ext[pl.ds(KERNEL - 1 - k, rows), :]
        term = cw_ref[k : k + 1, :] * moved
        d_u = term if d_u is None else d_u + term
        sm_ref[k : k + 1, :] += jnp.sum(u * moved, axis=0, keepdims=True)
    dp_ref[:, wide : wide + chans] = (r0 * d_u).astype(BF16)
    sm_ref[4:5, :] += jnp.sum(d_conv, axis=0, keepdims=True)
    sm_ref[5:6, :wide] += jnp.sum(x32 * dy, axis=0, keepdims=True)
    sm_ref[6:7, :LANES] += jnp.sum(d_pre, axis=0, keepdims=True)
    sm_ref[7:8, :LANES] += jnp.sum(dt * decay_grad, axis=0, keepdims=True)


def local(hidden, lengths, out_grad, norm_gain, w_in, w_dt, conv_weight, conv_bias, dt_bias, a_log, skip_gain, gate_gain, w_out):
    ranks = lax.axis_size("seq")
    rank = lax.axis_index("seq")
    owners = lax.axis_size("head")
    owner = lax.axis_index("head")
    local_len, width = hidden.shape[1], hidden.shape[2]
    heads = HEADS // ranks
    wide = heads * HEAD_DIM
    chans = wide + 2 * STATE
    cols = wide + chans + LANES
    tokens = ranks * local_len
    chunk = min(CHUNK, local_len)
    steps = tokens // chunk
    shard = w_in.shape[0]

    small = jnp.concatenate([conv_weight.reshape(-1), conv_bias, dt_bias, a_log, skip_gain, gate_gain])
    small = lax.all_gather(small, "head")
    cs = CHANNELS // owners
    hs = HEADS // owners
    gs = DI // owners
    conv_w = small[:, : KERNEL * cs].reshape(owners, KERNEL, cs).swapaxes(0, 1).reshape(KERNEL, CHANNELS)
    at = KERNEL * cs
    conv_b = small[:, at : at + cs].reshape(CHANNELS)
    at += cs
    dt_b = small[:, at : at + hs].reshape(HEADS)
    at += hs
    a_all = small[:, at : at + hs].reshape(HEADS)
    at += hs
    skip_all = small[:, at : at + hs].reshape(HEADS)
    at += hs
    gain_all = small[:, at : at + gs].reshape(DI)

    def mine(v, size):
        return lax.dynamic_slice_in_dim(v, rank * size, size, v.ndim - 1)

    cw = jnp.concatenate([mine(conv_w[:, :DI], wide), conv_w[:, DI:]], axis=1).astype(F32)
    cb = jnp.concatenate([mine(conv_b[:DI], wide), conv_b[DI:]])[None].astype(F32)
    cw = jnp.concatenate([cw, jnp.zeros((8 - KERNEL, chans), F32)], axis=0)
    cb = jnp.broadcast_to(cb, (8, chans))
    dtb = jnp.broadcast_to(jnp.pad(mine(dt_b, heads).astype(F32), (0, LANES - heads))[None], (8, LANES))
    rate = -jnp.exp(mine(a_all, heads).astype(F32))
    rowp = jnp.stack(
        [
            jnp.repeat(rate, HEAD_DIM),
            jnp.repeat(mine(skip_all, heads).astype(F32), HEAD_DIM),
            mine(gain_all, wide).astype(F32),
            jnp.pad(rate, (0, wide - heads)),
        ]
        + [jnp.zeros((wide,), F32)] * 4
    )
    colp = jnp.broadcast_to(jnp.pad(rate, (0, LANES - heads))[:, None], (LANES, LANES))
    head_of = jnp.arange(wide, dtype=jnp.int32) // HEAD_DIM
    expand = (jnp.arange(LANES, dtype=jnp.int32)[:, None] == head_of[None]).astype(BF16)
    seg = expand.T

    gain_rows = norm_gain.astype(F32)[:, None]

    def scaled(v):
        return (v.astype(F32) * gain_rows).astype(BF16)

    sent = jnp.concatenate(
        [
            scaled(lax.dynamic_slice_in_dim(w_in, rank * wide, wide, 1)),
            scaled(lax.dynamic_slice_in_dim(w_in, DI + rank * wide, wide, 1)),
            scaled(w_in[:, 2 * DI :]),
            scaled(lax.dynamic_slice_in_dim(w_dt, rank * heads, heads, 1)),
            jnp.zeros((shard, LANES - heads), BF16),
        ],
        axis=1,
    )
    w_t = lax.all_gather(sent, "head", axis=0, tiled=True)
    w_o = lax.dynamic_slice_in_dim(lax.all_gather(w_out, "head", axis=0, tiled=True), rank * wide, wide, 0)
    h_all = lax.all_gather(hidden[0], "seq", axis=0, tiled=True)
    og_all = lax.all_gather(out_grad[0], "seq", axis=0, tiled=True)

    def forth(size):
        return pl.BlockSpec((chunk, size), lambda j: (j, 0))

    def back(size):
        return pl.BlockSpec((chunk, size), lambda j: (steps - 1 - j, 0))

    def whole(a):
        return pl.BlockSpec(a.shape, lambda j: (0,) * a.ndim, pipeline_mode=pl.Buffered(1))

    params = pltpu.CompilerParams(
        dimension_semantics=("arbitrary",), vmem_limit_bytes=56 * 1024 * 1024
    )
    grid = (steps,)

    def sds(shape, kind):
        return jax.ShapeDtypeStruct(shape, kind)

    z, u, act, slope, aux = pl.pallas_call(
        functools.partial(project_kernel, heads=heads, wide=wide),
        grid=grid,
        in_specs=[forth(width), whole(w_t), whole(cw), whole(cb), whole(dtb)],
        out_specs=[forth(wide), forth(chans), forth(chans), forth(chans), forth(LANES)],
        out_shape=[
            sds((tokens, wide), BF16),
            sds((tokens, chans), BF16),
            sds((tokens, chans), BF16),
            sds((tokens, chans), BF16),
            sds((tokens, LANES), F32),
        ],
        scratch_shapes=[pltpu.VMEM((chunk + 8, chans), F32)],
        compiler_params=params,
        cost_estimate=pl.CostEstimate(
            flops=2 * tokens * width * cols, bytes_accessed=2 * tokens * (width + 4 * chans), transcendentals=0
        ),
        name="project",
    )(h_all, w_t, cw, cb, dtb)

    d0 = dot_t(og_all, w_o).astype(BF16)

    y, gg, states, stat = pl.pallas_call(
        functools.partial(scan_kernel, heads=heads, wide=wide),
        grid=grid,
        in_specs=[forth(chans), forth(LANES), forth(wide), forth(wide), whole(expand), whole(rowp), whole(colp)],
        out_specs=[
            forth(wide),
            forth(wide),
            pl.BlockSpec((1, STATE, wide), lambda j: (j, 0, 0)),
            forth(LANES),
        ],
        out_shape=[
            sds((tokens, wide), F32),
            sds((tokens, wide), BF16),
            sds((steps, STATE, wide), F32),
            sds((tokens, LANES), F32),
        ],
        scratch_shapes=[pltpu.VMEM((STATE, wide), F32)],
        compiler_params=params,
        cost_estimate=pl.CostEstimate(
            flops=2 * tokens * wide * 6 * chunk, bytes_accessed=tokens * wide * 16, transcendentals=tokens * chunk * heads
        ),
        name="scan",
    )(act, aux, z, d0, expand, rowp, colp)

    sums = lax.psum(stat[:, :2].T.reshape(2, tokens // LANES, LANES), "seq").reshape(2, tokens)
    mask = (jnp.arange(tokens, dtype=jnp.int32) < lengths[0]).astype(F32)
    r1 = lax.rsqrt(sums[0] / DI + EPS)
    r1m = r1 * mask
    coef = r1m * r1 * r1 * sums[1] / DI
    lane = jnp.arange(LANES, dtype=jnp.int32)[None]
    stat2 = jnp.where(lane == 0, r1m[:, None], jnp.where(lane == 1, coef[:, None], 0.0))

    partial = dot(gg, w_o).astype(BF16)
    branch = lax.psum_scatter(partial, "seq", scatter_dimension=0, tiled=True)

    og_scaled = (og_all.astype(F32) * r1m[:, None]).astype(BF16)
    wog = t_dot(gg, og_scaled).astype(BF16)

    dp, sm = pl.pallas_call(
        functools.partial(back_kernel, heads=heads, wide=wide),
        grid=grid,
        in_specs=[
            back(chans), back(LANES), back(wide), back(wide), back(wide),
            pl.BlockSpec((1, STATE, wide), lambda j: (steps - 1 - j, 0, 0)),
            back(chans), back(chans), back(LANES),
            whole(expand), whole(seg), whole(rowp), whole(colp), whole(cw),
        ],
        out_specs=[back(cols), pl.BlockSpec((8, chans), lambda j: (0, 0))],
        out_shape=[sds((tokens, cols), BF16), sds((8, chans), F32)],
        scratch_shapes=[pltpu.VMEM((STATE, wide), F32), pltpu.VMEM((chunk + 8, chans), F32)],
        compiler_params=params,
        cost_estimate=pl.CostEstimate(
            flops=2 * tokens * wide * 12 * chunk, bytes_accessed=tokens * wide * 24, transcendentals=tokens * chunk * heads
        ),
        name="scan_back",
    )(act, aux, z, d0, y, states, slope, u, stat2, expand, seg, rowp, colp, cw)

    wig = t_dot(h_all, dp).astype(BF16)
    dn_part = dot_t(dp, w_t).astype(BF16)
    dn = lax.psum_scatter(dn_part, "seq", scatter_dimension=0, tiled=True).astype(F32)

    n_own = DI // owners
    if owners % ranks == 0 and n_own % owners == 0:
        pieces = wog.reshape(owners // ranks, owners, n_own // owners, width)
        pieces = lax.psum_scatter(pieces, "head", scatter_dimension=1, tiled=False)
        pieces = lax.all_gather(pieces, "seq", axis=0, tiled=True)
        w_out_grad = lax.all_to_all(pieces, "head", 0, 0, tiled=True).reshape(n_own, width).astype(F32)
    else:
        full = lax.all_gather(lax.psum(wog, "head"), "seq", axis=0, tiled=True)
        w_out_grad = lax.dynamic_slice_in_dim(full, owner * n_own, n_own, 0).astype(F32)
    gate_gain_grad = jnp.sum(w_out.astype(F32) * w_out_grad, axis=1) / gate_gain.astype(F32)

    rows_in = lax.psum_scatter(wig, "head", scatter_dimension=0, tiled=True)
    rows_in = lax.all_gather(rows_in, "seq")
    bc_cols = jnp.sum(rows_in[:, :, 2 * wide : wide + chans].astype(F32), axis=0)
    raw_in = jnp.concatenate(
        [rows_in[r, :, :wide].astype(F32) for r in range(ranks)]
        + [rows_in[r, :, wide : 2 * wide].astype(F32) for r in range(ranks)]
        + [bc_cols],
        axis=1,
    )
    raw_dt = jnp.concatenate(
        [rows_in[r, :, wide + chans : wide + chans + heads].astype(F32) for r in range(ranks)], axis=1
    )
    w_in_grad = raw_in * gain_rows
    w_dt_grad = raw_dt * gain_rows
    norm_gain_grad = jnp.sum(raw_in * w_in.astype(F32), axis=1) + jnp.sum(raw_dt * w_dt.astype(F32), axis=1)

    h32 = hidden[0].astype(F32)
    own_r1m = lax.dynamic_slice_in_dim(r1m, rank * local_len, local_len, 0)[:, None]
    block_out = (h32 + own_r1m * branch.astype(F32)).astype(BF16)[None]
    r0 = lax.rsqrt(jnp.mean(h32 * h32, axis=1, keepdims=True) + EPS)
    mixed = jnp.sum(dn * h32, axis=1, keepdims=True) / width
    hidden_grad = (out_grad[0].astype(F32) + dn - h32 * (r0 * r0 * mixed))[None]

    def laid(v, total, size):
        base = jnp.zeros(v.shape[:-1] + (total,), F32)
        return lax.dynamic_update_slice_in_dim(base, v, rank * size, v.ndim - 1)

    conv_all = jnp.concatenate([laid(sm[:5, :wide], DI, wide), sm[:5, wide:]], axis=1)
    skip_h = jnp.sum(sm[5, :wide].reshape(heads, HEAD_DIM), axis=1)
    vec = jnp.stack([sm[6, :heads], sm[7, :heads], skip_h])
    packed = jnp.concatenate([conv_all.reshape(-1), laid(vec, HEADS, heads).reshape(-1)])
    packed = lax.psum(packed, EVERY)
    n_conv = 5 * CHANNELS
    conv_all = packed[:n_conv].reshape(5, CHANNELS)
    vec = packed[n_conv:].reshape(3, HEADS)
    conv_own = lax.dynamic_slice_in_dim(conv_all, owner * cs, cs, 1)
    vec_own = lax.dynamic_slice_in_dim(vec, owner * hs, hs, 1)

    return (
        block_out,
        hidden_grad,
        norm_gain_grad,
        w_in_grad,
        w_dt_grad,
        conv_own[:KERNEL],
        conv_own[KERNEL],
        vec_own[0],
        vec_own[1],
        vec_own[2],
        gate_gain_grad,
        w_out_grad,
    )


def solution(mesh):
    rows = P("head", "seq", None)
    return jax.shard_map(
        local,
        mesh=mesh,
        in_specs=(
            rows, P("head"), rows, P("head"), P("head", None), P("head", None), P(None, "head"),
            P("head"), P("head"), P("head"), P("head"), P("head"), P("head", None),
        ),
        out_specs=(
            rows, rows, P("head"), P("head", None), P("head", None), P(None, "head"),
            P("head"), P("head"), P("head"), P("head"), P("head"), P("head", None),
        ),
        check_vma=False,
    )
```

time: 3790 us -> 1210 us (0.32)
  waiting for transfers between devices: 1630 us -> 793 us
  blocking collectives: 805 us -> 41.8 us
  other arithmetic: 473 us -> 36.5 us
  matrix products: 447 us -> 98.8 us
  local copies, waits for them, and re-layouts: 344 us -> 65.3 us
  Pallas kernels: 0 us -> 137 us
  starting transfers between devices: 51.7 us -> 5.85 us
    reduce_scatter x4 -> x3, waiting for transfers between devices: 779 us -> 224 us  [the longest x1 87.2 us: local(): branch = lax.psum_scatter(partial, 'seq', scatter_dimension=0, tiled=True)]
    all_gather x10 -> x0, blocking collectives: 514 us -> none  [the longest x2 372 us: fetch_weights(): lax.all_gather(shards[8], 'head', axis=0, tiled=True)]
    dot_general x46 -> x5, matrix products: 428 us -> 98.8 us  [the longest x2 42.4 us: dot_t(): lax.dot_general(a, b, (((1,), (1,)), ((), ())), preferred_element_type=F32)]
    all_to_all x7 -> x1, waiting for transfers between devices: 200 us -> 0.01 us  [local(): lax.all_to_all(pieces, 'head', 0, 0, tiled=True).reshape(n_own, width)]
    all_to_all x2 -> x0, blocking collectives: 171 us -> none  [the longest x1 159 us: run_backward(): lax.all_to_all(d_x.astype(jnp.bfloat16), 'head', split_axis=0, concat_axi...]
    another operation x46 -> x2, other arithmetic: 165 us -> 0.02 us  [the longest x1 0.01 us: local(): jnp.stack([jnp.repeat(rate, HEAD_DIM), jnp.repeat(mine(skip_all, heads).a...]
    pallas_call x0 -> x3, Pallas kernels: none -> 137 us  [the longest x1 64.6 us: local(): pl.pallas_call(functools.partial(back_kernel, heads=heads, wide=wide), gr...]
    all_gather x9 -> x6, waiting for transfers between devices: 538 us -> 429 us  [the longest x1 150 us: local(): lax.all_gather(w_out, 'head', axis=0, tiled=True)]
  transfers between devices with their start and end apart: 25 -> 12, of which waited for: 15 -> 11; matrix products, arithmetic and copies ran while one was open for 16% -> 9% of each run, Pallas kernels for 0% -> 9%
where the time goes in v1:
time: 1210 us; the launch traced here: 1190 us
  waiting for transfers between devices  793 us (66%)
  Pallas kernels  137 us (11%)
  matrix products  98.8 us (8%)
  local copies, waits for them, and re-layouts  65.3 us (5%)
  blocking collectives  41.8 us (3%)
  other arithmetic  36.5 us (3%)
  between operations  16.2 us (1%)
    all_gather x1, waiting for transfers between devices, local(): lax.all_gather(w_out, 'head', axis=0, tiled=True)  150 us
    psum x1, waiting for transfers between devices, local(): packed = lax.psum(packed, EVERY)  136 us
    all_gather x1, waiting for transfers between devices, local(): w_t = lax.all_gather(sent, 'head', axis=0, tiled=True)  94.5 us
    reduce_scatter x1, waiting for transfers between devices, local(): branch = lax.psum_scatter(partial, 'seq', scatter_dimension=0, tiled=True)  87.2 us
    reduce_scatter x1, waiting for transfers between devices, local(): lax.psum_scatter(dn_part, 'seq', scatter_dimension=0, tiled=True)  80.2 us
    pallas_call x1, Pallas kernels, local(): pl.pallas_call(functools.partial(back_kernel, heads=heads, wide=wide), gr...  64.6 us
    reduce_scatter x1, waiting for transfers between devices, local(): rows_in = lax.psum_scatter(wig, 'head', scatter_dimension=0, tiled=True)  57.1 us
    all_gather x1, waiting for transfers between devices, local(): rows_in = lax.all_gather(rows_in, 'seq')  54 us
  transfers between devices with their start and end apart: 12, of which 11 were waited for; matrix products, arithmetic and copies ran while one was open for 9% of the time, Pallas kernels for 9%

profile of v1, /device:TPU:8, one launch (start us, length us, event | category | flops | bytes accessed | tf_op | source)
XLA Modules:
  0.0 1194.4 jit_solution(7335542695006288365)
XLA Ops:
  9.5 1.0 multiply_convert_fusion.6
  10.5 1.4 multiply_convert_fusion.4
  12.0 2.0 concatenate.36
  17.2 25.6 %all-reduce.4 = bf16[26048]{0:T(1024)(128)(2,1)S(1)} all-reduce(bf16[26048]{0:T(1024)(128)(2,1)S(1)} %dynamic-update-slice), channel_id=3, replica_groups=mesh['seq'=4,'head'=8] {'head'}, use_global_device_ids=true, to_apply=%add.4 | all-reduce | flops 26048 | bytes 104192
  48.1 50.7 %all-gather.16.cloned.1.call-done = bf16[1,2048,2048]{2,1,0:T(8,128)(2,1)} async-done(((bf16[1,512,2048]{2,1,0:T(8,128)(2,1)}), bf16[1,2048,2048]{2,1,0:T(8,128)(2,1)}) %all-gather.16.cloned.1.call-update) | async-done | bytes 8388624 | tf_op jit(solution)/shard_map/all_gather | solution.py:343
  98.8 94.5 %all-gather.12.cloned.1.call-done.w_ref = bf16[2048,2432]{1,0:T(8,128)(2,1)} async-done(((bf16[256,2432]{1,0:T(8,128)(2,1)}), bf16[2048,2432]{1,0:T(8,128)(2,1)}) %all-gather.12.cloned.1.call-update) | async-done | bytes 9961488 | tf_op jit(solution)/shard_map/all_gather | solution.py:341
  194.5 48.1 %project.1 = (bf16[2048,1024]{1,0:T(8,128)(2,1)}, bf16[2048,1280]{1,0:T(8,128)(2,1)}, bf16[2048,1280]{1,0:T(8,128)(2,1)}, bf16[2048,1280]{1,0:T(8,128)(2,1)}, f32[2048,128]{1,0:T(8,128)}) custom-call(bf16[2048,2048]{1,0:T(8,128)(2,1)} %bitcast.136, bf16[2048,2432]{1,0:T(8,128)(2,1)} %all-gather.12.cloned.1.call-done.w_ref, f32[8,1280]{1,0:T(8,128)} %fusion.23.cw_ref, ...), custom_call_target="tpu_custom_call" | custom-call | flops 20401094656 | bytes 29360128 | tf_op jit(solution)/shard_map/project/pallas_call | solution.py:363
  242.7 41.4 %all-gather.18.cloned.1.call-done = bf16[1,2048,2048]{2,1,0:T(8,128)(2,1)} async-done(((bf16[1,512,2048]{2,1,0:T(8,128)(2,1)}), bf16[1,2048,2048]{2,1,0:T(8,128)(2,1)}) %all-gather.18.cloned.1.call-update) | async-done | bytes 8388624 | tf_op jit(solution)/shard_map/all_gather | solution.py:344
  284.0 149.6 %all-gather.14.cloned.1.call-done = bf16[4096,2048]{1,0:T(8,128)(2,1)} async-done(((bf16[512,2048]{1,0:T(8,128)(2,1)}), bf16[4096,2048]{1,0:T(8,128)(2,1)}) %all-gather.14.cloned.1.call-update) | async-done | bytes 16777232 | tf_op jit(solution)/shard_map/all_gather | solution.py:342
  433.6 13.9 %convert_bitcast_fusion.d0_ref = bf16[2048,1024]{1,0:T(8,128)(2,1)} fusion(bf16[1,2048,2048]{2,1,0:T(8,128)(2,1)} %all-gather.18.cloned.1.call-done, bf16[4096,2048]{1,0:T(8,128)(2,1)} %all-gather.14.cloned.1.call-done, s32[]{:T(128)S(6)} %select_n.53), kind=kOutput, calls=%fused_computation.23 | convolution fusion | flops 8592031744 | bytes 16777220 | tf_op jit(solution)/shard_map/dot_general | solution.py:30
  448.2 24.1 %scan.1 = (f32[2048,1024]{1,0:T(8,128)}, bf16[2048,1024]{1,0:T(8,128)(2,1)}, f32[8,128,1024]{2,1,0:T(8,128)}, f32[2048,128]{1,0:T(8,128)}) custom-call(bf16[2048,1280]{1,0:T(8,128)(2,1)} %get-tuple-element.23.act_ref, f32[2048,128]{1,0:T(8,128)} %get-tuple-element.24.aux_ref, bf16[2048,1024]{1,0:T(8,128)(2,1)} %get-tuple-element.25.z_ref, ...), custom_call_target="tpu_custom_call" | custom-call | flops 6442450944 | bytes 33554432 | tf_op jit(solution)/shard_map/scan/pallas_call | solution.py:385
  472.3 1.6 copy.77
  473.8 16.2 %psum.14 = f32[2,16,128]{2,1,0:T(8,128)S(1)} all-reduce(f32[2,16,128]{2,1,0:T(8,128)S(1)} %copy.77), channel_id=1, replica_groups=mesh['seq'=4,'head'=8] {'seq'}, use_global_device_ids=true, to_apply=%region_0.1 | all-reduce | flops 4096 | bytes 32768 | tf_op jit(solution)/shard_map/psum | solution.py:409
  490.1 14.5 %fusion.13 = bf16[1024,2048]{1,0:T(8,128)(2,1)} fusion(bf16[2048,1024]{1,0:T(8,128)(2,1)} %get-tuple-element.27, bf16[1,2048,2048]{2,1,0:T(8,128)(2,1)} %all-gather.18.cloned.1.call-done, f32[2048]{0:T(1024)S(1)} %get-tuple-element.39), kind=kOutput, calls=%fused_computation.24 | convolution fusion | flops 8604614656 | bytes 16785408 | tf_op jit(solution)/shard_map/dot_general | solution.py:34
  504.6 1.6 select_select_fusion.stat_ref
  506.2 64.6 %scan_back.1 = (bf16[2048,2432]{1,0:T(8,128)(2,1)}, f32[8,1280]{1,0:T(8,128)}) custom-call(bf16[2048,1280]{1,0:T(8,128)(2,1)} %get-tuple-element.23.act_ref, f32[2048,128]{1,0:T(8,128)} %get-tuple-element.24.aux_ref, bf16[2048,1024]{1,0:T(8,128)(2,1)} %get-tuple-element.25.z_ref, bf16[2048,1024]{1,0:T(8,128)(2,1)} %convert_bitcast_fusion.d0_ref, ...), custom_call_target="tpu_custom_call" | custom-call | flops 12884901888 | bytes 50331648 | tf_op jit(solution)/shard_map/scan_back/pallas_call | solution.py:423
  570.8 27.8 %fusion = bf16[2048,2432]{0,1:T(8,128)(2,1)} fusion(bf16[2048,2432]{1,0:T(8,128)(2,1)} %get-tuple-element.32, bf16[1,2048,2048]{2,1,0:T(8,128)(2,1)} %all-gather.16.cloned.1.call-done), kind=kOutput, calls=%fused_computation.2 | convolution fusion | flops 20406075392 | bytes 28311552 | tf_op jit(solution)/shard_map/dot_general | solution.py:34
  598.7 1.7 all-reduce.11.cloned.1.call-done
  600.4 2.5 constant_dynamic-slice_fusion.3
  604.3 28.6 %convolution_convert_fusion.1 = bf16[2048,2048]{1,0:T(8,128)(2,1)} fusion(bf16[2048,2432]{1,0:T(8,128)(2,1)} %get-tuple-element.32, bf16[2048,2432]{1,0:T(8,128)(2,1)} %all-gather.12.cloned.1.call-done.w_ref), kind=kOutput, calls=%fused_computation.9 | convolution fusion | flops 20405288960 | bytes 28311552 | tf_op jit(solution)/shard_map/dot_general | solution.py:30
  633.0 14.0 %convolution_convert_fusion.2 = bf16[2048,2048]{1,0:T(8,128)(2,1)} fusion(bf16[2048,1024]{1,0:T(8,128)(2,1)} %get-tuple-element.27, bf16[4096,2048]{1,0:T(8,128)(2,1)} %all-gather.14.cloned.1.call-done, s32[]{:T(128)S(6)} %select_n.53), kind=kOutput, calls=%fused_computation.10 | convolution fusion | flops 8594128896 | bytes 16777220 | tf_op jit(solution)/shard_map/dot_general | solution.py:26
  647.1 57.1 %reduce-scatter.11.cloned.1.call-done = bf16[256,2432]{0,1:T(8,128)(2,1)} async-done(((bf16[2048,2432]{0,1:T(8,128)(2,1)}), bf16[256,2432]{0,1:T(8,128)(2,1)}) %reduce-scatter.11.cloned.1.call-update) | async-done | bytes 1245200 | tf_op jit(solution)/shard_map/reduce_scatter | solution.py:457
  704.3 39.0 %all-gather.22.cloned.1.call-done = bf16[8,1,64,2048]{3,2,1,0:T(8,128)(2,1)} async-done(((bf16[2,1,64,2048]{3,2,1,0:T(8,128)(2,1)}), bf16[8,1,64,2048]{3,2,1,0:T(8,128)(2,1)}) %all-gather.22.cloned.1.call-update) | async-done | bytes 2097168 | tf_op jit(solution)/shard_map/all_gather | solution.py:450
  743.2 5.4 all-to-all-start
  748.7 135.8 %all-reduce.9.cloned.1.call-done = f32[21952]{0:T(1024)} async-done(((f32[21952]{0:T(1024)}), f32[21952]{0:T(1024)}) %all-reduce.9.cloned.1.call-update) | async-done | bytes 87824 | tf_op jit(solution)/shard_map/psum | solution.py:488
  888.2 4.8 multiply_reduce_fusion.1
  893.6 80.2 %reduce-scatter.9.cloned.1.call-done = bf16[512,2048]{1,0:T(8,128)(2,1)} async-done(((bf16[2048,2048]{1,0:T(8,128)(2,1)}), bf16[512,2048]{1,0:T(8,128)(2,1)}) %reduce-scatter.9.cloned.1.call-update) | async-done | bytes 2097168 | tf_op jit(solution)/shard_map/reduce_scatter | solution.py:444
  973.7 2.5 fusion.9
  976.2 87.2 %reduce-scatter.7.cloned.1.call-done = bf16[512,2048]{1,0:T(8,128)(2,1)} async-done(((bf16[2048,2048]{1,0:T(8,128)(2,1)}), bf16[512,2048]{1,0:T(8,128)(2,1)}) %reduce-scatter.7.cloned.1.call-update) | async-done | bytes 2097168 | tf_op jit(solution)/shard_map/reduce_scatter | solution.py:418
  1063.4 7.0 fusion.7
  1070.3 54.0 %all-gather.20.cloned.1.call-done = bf16[1024,2432]{0,1:T(8,128)(2,1)} async-done(((bf16[256,2432]{0,1:T(8,128)(2,1)}), bf16[1024,2432]{0,1:T(8,128)(2,1)}) %all-gather.20.cloned.1.call-update) | async-done | bytes 4980752 | tf_op jit(solution)/shard_map/all_gather | solution.py:458
  1124.3 10.0 reshape.222
  1134.3 1.0 fusion.37
  1135.3 1.8 convert_reduce_fusion
  1137.1 14.8 %fusion.38 = (bf16[1,256,1024]{1,0,2:T(2,128)(2,1)}, bf16[1,256,1024]{1,0,2:T(2,128)(2,1)}, bf16[1,256,1024]{1,0,2:T(2,128)(2,1)}, bf16[1,256,1024]{1,0,2:T(2,12...) fusion(bf16[4,256,2432]{1,0,2:T(4,128)(2,1)} %reshape.222), kind=kLoop, calls=%fused_computation.106 | loop fusion | bytes 8388608 | tf_op jit(solution)/shard_map/slice | solution.py:462
  1152.7 3.5 copy.101
  1156.2 3.5 copy.100
  1159.7 3.5 copy.99
  1163.2 3.5 copy.98
  1166.8 3.5 copy.97
  1170.2 2.3 copy.96
  1172.5 1.3 copy.95
  1173.8 1.3 copy.94
  1175.4 1.2 convert_dynamic-update-slice_fusion.5
  1176.6 1.3 convert_dynamic-update-slice_fusion.4
  1177.8 1.3 convert_dynamic-update-slice_fusion.3
  1179.1 1.1 convert_dynamic-update-slice_fusion.2
  1181.4 4.9 broadcast_multiply_fusion
  (145 shorter events, 20.3 us)
Async XLA Ops:
  7.2 8.3 copy-start.11
  7.2 8.2 copy-start.7
  7.2 9.5 copy-start.8
  7.2 9.5 copy-start.14
  7.2 9.5 copy-start.13
  7.2 9.5 copy-start.12
  7.2 9.5 copy-start.10
  7.3 91.5 %all-gather.16.cloned.1.call-start = ((), (), s32[]{:S(2)}) async-start(), calls=%async_computation.10 | async-start | bytes 10485760 | tf_op jit(solution)/shard_map/all_gather | solution.py:343
  8.0 185.3 %all-gather.12.cloned.1.call-start = ((), (), s32[]{:S(2)}) async-start(), calls=%async_computation.4 | async-start | bytes 11206656 | tf_op jit(solution)/shard_map/all_gather | solution.py:341
  8.7 3.3 copy-start.5
  14.0 270.0 %all-gather.18.cloned.1.call-start = ((), (), s32[]{:S(2)}) async-start(), calls=%async_computation.11 | async-start | bytes 10485760 | tf_op jit(solution)/shard_map/all_gather | solution.py:344
  14.7 418.9 %all-gather.14.cloned.1.call-start = ((), (), s32[]{:S(2)}) async-start(), calls=%async_computation.5 | async-start | bytes 18874368 | tf_op jit(solution)/shard_map/all_gather | solution.py:342
  15.3 585.1 %all-reduce.11.cloned.1.call-start = ((), (), s32[]{:S(2)}) async-start(), calls=%async_computation.14 | async-start | bytes 8388608
  504.6 199.7 %reduce-scatter.11.cloned.1.call-start = ((), (), s32[]{:S(2)}) async-start(), calls=%async_computation.8 | async-start | bytes 11206656 | tf_op jit(solution)/shard_map/reduce_scatter | solution.py:457
  598.7 4.4 copy-start.3
  598.7 144.5 %all-gather.22.cloned.1.call-start = ((), (), s32[]{:S(2)}) async-start(), calls=%async_computation.13 | async-start | bytes 2621440 | tf_op jit(solution)/shard_map/all_gather | solution.py:450
  603.0 281.6 %all-reduce.9.cloned.1.call-start = ((), (), s32[]{:S(2)}) async-start(), calls=%async_computation.9 | async-start | bytes 180224 | tf_op jit(solution)/shard_map/psum | solution.py:488
  604.3 369.4 %reduce-scatter.9.cloned.1.call-start = ((), (), s32[]{:S(2)}) async-start(), calls=%async_computation.7 | async-start | bytes 10485760 | tf_op jit(solution)/shard_map/reduce_scatter | solution.py:444
  632.9 430.4 %reduce-scatter.7.cloned.1.call-start = ((), (), s32[]{:S(2)}) async-start(), calls=%async_computation.6 | async-start | bytes 10485760 | tf_op jit(solution)/shard_map/reduce_scatter | solution.py:418
  647.0 245.9 %copy-start.9 = (bf16[512]{0:T(512)(128)(2,1)S(1)}, bf16[512]{0:T(512)(128)(2,1)}, u32[]{:S(2)}) copy-start(bf16[512]{0:T(512)(128)(2,1)} %param.24) | copy-start | bytes 3076
  647.1 326.7 %copy-start = (bf16[1,512,2048]{2,1,0:T(8,128)(2,1)S(1)}, bf16[1,512,2048]{2,1,0:T(8,128)(2,1)}, u32[]{:S(2)}) copy-start(bf16[1,512,2048]{2,1,0:T(8,128)(2,1)} %param.13) | copy-start | bytes 6291460
  647.1 477.3 %all-gather.20.cloned.1.call-start = ((), (), s32[]{:S(2)}) async-start(), calls=%async_computation.12 | async-start | bytes 6225920 | tf_op jit(solution)/shard_map/all_gather | solution.py:458
  743.2 145.0 %all-to-all-start = ((bf16[8,64,2048]{2,1,0:T(8,128)(2,1)}), bf16[8,64,2048]{2,1,0:T(8,128)(2,1)}, u32[]{:S(2)}, u32[]{:S(2)}) async-start(bf16[8,64,2048]{2,1,0:T(8,128)(2,1)} %bitcast.124), calls=%async_computation.3 | async-start | bytes 4194304 | tf_op jit(solution)/shard_map/all_to_all | solution.py:451
  1172.5 8.9 slice-start
  1172.5 8.9 copy-start.6
  1175.2 5.0 copy-start.2
  1175.2 5.1 copy-start.1
  1176.6 4.8 slice-start.1
  1181.4 4.9 copy-start.4
Sparse Core Ops, SparseCore 0:
  9.9 88.8 all-gather.15
  101.0 92.2 all-gather.11
  195.2 88.8 all-gather.17
  285.5 148.1 all-gather.13
  504.7 95.6 all-reduce.10
  602.6 101.6 reduce-scatter.10
  706.7 36.5 all-gather.21
  749.4 135.1 all-reduce.8
  888.2 85.4 reduce-scatter.8
  976.9 86.4 reduce-scatter.6
  1065.2 59.0 all-gather.19

commit v2 on v1

--- a/solution.py
+++ b/solution.py
@@ -38,41 +38,310 @@
     return 1.0 / (1.0 + jnp.exp(-v))
 
 
-def project_kernel(h_ref, w_ref, cw_ref, cb_ref, dtb_ref, z_ref, u_ref, act_ref, slope_ref, aux_ref, ext, *, heads, wide):
-    step = pl.program_id(0)
-    rows = h_ref.shape[0]
-    chans = u_ref.shape[1]
-    h = h_ref[...]
-    h32 = h.astype(F32)
-    r0 = lax.rsqrt(jnp.mean(h32 * h32, axis=1, keepdims=True) + EPS)
-    z_ref[...] = (dot(h, w_ref[:, :wide]) * r0).astype(BF16)
-    u = (dot(h, w_ref[:, wide : wide + chans]) * r0).astype(BF16)
-    dt_raw = dot(h, w_ref[:, wide + chans :]) * r0
-
-    @pl.when(step == 0)
-    def _():
-        ext[0:8, :] = jnp.zeros((8, chans), F32)
-
-    @pl.when(step > 0)
-    def _():
-        ext[0:8, :] = ext[rows : rows + 8, :]
-
-    u_ref[...] = u
-    ext[8 : rows + 8, :] = u.astype(F32)
-    pre = cb_ref[0:1, :]
-    for k in range(KERNEL):
-        pre = pre + cw_ref[k : k + 1, :] * ext[pl.ds(8 - (KERNEL - 1) + k, rows), :]
-    sig = sigmoid(pre)
-    act_ref[...] = (pre * sig).astype(BF16)
-    slope_ref[...] = (sig * (1.0 + pre * (1.0 - sig))).astype(BF16)
-    v = dt_raw + dtb_ref[0:1, :]
-    soft = jnp.maximum(v, 0.0) + jnp.log1p(jnp.exp(-jnp.abs(v)))
-    soft = soft.astype(BF16).astype(F32)
-    lane = lax.broadcasted_iota(jnp.int32, v.shape, 1)
-    aux = jnp.where(lane < heads, soft, 0.0)
-    sig_v = pltpu.roll(sigmoid(v), heads, 1)
-    aux = jnp.where((lane >= heads) & (lane < 2 * heads), sig_v, aux)
-    aux_ref[...] = jnp.where(lane == 2 * heads, r0, aux)
+def remote(src, dst, send, recv, target):
+    return pltpu.make_async_remote_copy(
+        src_ref=src, dst_ref=dst, send_sem=send, recv_sem=recv, device_id=target, device_id_type=pl.DeviceIdType.MESH
+    )
+
+
+def greet(peers, extra=()):
+    barrier = pltpu.get_barrier_semaphore()
+    count = len(peers)
+
+    def hello(peer):
+        pl.semaphore_signal(barrier, inc=1, device_id=peer, device_id_type=pl.DeviceIdType.MESH)
+
+    for peer in peers:
+        hello(peer)
+    for there, peer in extra:
+        pl.when(there)(functools.partial(hello, peer))
+        count = count + jnp.where(there, 1, 0)
+    pl.semaphore_wait(barrier, count)
+
+
+def gather_kernel(
+    hid_ref, og_ref, w_ref, wo_in_ref, gain_ref, dtw_ref,
+    hall_ref, ogall_ref, wt_ref, wo_ref, z_ref, u_ref, d_ref, d0_ref,
+    hv, ov, wv, wov, stage, zv, uv, dv, d0v,
+    h_send, h_recv, o_send, o_recv, z_up, z_dn, z_recv, s_send, s_recv,
+    c_up, c_dn, c_recv, t_send, t_recv, local_sem, out_sem, *, ring, wide,
+):
+    s = lax.axis_index("seq")
+    q = hid_ref.shape[0]
+    half = q // 2
+    x_peer = s + 1 - 2 * lax.rem(s, 2)
+    y_peer = lax.rem(s + 2, 4)
+    far = 3 - s
+    to_x, to_y = {"seq": x_peer}, {"seq": y_peer}
+    chans = uv.shape[1]
+    n_main = stage.shape[1]
+    n = stage.shape[0]
+    peers = [to_x, to_y]
+    extra = []
+
+    def block(ref, at, start, size):
+        return ref.at[pl.ds(pl.multiple_of(at * q + start, 16), size), :]
+
+    if ring:
+        h = lax.axis_index("head")
+        core = lax.rem(h, 2)
+        r = h // 2
+        last = lax.axis_size("head") // 2 - 1
+        to_sib, to_up, to_down = {"head": h + 1 - 2 * core}, {"head": lax.rem(h + 2, 2 * last + 2)}, {"head": lax.rem(h + 2 * last, 2 * last + 2)}
+        above, below = r < last, r > 0
+        peers.append(to_sib)
+        extra = [(above, to_up), (below, to_down)]
+        first = pl.multiple_of(s * wide, LANES)
+        second = pl.multiple_of(DI + s * wide, LANES)
+        loads = [
+            pltpu.make_async_copy(w_ref.at[:, pl.ds(first, wide)], stage.at[:, :wide], local_sem.at[0]),
+            pltpu.make_async_copy(w_ref.at[:, pl.ds(second, wide)], stage.at[:, wide : 2 * wide], local_sem.at[1]),
+            pltpu.make_async_copy(w_ref.at[:, 2 * DI :], stage.at[:, 2 * wide :], local_sem.at[2]),
+        ]
+        is_root = r == s
+        n_o = wov.shape[0] // 2
+        load_o = pltpu.make_async_copy(
+            wo_in_ref, wov.at[pl.ds(pl.multiple_of(core * n_o, 16), n_o), :], local_sem.at[5]
+        )
+        pl.when(is_root)(load_o.start)
+    else:
+        loads = [
+            pltpu.make_async_copy(w_ref, wv, local_sem.at[0]),
+            pltpu.make_async_copy(wo_in_ref, wov, local_sem.at[5]),
+        ]
+    for copy in loads:
+        copy.start()
+    own_h = pltpu.make_async_copy(hid_ref, block(hv, s, 0, q), local_sem.at[3])
+    own_o = pltpu.make_async_copy(og_ref, block(ov, s, 0, q), local_sem.at[4])
+    own_h.start()
+    own_o.start()
+    greet(peers, extra)
+
+    sent = []
+
+    def send(src, dst, sems, i, target):
+        copy = remote(src, dst, sems[0].at[i], sems[1].at[i], target)
+        copy.start()
+        sent.append(copy)
+        return copy
+
+    def open_exchange(src, buf, sems):
+        return (
+            send(src, block(buf, s, 0, q), sems, 0, to_x),
+            send(src, block(buf, s, 0, q), sems, 1, to_y),
+        )
+
+    def relay(buf, sems, heads_in):
+        heads_in[0].wait_recv()
+        a = block(buf, x_peer, 0, half)
+        first = send(a, a, sems, 2, to_y)
+        heads_in[1].wait_recv()
+        b = block(buf, y_peer, half, half)
+        return first, send(b, b, sems, 3, to_x)
+
+    h_sems, o_sems = (h_send, h_recv), (o_send, o_recv)
+    h_open = open_exchange(hid_ref, hv, h_sems)
+
+    closing = []
+    if ring:
+        def w_block(at):
+            return wv.at[pl.ds(pl.multiple_of((2 * at + core) * n, 16), n), :]
+
+        def w_copy(at, sems, target):
+            return remote(w_block(at), w_block(at), sems.at[at], z_recv.at[at], target)
+
+        def w_swap(at):
+            return remote(w_block(at), w_block(at), s_send.at[at], s_recv.at[at], to_sib)
+
+        def launch(there, make):
+            @pl.when(there)
+            def _():
+                make().start()
+
+            def finish():
+                @pl.when(there)
+                def _():
+                    make().wait_send()
+
+            closing.append(finish)
+
+        always = r >= 0
+
+        def w_step(k):
+            lower, upper = r - k, r + k
+            has_lower, has_upper = lower >= 0, upper <= last
+
+            @pl.when(has_lower)
+            def _():
+                w_copy(lower, z_up, to_up).wait_recv()
+
+            launch(has_lower & above, lambda: w_copy(lower, z_up, to_up))
+            launch(has_lower, lambda: w_swap(lower))
+
+            @pl.when(has_upper)
+            def _():
+                w_copy(upper, z_dn, to_down).wait_recv()
+
+            launch(has_upper & below, lambda: w_copy(upper, z_dn, to_down))
+            launch(has_upper, lambda: w_swap(upper))
+
+        chunks = c_recv.shape[0]
+        n_c = n_o // chunks
+        dist = jnp.where(r > s, r - s, s - r)
+
+        def o_block(i):
+            return wov.at[pl.ds(pl.multiple_of(core * n_o + i * n_c, 16), n_c), :]
+
+        def o_copy(i, sems, target):
+            return remote(o_block(i), o_block(i), sems.at[i], c_recv.at[i], target)
+
+        def o_swap(i):
+            return remote(o_block(i), o_block(i), t_send.at[i], t_recv.at[i], to_sib)
+
+        def o_root():
+            @pl.when(is_root)
+            def _():
+                load_o.wait()
+
+            for i in range(chunks):
+                launch(is_root & above, lambda i=i: o_copy(i, c_up, to_up))
+                launch(is_root & below, lambda i=i: o_copy(i, c_dn, to_down))
+                launch(is_root, lambda i=i: o_swap(i))
+
+        def o_tick(t):
+            i = t - dist
+            live = (dist >= 1) & (i >= 0) & (i < chunks)
+
+            @pl.when(live)
+            def _():
+                o_copy(i, c_up, to_up).wait_recv()
+
+            pl.when(live & (r > s) & above)(lambda: o_copy(i, c_up, to_up).start())
+            pl.when(live & (r < s) & below)(lambda: o_copy(i, c_dn, to_down).start())
+            pl.when(live)(lambda: o_swap(i).start())
+
+        def o_finish():
+            for i in range(chunks):
+                pl.when((r > s) & above)(lambda: o_copy(i, c_up, to_up).wait_send())
+                pl.when((r < s) & below)(lambda: o_copy(i, c_dn, to_down).wait_send())
+                pl.when(dist >= 1)(lambda: o_swap(i).wait_send())
+
+        closing.append(o_finish)
+        for copy in loads:
+            copy.wait()
+        own = pl.ds(pl.multiple_of(h * n, 16), n)
+        wv[own, :n_main] = (stage[...].astype(F32) * gain_ref[...]).astype(BF16)
+        wv[own, n_main:] = dtw_ref[...]
+        launch(above, lambda: w_copy(r, z_up, to_up))
+        launch(below, lambda: w_copy(r, z_dn, to_down))
+        launch(always, lambda: w_swap(r))
+        w_step(1)
+    else:
+        for copy in loads:
+            copy.wait()
+
+    h_far = relay(hv, h_sems, h_open)
+    if ring:
+        w_step(2)
+        o_root()
+    for copy in h_far:
+        copy.wait_recv()
+    o_open = open_exchange(og_ref, ov, o_sems)
+    if ring:
+        o_tick(1)
+        w_step(3)
+        for at in range(4):
+            w_swap(at).wait_recv()
+    own_h.wait()
+    own_o.wait()
+
+    rows = min(CHUNK, q)
+
+    def cut(at_block):
+        return pl.ds(pl.multiple_of(at_block * q, 16), q)
+
+    def project_outs(at_block, i):
+        at = cut(at_block)
+        pairs = ((hv, hall_ref), (zv, z_ref), (uv, u_ref), (dv, d_ref))
+        return [
+            pltpu.make_async_copy(src.at[at, :], dst.at[at, :], out_sem.at[4 * i + k])
+            for k, (src, dst) in enumerate(pairs)
+        ]
+
+    def pull_outs(at_block, i):
+        at = cut(at_block)
+        pairs = ((ov, ogall_ref), (d0v, d0_ref))
+        return [
+            pltpu.make_async_copy(src.at[at, :], dst.at[at, :], out_sem.at[16 + 2 * i + k])
+            for k, (src, dst) in enumerate(pairs)
+        ]
+
+    def nth(i):
+        return jnp.where(i == 0, s, jnp.where(i == 1, x_peer, jnp.where(i == 2, y_peer, far)))
+
+    w_out = pltpu.make_async_copy(wv, wt_ref, out_sem.at[24])
+    o_out = pltpu.make_async_copy(wov, wo_ref, out_sem.at[25])
+    w_out.start()
+
+    def project(at_block):
+        @pl.loop(0, q // rows)
+        def _(j):
+            at = pl.ds(pl.multiple_of(at_block * q + j * rows, 16), rows)
+            hb = hv[at, :]
+            h32 = hb.astype(F32)
+            r0 = lax.rsqrt(jnp.mean(h32 * h32, axis=1, keepdims=True) + EPS)
+            zv[at, :] = (dot(hb, wv[:, :wide]) * r0).astype(BF16)
+            uv[at, :] = (dot(hb, wv[:, wide : wide + chans]) * r0).astype(BF16)
+            raw = dot(hb, wv[:, wide + chans :]) * r0
+            lane = lax.broadcasted_iota(jnp.int32, raw.shape, 1)
+            dv[at, :] = jnp.where(lane == LANES - 1, r0, raw)
+
+    def pull(at_block):
+        at = cut(at_block)
+
+        @pl.loop(0, wide // 256)
+        def _(j):
+            to = pl.ds(pl.multiple_of(j * 256, 256), 256)
+            d0v[at, to] = dot_t(ov[at, :], wov[to, :]).astype(BF16)
+
+    @pl.loop(0, 4)
+    def _(i):
+        at_block = nth(i)
+        project(at_block)
+        for copy in project_outs(at_block, i):
+            copy.start()
+        if ring:
+            o_tick(2 + i)
+
+    o_far = relay(ov, o_sems, o_open)
+    if ring:
+        o_tick(6)
+        for i in range(chunks):
+            o_swap(i).wait_recv()
+    o_out.start()
+
+    @pl.loop(0, 4)
+    def _(i):
+        at_block = nth(i)
+
+        @pl.when(i == 3)
+        def _():
+            for copy in o_far:
+                copy.wait_recv()
+
+        pull(at_block)
+        for copy in pull_outs(at_block, i):
+            copy.start()
+
+    for i, at_block in enumerate((s, x_peer, y_peer, far)):
+        for copy in project_outs(at_block, i) + pull_outs(at_block, i):
+            copy.wait()
+    w_out.wait()
+    o_out.wait()
+    for copy in sent:
+        copy.wait_send()
+    for finish in closing:
+        finish()
 
 
 def decays(aux, heads, expand, rate_e, rate_row, rate_col):
@@ -90,20 +359,48 @@
     return causal, dt_e, cum_e, cum_c, cum_t
 
 
-def scan_kernel(act_ref, aux_ref, z_ref, d0_ref, exp_ref, rowp_ref, colp_ref, y_ref, gg_ref, st_ref, stat_ref, state, *, heads, wide):
+def scan_kernel(
+    u_ref, d_ref, z_ref, d0_ref, cw_ref, cb_ref, dtb_ref, exp_ref, rowp_ref, colp_ref,
+    act_ref, slope_ref, aux_ref, y_ref, gg_ref, st_ref, sum_ref, state, ext, *, heads, wide,
+):
     step = pl.program_id(0)
+    rows = u_ref.shape[0]
+    chans = u_ref.shape[1]
 
     @pl.when(step == 0)
     def _():
         state[...] = jnp.zeros_like(state)
-
-    rows = act_ref.shape[0]
-    x = act_ref[:, :wide]
+        ext[0:8, :] = jnp.zeros((8, chans), F32)
+
+    @pl.when(step > 0)
+    def _():
+        ext[0:8, :] = ext[rows : rows + 8, :]
+
+    ext[8 : rows + 8, :] = u_ref[...].astype(F32)
+    pre = cb_ref[0:1, :]
+    for k in range(KERNEL):
+        pre = pre + cw_ref[k : k + 1, :] * ext[pl.ds(8 - (KERNEL - 1) + k, rows), :]
+    sig = sigmoid(pre)
+    act = (pre * sig).astype(BF16)
+    act_ref[...] = act
+    slope_ref[...] = (sig * (1.0 + pre * (1.0 - sig))).astype(BF16)
+    raw = d_ref[...]
+    v = raw + dtb_ref[0:1, :]
+    soft = jnp.maximum(v, 0.0) + jnp.log1p(jnp.exp(-jnp.abs(v)))
+    soft = soft.astype(BF16).astype(F32)
+    lane = lax.broadcasted_iota(jnp.int32, v.shape, 1)
+    aux = jnp.where(lane < heads, soft, 0.0)
+    sig_v = pltpu.roll(sigmoid(v), heads, 1)
+    aux = jnp.where((lane >= heads) & (lane < 2 * heads), sig_v, aux)
+    aux = jnp.where(lane == LANES - 1, raw, aux)
+    aux_ref[...] = aux
+
+    x = act[:, :wide]
     x32 = x.astype(F32)
-    b = act_ref[:, wide : wide + STATE]
-    c = act_ref[:, wide + STATE :]
+    b = act[:, wide : wide + STATE]
+    c = act[:, wide + STATE :]
     causal, dt_e, cum_e, cum_c, cum_t = decays(
-        aux_ref[...], heads, exp_ref[...], rowp_ref[0:1, :], rowp_ref[3:4, :LANES], colp_ref[:, 0:1]
+        aux, heads, exp_ref[...], rowp_ref[0:1, :], rowp_ref[3:4, :LANES], colp_ref[:, 0:1]
     )
     xdt = x32 * dt_e
     xdt16 = xdt.astype(BF16)
@@ -128,13 +425,13 @@
     ssd = (y + rowp_ref[1:2, :] * x32).astype(BF16).astype(F32)
     z = z_ref[...].astype(F32)
     g = ssd * (z * sigmoid(z))
-    gain = rowp_ref[2:3, :]
-    gg = g * gain
+    gg = g * rowp_ref[2:3, :]
     gg_ref[...] = gg.astype(BF16)
-    ssq = jnp.sum(g * g, axis=1, keepdims=True)
-    cross = jnp.sum(gg * d0_ref[...].astype(F32), axis=1, keepdims=True)
-    lane = lax.broadcasted_iota(jnp.int32, (rows, LANES), 1)
-    stat_ref[...] = jnp.where(lane == 0, ssq, jnp.where(lane == 1, cross, 0.0))
+    ones = jnp.ones((8, wide), BF16)
+    ssq = dot_t(ones, (g * g).astype(BF16))
+    cross = dot_t(ones, (gg * d0_ref[...].astype(F32)).astype(BF16))
+    sub = lax.broadcasted_iota(jnp.int32, ssq.shape, 0)
+    sum_ref[...] = jnp.where(sub == 0, ssq, cross)
 
 
 def seg_dot(v, seg):
@@ -172,7 +469,7 @@
     stat = stat_ref[...]
     r1m = stat[:, 0:1]
     coef = stat[:, 1:2]
-    r0 = aux[:, 2 * heads : 2 * heads + 1]
+    r0 = aux[:, LANES - 1 : LANES]
     skip_e = rowp_ref[1:2, :]
     gain = rowp_ref[2:3, :]
 
@@ -268,6 +565,271 @@
     sm_ref[7:8, :LANES] += jnp.sum(dt * decay_grad, axis=0, keepdims=True)
 
 
+def grads_kernel(
+    dp_ref, w_ref, h_ref, piece_ref, tiny_ref,
+    dn_ref, win_ref, wout_ref,
+    dpv, wv, hb, far_p, y_p, x_p, far_a, far_b, y_f, x_f, dn_o, sib_s, mine_s, own_s, z_u, z_d, pv,
+    load_sem, hb_sem, d_send, d_recv, s_send, s_recv, zu_send, zu_recv, zd_send, zd_recv,
+    g_send, g_recv, p_send, p_recv, w_send, w_recv, out_sem,
+):
+    s = lax.axis_index("seq")
+    h = lax.axis_index("head")
+    owners = lax.axis_size("head")
+    last = owners // 2 - 1
+    core = lax.rem(h, 2)
+    r = h // 2
+    x_peer = s + 1 - 2 * lax.rem(s, 2)
+    y_peer = lax.rem(s + 2, 4)
+    far = 3 - s
+    to_x, to_y = {"seq": x_peer}, {"seq": y_peer}
+    to_sib = {"head": h + 1 - 2 * core}
+    to_up, to_down = {"head": lax.rem(h + 2, owners)}, {"head": lax.rem(h + owners - 2, owners)}
+    above, below = r < last, r > 0
+    q = far_p.shape[0]
+    half = q // 2
+    n, cols = own_s.shape[1], own_s.shape[2]
+    spare = LANES // 2
+    tiles = cols // LANES
+    edges = [LANES * (tiles * k // 4) for k in range(5)]
+    spans = list(zip(edges[:-1], edges[1:]))
+    sent = []
+    closing = []
+
+    def push(src, dst, sems, i, target):
+        copy = remote(src, dst, sems[0].at[i], sems[1].at[i], target)
+        copy.start()
+        sent.append(copy)
+        return copy
+
+    def launch(there, make):
+        @pl.when(there)
+        def _():
+            make().start()
+
+        def finish():
+            @pl.when(there)
+            def _():
+                make().wait_send()
+
+        closing.append(finish)
+
+    load_dp = pltpu.make_async_copy(dp_ref, dpv, load_sem.at[0])
+    load_w = pltpu.make_async_copy(w_ref, wv, load_sem.at[1])
+    load_dp.start()
+    load_w.start()
+
+    def chip(i):
+        return jnp.where(lax.rem(i, 2) == 0, last - i // 2, i // 2)
+
+    def load_h(i, other):
+        at = 2 * chip(i) + (1 - core if other else core)
+        slot = 0 if other else 1
+        return pltpu.make_async_copy(
+            h_ref.at[:, pl.ds(pl.multiple_of(at * n, LANES), n)], hb.at[slot], hb_sem.at[slot]
+        )
+
+    load_h(0, True).start()
+    load_h(0, False).start()
+    to_heads = [{"head": lax.rem(h + k, owners)} for k in range(1, owners)]
+    greet([to_x, to_y] + to_heads)
+
+    d_sems = (d_send, d_recv)
+    g_sems = (g_send, g_recv)
+
+    w_sems = (w_send, w_recv)
+    own_piece = pltpu.make_async_copy(piece_ref, pv.at[s], load_sem.at[2])
+    own_piece.start()
+    w0 = push(piece_ref, pv.at[s], w_sems, 0, to_x)
+    w1 = push(piece_ref, pv.at[s], w_sems, 1, to_y)
+    tile = 256
+
+    def part(block, out):
+        at = pl.ds(pl.multiple_of(block * q, 16), q)
+
+        @pl.loop(0, wv.shape[0] // tile)
+        def _(j):
+            to = pl.ds(pl.multiple_of(j * tile, tile), tile)
+            out[:, to] = dot_t(dpv[at, :], wv[to, :]).astype(BF16)
+
+    def add_to(out, at, extra):
+        out[at, :] = (out[at, :].astype(F32) + extra.astype(F32)).astype(BF16)
+
+    def swap(i):
+        t = chip(i)
+        return remote(sib_s.at[lax.rem(i, 2)], own_s.at[t], s_send.at[t], s_recv.at[t], to_sib)
+
+    def rows_of(i):
+        t = chip(i)
+        slot = lax.rem(i, 2)
+
+        @pl.when(i >= 2)
+        def _():
+            swap(i - 2).wait_send()
+
+        load_h(i, True).wait()
+        for lo, hi in spans:
+            sib_s[slot, :, lo:hi] = t_dot(hb[0], dpv[:, lo:hi]).astype(BF16)
+        sib_s[slot, :, cols - spare :] = tiny_ref[...]
+        swap(i).start()
+
+        @pl.when(i < 3)
+        def _():
+            load_h(i + 1, True).start()
+
+        load_h(i, False).wait()
+        for lo, hi in spans:
+            mine_s[:, lo:hi] = t_dot(hb[1], dpv[:, lo:hi]).astype(BF16)
+        mine_s[:, cols - spare :] = tiny_ref[...]
+
+        @pl.when(i < 3)
+        def _():
+            load_h(i + 1, False).start()
+
+        swap(i).wait_recv()
+        join(t, mine_s)
+
+    def join(t, extra):
+        for lo, hi in spans:
+            own_s[t, :, lo:hi] = (own_s[t, :, lo:hi].astype(F32) + extra[:, lo:hi].astype(F32)).astype(BF16)
+
+    def up_copy(t):
+        return remote(own_s.at[t], z_u.at[t - 1], zu_send.at[t], zu_recv.at[t], to_up)
+
+    def down_copy(t):
+        return remote(own_s.at[t], z_d.at[t], zd_send.at[t], zd_recv.at[t], to_down)
+
+    def up_add(t):
+        up_copy(t).wait_recv()
+        join(t, z_u.at[t - 1])
+
+    def down_add(t):
+        down_copy(t).wait_recv()
+        join(t, z_d.at[t])
+
+    def pass_on(t, there, add, make):
+        pl.when(there)(functools.partial(add, t))
+        launch(there, lambda: make(t))
+
+    def follow(t, there, make, before):
+        @pl.when(there)
+        def _():
+            make(before).wait_send()
+            make(t).start()
+
+    def finish_later(t, there, make):
+        def finish():
+            @pl.when(there)
+            def _():
+                make(t).wait_send()
+
+        closing.append(finish)
+
+    load_dp.wait()
+    load_w.wait()
+    part(far, far_p)
+    d0 = push(far_p.at[:half], far_a, d_sems, 0, to_x)
+    d1 = push(far_p.at[half:], far_b, d_sems, 1, to_y)
+    own_piece.wait()
+    w0.wait_recv()
+    piece_a = pv.at[x_peer, 0]
+    w2 = push(piece_a, piece_a, w_sems, 2, to_y)
+    w1.wait_recv()
+    piece_b = pv.at[y_peer, 1]
+    w3 = push(piece_b, piece_b, w_sems, 3, to_x)
+    pl.loop(0, 2)(rows_of)
+    @pl.when(r == 0)
+    def _():
+        up_copy(last).start()
+
+    @pl.when(r == last)
+    def _():
+        down_copy(0).start()
+
+    part(y_peer, y_p)
+    d0.wait_recv()
+    add_to(y_p, slice(0, half), far_a[...])
+    d2 = push(y_p, y_f, d_sems, 2, to_y)
+    part(x_peer, x_p)
+    d1.wait_recv()
+    add_to(x_p, slice(half, q), far_b[...])
+    d3 = push(x_p, x_f, d_sems, 3, to_x)
+    pl.loop(2, 4)(rows_of)
+
+    follow(2, r == 0, up_copy, last)
+    follow(1, r == last, down_copy, 0)
+    pass_on(last, (r > 0) & above, up_add, up_copy)
+    pass_on(0, (r < last) & below, down_add, down_copy)
+    follow(1, r == 0, up_copy, 2)
+    follow(2, r == last, down_copy, 1)
+    pass_on(2, r == 1, up_add, up_copy)
+    pass_on(1, r == 2, down_add, down_copy)
+    finish_later(1, r == 0, up_copy)
+    finish_later(2, r == last, down_copy)
+    pl.when(r > 0)(lambda: up_add(r))
+    pl.when(r < last)(lambda: down_add(r))
+
+    red = own_s.at[r]
+    g0 = push(red, win_ref.at[s], g_sems, 0, to_x)
+    g1 = push(red, win_ref.at[s], g_sems, 1, to_y)
+    own_win = pltpu.make_async_copy(red, win_ref.at[s], load_sem.at[3])
+    own_win.start()
+    w2.wait_recv()
+    w3.wait_recv()
+    per = owners // 4
+
+    def piece_of(head):
+        return pv.at[head // per, lax.rem(head, per)]
+
+    pieces = []
+    for k, peer in enumerate(to_heads):
+        pieces.append(push(piece_of(peer["head"]), wout_ref.at[h], (p_send, p_recv), k, peer))
+    own_piece = pltpu.make_async_copy(piece_of(h), wout_ref.at[h], load_sem.at[2])
+    own_piece.start()
+
+    d2.wait_recv()
+    d3.wait_recv()
+
+    def dn_out(j):
+        to = pl.ds(pl.multiple_of(j * tile, tile), tile)
+        return pltpu.make_async_copy(dn_o.at[lax.rem(j, 2)], dn_ref.at[:, to], out_sem.at[lax.rem(j, 2)])
+
+    own_at = pl.ds(pl.multiple_of(s * q, 16), q)
+    tiles_n = wv.shape[0] // tile
+
+    @pl.loop(0, tiles_n)
+    def _(j):
+        to = pl.ds(pl.multiple_of(j * tile, tile), tile)
+        got = dot_t(dpv[own_at, :], wv[to, :])
+
+        @pl.when(j > 1)
+        def _():
+            dn_out(j - 2).wait()
+
+        dn_o[lax.rem(j, 2)] = got + y_f[:, to].astype(F32) + x_f[:, to].astype(F32)
+        dn_out(j).start()
+
+    g0.wait_recv()
+    part_a = win_ref.at[x_peer, : n // 2]
+    g2 = push(part_a, part_a, g_sems, 2, to_y)
+    g1.wait_recv()
+    part_b = win_ref.at[y_peer, n // 2 :]
+    g3 = push(part_b, part_b, g_sems, 3, to_x)
+    dn_out(tiles_n - 2).wait()
+    dn_out(tiles_n - 1).wait()
+    own_win.wait()
+    own_piece.wait()
+    for copy in pieces:
+        copy.wait_recv()
+    g2.wait_recv()
+    g3.wait_recv()
+    for i in (2, 3):
+        swap(i).wait_send()
+    for copy in sent:
+        copy.wait_send()
+    for finish in closing:
+        finish()
+
+
 def local(hidden, lengths, out_grad, norm_gain, w_in, w_dt, conv_weight, conv_bias, dt_bias, a_log, skip_gain, gate_gain, w_out):
     ranks = lax.axis_size("seq")
     rank = lax.axis_index("seq")
@@ -283,8 +845,87 @@
     steps = tokens // chunk
     shard = w_in.shape[0]
 
+    gain_rows = norm_gain.astype(F32)[:, None]
+
+    def scaled(v):
+        return (v.astype(F32) * gain_rows).astype(BF16)
+
+    spare = LANES // 2
     small = jnp.concatenate([conv_weight.reshape(-1), conv_bias, dt_bias, a_log, skip_gain, gate_gain])
-    small = lax.all_gather(small, "head")
+    n_small = small.shape[0]
+    small = jnp.pad(small, (0, shard * spare - n_small)).reshape(shard, spare)
+    last_block = jnp.concatenate(
+        [
+            scaled(lax.dynamic_slice_in_dim(w_dt, rank * heads, heads, 1)),
+            jnp.zeros((shard, LANES - spare - heads), BF16),
+            small,
+        ],
+        axis=1,
+    )
+    ring = owners == 2 * ranks
+    if ring:
+        w_given, o_given = w_in, w_out
+    else:
+        w_given = lax.all_gather(
+            jnp.concatenate(
+                [
+                    scaled(lax.dynamic_slice_in_dim(w_in, rank * wide, wide, 1)),
+                    scaled(lax.dynamic_slice_in_dim(w_in, DI + rank * wide, wide, 1)),
+                    scaled(w_in[:, 2 * DI :]),
+                    last_block,
+                ],
+                axis=1,
+            ),
+            "head", axis=0, tiled=True,
+        )
+        o_given = lax.dynamic_slice_in_dim(lax.all_gather(w_out, "head", axis=0, tiled=True), rank * wide, wide, 0)
+
+    def sds(shape, kind):
+        return jax.ShapeDtypeStruct(shape, kind)
+
+    hbm = pl.BlockSpec(memory_space=pl.ANY)
+    vmem = pl.BlockSpec(memory_space=pltpu.VMEM)
+
+    def dma(count):
+        return pltpu.SemaphoreType.DMA((count,))
+
+    h_all, og_all, w_t, w_o, z, u, d_raw, d0 = pl.pallas_call(
+        functools.partial(gather_kernel, ring=ring, wide=wide),
+        in_specs=[hbm, hbm, hbm, hbm, vmem, vmem],
+        out_specs=[hbm] * 8,
+        out_shape=[
+            sds((tokens, width), BF16),
+            sds((tokens, width), BF16),
+            sds((width, cols), BF16),
+            sds((wide, width), BF16),
+            sds((tokens, wide), BF16),
+            sds((tokens, chans), BF16),
+            sds((tokens, LANES), F32),
+            sds((tokens, wide), BF16),
+        ],
+        scratch_shapes=[
+            pltpu.VMEM((tokens, width), BF16),
+            pltpu.VMEM((tokens, width), BF16),
+            pltpu.VMEM((width, cols), BF16),
+            pltpu.VMEM((wide, width), BF16),
+            pltpu.VMEM((shard, cols - LANES), BF16),
+            pltpu.VMEM((tokens, wide), BF16),
+            pltpu.VMEM((tokens, chans), BF16),
+            pltpu.VMEM((tokens, LANES), F32),
+            pltpu.VMEM((tokens, wide), BF16),
+        ]
+        + [dma(4)] * 14
+        + [dma(6), dma(26)],
+        compiler_params=pltpu.CompilerParams(
+            collective_id=0, has_side_effects=True, vmem_limit_bytes=56 * 1024 * 1024
+        ),
+        cost_estimate=pl.CostEstimate(
+            flops=2 * tokens * width * (cols + wide), bytes_accessed=4 * tokens * (width + cols), transcendentals=0
+        ),
+        name="gather_project",
+    )(hidden[0], out_grad[0], w_given, o_given, gain_rows, last_block)
+
+    small = w_t.reshape(owners, shard, cols)[:, :, cols - spare :].reshape(owners, shard * spare)
     cs = CHANNELS // owners
     hs = HEADS // owners
     gs = DI // owners
@@ -323,26 +964,6 @@
     expand = (jnp.arange(LANES, dtype=jnp.int32)[:, None] == head_of[None]).astype(BF16)
     seg = expand.T
 
-    gain_rows = norm_gain.astype(F32)[:, None]
-
-    def scaled(v):
-        return (v.astype(F32) * gain_rows).astype(BF16)
-
-    sent = jnp.concatenate(
-        [
-            scaled(lax.dynamic_slice_in_dim(w_in, rank * wide, wide, 1)),
-            scaled(lax.dynamic_slice_in_dim(w_in, DI + rank * wide, wide, 1)),
-            scaled(w_in[:, 2 * DI :]),
-            scaled(lax.dynamic_slice_in_dim(w_dt, rank * heads, heads, 1)),
-            jnp.zeros((shard, LANES - heads), BF16),
-        ],
-        axis=1,
-    )
-    w_t = lax.all_gather(sent, "head", axis=0, tiled=True)
-    w_o = lax.dynamic_slice_in_dim(lax.all_gather(w_out, "head", axis=0, tiled=True), rank * wide, wide, 0)
-    h_all = lax.all_gather(hidden[0], "seq", axis=0, tiled=True)
-    og_all = lax.all_gather(out_grad[0], "seq", axis=0, tiled=True)
-
     def forth(size):
         return pl.BlockSpec((chunk, size), lambda j: (j, 0))
 
@@ -357,56 +978,36 @@
     )
     grid = (steps,)
 
-    def sds(shape, kind):
-        return jax.ShapeDtypeStruct(shape, kind)
-
-    z, u, act, slope, aux = pl.pallas_call(
-        functools.partial(project_kernel, heads=heads, wide=wide),
+    act, slope, aux, y, gg, states, sums = pl.pallas_call(
+        functools.partial(scan_kernel, heads=heads, wide=wide),
         grid=grid,
-        in_specs=[forth(width), whole(w_t), whole(cw), whole(cb), whole(dtb)],
-        out_specs=[forth(wide), forth(chans), forth(chans), forth(chans), forth(LANES)],
+        in_specs=[
+            forth(chans), forth(LANES), forth(wide), forth(wide),
+            whole(cw), whole(cb), whole(dtb), whole(expand), whole(rowp), whole(colp),
+        ],
+        out_specs=[
+            forth(chans), forth(chans), forth(LANES), forth(wide), forth(wide),
+            pl.BlockSpec((1, STATE, wide), lambda j: (j, 0, 0)),
+            pl.BlockSpec((8, chunk), lambda j: (0, j)),
+        ],
         out_shape=[
-            sds((tokens, wide), BF16),
-            sds((tokens, chans), BF16),
             sds((tokens, chans), BF16),
             sds((tokens, chans), BF16),
             sds((tokens, LANES), F32),
-        ],
-        scratch_shapes=[pltpu.VMEM((chunk + 8, chans), F32)],
-        compiler_params=params,
-        cost_estimate=pl.CostEstimate(
-            flops=2 * tokens * width * cols, bytes_accessed=2 * tokens * (width + 4 * chans), transcendentals=0
-        ),
-        name="project",
-    )(h_all, w_t, cw, cb, dtb)
-
-    d0 = dot_t(og_all, w_o).astype(BF16)
-
-    y, gg, states, stat = pl.pallas_call(
-        functools.partial(scan_kernel, heads=heads, wide=wide),
-        grid=grid,
-        in_specs=[forth(chans), forth(LANES), forth(wide), forth(wide), whole(expand), whole(rowp), whole(colp)],
-        out_specs=[
-            forth(wide),
-            forth(wide),
-            pl.BlockSpec((1, STATE, wide), lambda j: (j, 0, 0)),
-            forth(LANES),
-        ],
-        out_shape=[
             sds((tokens, wide), F32),
             sds((tokens, wide), BF16),
             sds((steps, STATE, wide), F32),
-            sds((tokens, LANES), F32),
+            sds((8, tokens), F32),
         ],
-        scratch_shapes=[pltpu.VMEM((STATE, wide), F32)],
+        scratch_shapes=[pltpu.VMEM((STATE, wide), F32), pltpu.VMEM((chunk + 8, chans), F32)],
         compiler_params=params,
         cost_estimate=pl.CostEstimate(
-            flops=2 * tokens * wide * 6 * chunk, bytes_accessed=tokens * wide * 16, transcendentals=tokens * chunk * heads
+            flops=2 * tokens * wide * 12 * chunk, bytes_accessed=tokens * wide * 16, transcendentals=tokens * chunk * heads
         ),
         name="scan",
-    )(act, aux, z, d0, expand, rowp, colp)
-
-    sums = lax.psum(stat[:, :2].T.reshape(2, tokens // LANES, LANES), "seq").reshape(2, tokens)
+    )(u, d_raw, z, d0, cw, cb, dtb, expand, rowp, colp)
+
+    sums = lax.psum(sums[:2].reshape(2, tokens // LANES, LANES), "seq").reshape(2, tokens)
     mask = (jnp.arange(tokens, dtype=jnp.int32) < lengths[0]).astype(F32)
     r1 = lax.rsqrt(sums[0] / DI + EPS)
     r1m = r1 * mask
@@ -415,10 +1016,10 @@
     stat2 = jnp.where(lane == 0, r1m[:, None], jnp.where(lane == 1, coef[:, None], 0.0))
 
     partial = dot(gg, w_o).astype(BF16)
-    branch = lax.psum_scatter(partial, "seq", scatter_dimension=0, tiled=True)
-
     og_scaled = (og_all.astype(F32) * r1m[:, None]).astype(BF16)
     wog = t_dot(gg, og_scaled).astype(BF16)
+    stat2, wog, partial = lax.optimization_barrier((stat2, wog, partial))
+    branch = lax.psum_scatter(partial, "seq", scatter_dimension=0, tiled=True)
 
     dp, sm = pl.pallas_call(
         functools.partial(back_kernel, heads=heads, wide=wide),
@@ -439,23 +1040,65 @@
         name="scan_back",
     )(act, aux, z, d0, y, states, slope, u, stat2, expand, seg, rowp, colp, cw)
 
-    wig = t_dot(h_all, dp).astype(BF16)
-    dn_part = dot_t(dp, w_t).astype(BF16)
-    dn = lax.psum_scatter(dn_part, "seq", scatter_dimension=0, tiled=True).astype(F32)
-
+    skip_h = jnp.sum(sm[5, :wide].reshape(heads, HEAD_DIM), axis=1)
+    tiny = jnp.concatenate([sm[:5].reshape(-1), sm[6, :heads], sm[7, :heads], skip_h])
     n_own = DI // owners
-    if owners % ranks == 0 and n_own % owners == 0:
-        pieces = wog.reshape(owners // ranks, owners, n_own // owners, width)
-        pieces = lax.psum_scatter(pieces, "head", scatter_dimension=1, tiled=False)
-        pieces = lax.all_gather(pieces, "seq", axis=0, tiled=True)
-        w_out_grad = lax.all_to_all(pieces, "head", 0, 0, tiled=True).reshape(n_own, width).astype(F32)
+    if ring:
+        piece = n_own // owners
+        pieces = wog.reshape(owners // ranks, owners, piece, width).swapaxes(0, 1)
+        pieces = lax.psum_scatter(pieces, "head", scatter_dimension=0, tiled=False)
+        dp, pieces, branch = lax.optimization_barrier((dp, pieces, branch))
+        laid = jnp.pad(tiny, (0, shard * spare - tiny.shape[0])).reshape(shard, spare).astype(BF16)
+        dn, rows_in, w_out_grad = pl.pallas_call(
+            grads_kernel,
+            in_specs=[hbm, hbm, hbm, hbm, vmem],
+            out_specs=[hbm] * 3,
+            out_shape=[
+                sds((local_len, width), F32),
+                sds((ranks, shard, cols), BF16),
+                sds((owners, piece, width), BF16),
+            ],
+            scratch_shapes=[
+                pltpu.VMEM((tokens, cols), BF16),
+                pltpu.VMEM((width, cols), BF16),
+                pltpu.VMEM((2, tokens, shard), BF16),
+            ]
+            + [pltpu.VMEM((local_len, width), BF16)] * 3
+            + [pltpu.VMEM((local_len // 2, width), BF16)] * 2
+            + [pltpu.VMEM((local_len, width), BF16)] * 2
+            + [
+                pltpu.VMEM((2, local_len, 256), F32),
+                pltpu.VMEM((2, shard, cols), BF16),
+                pltpu.VMEM((shard, cols), BF16),
+                pltpu.VMEM((4, shard, cols), BF16),
+                pltpu.VMEM((3, shard, cols), BF16),
+                pltpu.VMEM((3, shard, cols), BF16),
+                pltpu.VMEM((ranks, owners // ranks, piece, width), BF16),
+            ]
+            + [dma(4), dma(2)]
+            + [dma(4)] * 10
+            + [dma(owners)] * 2
+            + [dma(4)] * 2
+            + [dma(2)],
+            compiler_params=pltpu.CompilerParams(
+                collective_id=1, has_side_effects=True, vmem_limit_bytes=56 * 1024 * 1024
+            ),
+            cost_estimate=pl.CostEstimate(
+                flops=4 * tokens * width * cols, bytes_accessed=8 * tokens * cols, transcendentals=0
+            ),
+            name="weight_grads",
+        )(dp, w_t, h_all, pieces, laid)
+        w_out_grad = w_out_grad.reshape(n_own, width).astype(F32)
+        tiny_all = rows_in[:, :, cols - spare :].reshape(ranks, shard * spare)[:, : tiny.shape[0]].astype(F32)
     else:
         full = lax.all_gather(lax.psum(wog, "head"), "seq", axis=0, tiled=True)
         w_out_grad = lax.dynamic_slice_in_dim(full, owner * n_own, n_own, 0).astype(F32)
+        wig = t_dot(h_all, dp).astype(BF16)
+        dn = lax.psum_scatter(dot_t(dp, w_t).astype(BF16), "seq", scatter_dimension=0, tiled=True).astype(F32)
+        rows_in = lax.all_gather(lax.psum_scatter(wig, "head", scatter_dimension=0, tiled=True), "seq")
+        tiny_all = lax.all_gather(lax.psum(tiny, "head"), "seq")
     gate_gain_grad = jnp.sum(w_out.astype(F32) * w_out_grad, axis=1) / gate_gain.astype(F32)
 
-    rows_in = lax.psum_scatter(wig, "head", scatter_dimension=0, tiled=True)
-    rows_in = lax.all_gather(rows_in, "seq")
     bc_cols = jnp.sum(rows_in[:, :, 2 * wide : wide + chans].astype(F32), axis=0)
     raw_in = jnp.concatenate(
         [rows_in[r, :, :wide].astype(F32) for r in range(ranks)]
@@ -477,18 +1120,12 @@
     mixed = jnp.sum(dn * h32, axis=1, keepdims=True) / width
     hidden_grad = (out_grad[0].astype(F32) + dn - h32 * (r0 * r0 * mixed))[None]
 
-    def laid(v, total, size):
-        base = jnp.zeros(v.shape[:-1] + (total,), F32)
-        return lax.dynamic_update_slice_in_dim(base, v, rank * size, v.ndim - 1)
-
-    conv_all = jnp.concatenate([laid(sm[:5, :wide], DI, wide), sm[:5, wide:]], axis=1)
-    skip_h = jnp.sum(sm[5, :wide].reshape(heads, HEAD_DIM), axis=1)
-    vec = jnp.stack([sm[6, :heads], sm[7, :heads], skip_h])
-    packed = jnp.concatenate([conv_all.reshape(-1), laid(vec, HEADS, heads).reshape(-1)])
-    packed = lax.psum(packed, EVERY)
-    n_conv = 5 * CHANNELS
-    conv_all = packed[:n_conv].reshape(5, CHANNELS)
-    vec = packed[n_conv:].reshape(3, HEADS)
+    n_conv = 5 * chans
+    conv_all = tiny_all[:, :n_conv].reshape(ranks, 5, chans)
+    conv_all = jnp.concatenate(
+        [conv_all[:, :, :wide].swapaxes(0, 1).reshape(5, DI), jnp.sum(conv_all[:, :, wide:], axis=0)], axis=1
+    )
+    vec = tiny_all[:, n_conv:].reshape(ranks, 3, heads).swapaxes(0, 1).reshape(3, HEADS)
     conv_own = lax.dynamic_slice_in_dim(conv_all, owner * cs, cs, 1)
     vec_own = lax.dynamic_slice_in_dim(vec, owner * hs, hs, 1)
 

time: 1210 us -> 671 us (0.55)
  waiting for transfers between devices: 793 us -> 86.5 us
  Pallas kernels: 137 us -> 457 us
  matrix products: 98.8 us -> 27.1 us
  local copies, waits for them, and re-layouts: 65.3 us -> 21.7 us
  blocking collectives: 41.8 us -> 15.5 us
    all_gather x6 -> x0, waiting for transfers between devices: 429 us -> none  [the longest x1 150 us: local(): lax.all_gather(w_out, 'head', axis=0, tiled=True)]
    pallas_call x1 -> x2, Pallas kernels: 48.1 us -> 354 us  [the longest x1 208 us: local(): pl.pallas_call(grads_kernel, in_specs=[hbm, hbm, hbm, hbm, vmem], out_spe...]
    reduce_scatter x2 -> x1, waiting for transfers between devices: 137 us -> 0.01 us  [local(): pieces = lax.psum_scatter(pieces, 'head', scatter_dimension=0, tiled=False)]
    psum x1 -> x0, waiting for transfers between devices: 136 us -> none  [local(): packed = lax.psum(packed, EVERY)]
    dot_general x2 -> x0, matrix products: 42.4 us -> none  [dot_t(): lax.dot_general(a, b, (((1,), (1,)), ((), ())), preferred_element_type=F32)]
    dot_general x2 -> x1, matrix products: 42.3 us -> 13.1 us  [t_dot(): lax.dot_general(a, b, (((0,), (0,)), ((), ())), preferred_element_type=F32)]
    unnamed x1 -> x0, blocking collectives: 25.6 us -> none
    unnamed x52 -> x26, local copies, waits for them, and re-layouts: 26.1 us -> 1.8 us
  transfers between devices with their start and end apart: 12 -> 2, of which waited for: 11 -> 1; matrix products, arithmetic and copies ran while one was open for 9% -> 1% of each run, Pallas kernels for 9% -> 10%
where the time goes in v2:
time: 671 us; the launch traced here: 664 us
  Pallas kernels  457 us (68%)
  waiting for transfers between devices  86.5 us (13%)
  other arithmetic  40.3 us (6%)
  matrix products  27.1 us (4%)
  local copies, waits for them, and re-layouts  21.7 us (3%)
  blocking collectives  15.5 us (2%)
  between operations  15.5 us (2%)
    pallas_call x1, Pallas kernels, local(): pl.pallas_call(grads_kernel, in_specs=[hbm, hbm, hbm, hbm, vmem], out_spe...  208 us
    pallas_call x1, Pallas kernels, local(): pl.pallas_call(functools.partial(gather_kernel, ring=ring, wide=wide), in...  146 us
    reduce_scatter x1, waiting for transfers between devices, local(): branch = lax.psum_scatter(partial, 'seq', scatter_dimension=0, tiled=True)  85.9 us
    pallas_call x1, Pallas kernels, local(): pl.pallas_call(functools.partial(back_kernel, heads=heads, wide=wide), gr...  64.1 us
    pallas_call x1, Pallas kernels, local(): pl.pallas_call(functools.partial(scan_kernel, heads=heads, wide=wide), gr...  38.9 us
    psum x1, blocking collectives, local(): lax.psum(sums[:2].reshape(2, tokens // LANES, LANES), 'seq')  15.5 us
    dot_general x1, matrix products, dot(): return jnp.dot(a, b, preferred_element_type=F32)  14 us
  transfers between devices with their start and end apart: 2, of which 1 were waited for; matrix products, arithmetic and copies ran while one was open for 1% of the time, Pallas kernels for 10%

profile of v2, /device:TPU:8, one launch (start us, length us, event | category | flops | bytes accessed | tf_op | source)
XLA Modules:
  0.0 663.6 jit_solution(3813228789642135615)
XLA Ops:
  7.2 0.7 convert_element_type.159
  7.9 0.8 copy.46.gain_ref
  8.7 0.8 reshape.205
  9.5 3.5 concatenate.37
  13.0 0.7 multiply_convert_fusion.4
  14.0 0.7 pad_maximum_fusion.dtw_ref
  14.7 145.7 %gather_project.1 = (bf16[2048,2048]{1,0:T(8,128)(2,1)}, bf16[2048,2048]{1,0:T(8,128)(2,1)}, bf16[2048,2432]{1,0:T(8,128)(2,1)}, bf16[1024,2048]{1,0:T(8,128)(2,...) custom-call(bf16[512,2048]{1,0:T(8,128)(2,1)} %bitcast.99, ...), custom_call_target="tpu_custom_call" | custom-call | flops 28991029248 | bytes 36700160 | tf_op jit(solution)/shard_map/gather_project/pallas_call | solution.py:892
  160.3 1.2 slice.173
  163.0 0.8 fusion.9.exp_ref
  164.3 0.6 fusion.15.cw_ref
  164.9 0.6 stack.19.rowp_ref
  165.6 0.6 broadcast_in_dim.84.cb_ref
  166.2 0.6 broadcast_in_dim.85.dtb_ref
  166.8 0.7 broadcast_in_dim.88.colp_ref
  167.5 38.9 %scan.1 = (bf16[2048,1280]{1,0:T(8,128)(2,1)}, bf16[2048,1280]{1,0:T(8,128)(2,1)}, f32[2048,128]{1,0:T(8,128)}, f32[2048,1024]{1,0:T(8,128)}, bf16[2048,1024]{1,...) custom-call(bf16[2048,1280]{1,0:T(8,128)(2,1)} %get-tuple-element.38.u_ref, ...), custom_call_target="tpu_custom_call" | custom-call | flops 12884901888 | bytes 33554432 | tf_op jit(solution)/shard_map/scan/pallas_call | solution.py:981
  206.4 0.8 slice_bitcast_fusion.4
  207.2 15.5 %psum.7 = f32[2,16,128]{2,1,0:T(8,128)S(1)} all-reduce(f32[2,16,128]{2,1,0:T(8,128)S(1)} %bitcast.107), channel_id=1, replica_groups=mesh['seq'=4,'head'=8] {'seq'}, use_global_device_ids=true, to_apply=%region_0.1 | all-reduce | flops 4096 | bytes 32768 | tf_op jit(solution)/shard_map/psum | solution.py:1010
  223.4 14.0 %convolution_convert_fusion = bf16[2048,2048]{1,0:T(8,128)(2,1)} fusion(bf16[2048,1024]{1,0:T(8,128)(2,1)} %get-tuple-element.49, bf16[1024,2048]{1,0:T(8,128)(2,1)} %get-tuple-element.51), kind=kOutput, calls=%fused_computation.4 | convolution fusion | flops 8594128896 | bytes 16777216 | tf_op jit(solution)/shard_map/dot_general | solution.py:26
  237.4 13.1 %fusion.7 = bf16[1024,2048]{1,0:T(8,128)(2,1)S(1)} fusion(bf16[2048,1024]{1,0:T(8,128)(2,1)} %get-tuple-element.49, bf16[2048,2048]{1,0:T(8,128)(2,1)} %get-tuple-element.50, f32[2048]{0:T(1024)S(1)} %get-tuple-element.119), kind=kOutput, calls=%fused_computation.17 | convolution fusion | flops 8604614656 | bytes 16785408 | tf_op jit(solution)/shard_map/dot_general | solution.py:34
  250.5 1.6 select_select_fusion.stat_ref
  252.1 2.3 copy.58
  255.3 0.9 fusion.10.seg_ref
  256.3 64.1 %scan_back.1 = (bf16[2048,2432]{1,0:T(8,128)(2,1)}, f32[8,1280]{1,0:T(8,128)}) custom-call(bf16[2048,1280]{1,0:T(8,128)(2,1)} %get-tuple-element.44.act_ref, f32[2048,128]{1,0:T(8,128)} %get-tuple-element.45.aux_ref, bf16[2048,1024]{1,0:T(8,128)(2,1)} %get-tuple-element.40.z_ref, bf16[2048,1024]{1,0:T(8,128)(2,1)} %get-tuple-element.41.d0_ref, ...), custom_call_target="tpu_custom_call" | custom-call | flops 12884901888 | bytes 50331648 | tf_op jit(solution)/shard_map/scan_back/pallas_call | solution.py:1024
  320.3 0.8 convert.35
  321.2 0.8 slice_reduce_fusion.1
  322.2 0.7 convert_element_type.174.tiny_ref
  323.0 85.9 %reduce-scatter.5.cloned.1.call-done = bf16[512,2048]{1,0:T(8,128)(2,1)} async-done(((bf16[2048,2048]{1,0:T(8,128)(2,1)}), bf16[512,2048]{1,0:T(8,128)(2,1)}) %reduce-scatter.5.cloned.1.call-update) | async-done | bytes 2097168 | tf_op jit(solution)/shard_map/reduce_scatter | solution.py:1022
  409.0 208.2 %weight_grads.1 = (f32[512,2048]{1,0:T(8,128)}, bf16[4,256,2432]{2,1,0:T(8,128)(2,1)}, bf16[8,64,2048]{2,1,0:T(8,128)(2,1)}) custom-call(bf16[2048,2432]{1,0:T(8,128)(2,1)} %get-tuple-element.57.dp_ref, bf16[2048,2432]{1,0:T(8,128)(2,1)} %get-tuple-element.42.w_ref, bf16[2048,2048]{1,0:T(8,128)(2,1)} %get-tuple-element.58.h_ref, ...), custom_call_target="tpu_custom_call" | custom-call | flops 40802189312 | bytes 39845888 | tf_op jit(solution)/shard_map/weight_grads/pallas_call | solution.py:1052
  617.2 2.3 convert_dynamic-update-slice_fusion.7
  619.5 1.1 convert_reduce_fusion
  620.6 1.0 slice_bitcast_fusion.3
  621.6 1.1 slice.162
  623.1 0.6 slice.193
  623.7 0.6 slice_reduce_fusion.2
  624.3 3.2 fusion.3
  627.5 1.1 convert_dynamic-update-slice_fusion.6
  628.6 1.1 convert_dynamic-update-slice_fusion.5
  629.7 1.1 convert_dynamic-update-slice_fusion.4
  630.8 1.1 convert_dynamic-update-slice_fusion.3
  631.9 1.1 convert_dynamic-update-slice_fusion.2
  633.0 1.1 convert_dynamic-update-slice_fusion.1
  634.1 1.1 convert_dynamic-update-slice_fusion
  635.2 0.7 constant_dynamic-update-slice_fusion
  635.9 8.3 %broadcast_multiply_fusion = (f32[256,8448]{1,0:T(8,128)}, f32[256]{0:T(256)S(1)}) fusion(f32[256,8448]{1,0:T(8,128)} %constant_dynamic-update-slice_fusion, f32[256]{0:T(256)S(1)} %convert_element_type.159, bf16[256,8448]{1,0:T(8,128)(2,1)S(1)} %bitcast.101), kind=kLoop, calls=%fused_computation.9 | loop fusion | flops 8650496 | bytes 21628928 | tf_op jit(solution)/shard_map/mul | solution.py:1112
  644.4 0.7 copy.51
  645.9 5.1 multiply_reduce_fusion.1
  651.0 0.6 convert_divide_fusion
  652.3 4.0 fusion.6
  (93 shorter events, 5.5 us)
Async XLA Ops:
  7.2 315.9 %reduce-scatter.3.cloned.1.call-start = ((), (), s32[]{:S(2)}) async-start(), calls=%async_computation.2 | async-start | bytes 4718592 | tf_op jit(solution)/shard_map/reduce_scatter | solution.py:1049
  254.4 0.8 copy-start.6
  254.5 154.5 %reduce-scatter.5.cloned.1.call-start = ((), (), s32[]{:S(2)}) async-start(), calls=%async_computation.3 | async-start | bytes 10485760 | tf_op jit(solution)/shard_map/reduce_scatter | solution.py:1022
  617.2 7.2 %copy-start.1 = (bf16[1,512,2048]{2,1,0:T(8,128)(2,1)S(1)}, bf16[1,512,2048]{2,1,0:T(8,128)(2,1)}, u32[]{:S(2)}) copy-start(bf16[1,512,2048]{2,1,0:T(8,128)(2,1)} %param.13) | copy-start | bytes 6291460
  622.9 6.8 %copy-start.5 = (f32[4,6448]{1,0:T(4,128)}, f32[4,6448]{1,0:T(4,128)S(1)}, u32[]{:S(2)}) copy-start(f32[4,6448]{1,0:T(4,128)S(1)} %slice_convert_fusion) | copy-start | bytes 309508
  623.0 4.5 copy-start.2
  624.3 11.6 %slice-start = ((s8[4325376]{0:T(1024)(128)(4,1)}), s8[4194304]{0:T(1024)(128)(4,1)S(1)}, s32[]{:S(2)}) async-start(s8[4325376]{0:T(1024)(128)(4,1)} %bitcast.100), calls=%async_computation.4 | async-start | bytes 8388608
  628.6 7.3 %slice-start.1 = ((s8[4325376]{0:T(1024)(128)(4,1)}), s8[131072]{0:T(1024)(128)(4,1)S(1)}, s32[]{:S(2)}) async-start(s8[4325376]{0:T(1024)(128)(4,1)} %bitcast.100), calls=%async_computation.5 | async-start | bytes 262144
  635.9 9.2 %slice-start.2 = ((f32[4,6448]{1,0:T(4,128)}), f32[4,48]{1,0:T(4,128)S(1)}, s32[]{:S(2)}) async-start(f32[4,6448]{1,0:T(4,128)} %copy-done.5), calls=%async_computation.6 | async-start | bytes 4096 | tf_op jit(solution)/shard_map/slice | solution.py:1128
  644.3 6.7 %copy-start.7 = (bf16[512]{0:T(512)(128)(2,1)S(1)}, bf16[512]{0:T(512)(128)(2,1)}, u32[]{:S(2)}) copy-start(bf16[512]{0:T(512)(128)(2,1)} %param.24) | copy-start | bytes 3076
  645.3 7.0 %copy-start = (f32[512,2048]{1,0:T(8,128)S(1)}, f32[512,2048]{1,0:T(8,128)}, u32[]{:S(2)}) copy-start(f32[512,2048]{1,0:T(8,128)} %get-tuple-element.61) | copy-start | bytes 12582916
  645.3 7.0 %copy-start.3 = (bf16[1,512,2048]{2,1,0:T(8,128)(2,1)S(1)}, bf16[1,512,2048]{2,1,0:T(8,128)(2,1)}, u32[]{:S(2)}) copy-start(bf16[1,512,2048]{2,1,0:T(8,128)(2,1)} %param.15) | copy-start | bytes 6291460
  645.3 7.0 %copy-start.4 = (bf16[512,2048]{1,0:T(8,128)(2,1)S(1)}, bf16[512,2048]{1,0:T(8,128)(2,1)}, u32[]{:S(2)}) copy-start(bf16[512,2048]{1,0:T(8,128)(2,1)} %reduce-scatter.5.cloned.1.call-done) | copy-start | bytes 6291460
Sparse Core Ops, SparseCore 0:
  254.6 62.8 reduce-scatter.2
  320.5 88.3 reduce-scatter.4

commit v3 on v2

--- a/solution.py
+++ b/solution.py
@@ -442,14 +442,72 @@
     return dot(hi, seg) + dot(mid, seg) + dot(low, seg)
 
 
+def gate_kernel(x_ref, aux_ref, z_ref, d0_ref, y_ref, stat_ref, rowp_ref, dy_ref, dpg_ref):
+    stat = stat_ref[...]
+    r1m = stat[:, 0:1]
+    coef = stat[:, 1:2]
+    r0 = aux_ref[:, LANES - 1 : LANES]
+    ssd = (y_ref[...] + rowp_ref[1:2, :] * x_ref[...].astype(F32)).astype(BF16).astype(F32)
+    z = z_ref[...].astype(F32)
+    sig = sigmoid(z)
+    sz = z * sig
+    d_gated = (r1m * rowp_ref[2:3, :]) * d0_ref[...].astype(F32) - (ssd * sz) * coef
+    dy_ref[...] = (d_gated * sz).astype(BF16)
+    dpg_ref[...] = (r0 * (d_gated * ssd * (sig * (1.0 + z * (1.0 - sig))))).astype(BF16)
+
+
 def back_kernel(
-    act_ref, aux_ref, z_ref, d0_ref, y_ref, st_ref, slope_ref, u_ref, stat_ref,
+    act_ref, aux_ref, dy_ref, y_ref, st_ref, slope_ref, u_ref, part_ref,
     exp_ref, seg_ref, rowp_ref, colp_ref, cw_ref,
-    dp_ref, sm_ref, adj, ext, *, heads, wide,
+    dp_ref, sm_ref, br_ref, adj, ext, y_b, x_b, own_b, far_a, far_b, y_f, x_f, br_o,
+    b_send, b_recv, b_load, *, heads, wide,
 ):
     step = pl.program_id(0)
+    steps = pl.num_programs(0)
     rows = act_ref.shape[0]
     chans = u_ref.shape[1]
+
+    s = lax.axis_index("seq")
+    q = y_b.shape[0]
+    half = q // 2
+    x_peer = s + 1 - 2 * lax.rem(s, 2)
+    y_peer = lax.rem(s + 2, 4)
+    to_x, to_y = {"seq": x_peer}, {"seq": y_peer}
+
+    def at_rows(block, start, size):
+        return part_ref.at[pl.ds(pl.multiple_of(block * q + start, 16), size), :]
+
+    def b_copy(src, dst, i, target):
+        return remote(src, dst, b_send.at[i], b_recv.at[i], target)
+
+    out_a = b_copy(at_rows(3 - s, 0, half), far_a, 0, to_x)
+    out_b = b_copy(at_rows(3 - s, half, half), far_b, 1, to_y)
+    out_y = b_copy(y_b, y_f, 2, to_y)
+    out_x = b_copy(x_b, x_f, 3, to_x)
+    b_loads = [
+        pltpu.make_async_copy(at_rows(y_peer, 0, q), y_b, b_load.at[0]),
+        pltpu.make_async_copy(at_rows(x_peer, 0, q), x_b, b_load.at[1]),
+        pltpu.make_async_copy(at_rows(s, 0, q), own_b, b_load.at[2]),
+    ]
+
+    @pl.when(step == 0)
+    def _():
+        greet([to_x, to_y])
+        out_a.start()
+        out_b.start()
+        for copy in b_loads:
+            copy.start()
+
+    @pl.when(step == 3)
+    def _():
+        for copy in b_loads:
+            copy.wait()
+        out_a.wait_recv()
+        y_b[:half, :] = (y_b[:half, :].astype(F32) + far_a[...].astype(F32)).astype(BF16)
+        out_y.start()
+        out_b.wait_recv()
+        x_b[half:, :] = (x_b[half:, :].astype(F32) + far_b[...].astype(F32)).astype(BF16)
+        out_x.start()
 
     @pl.when(step == 0)
     def _():
@@ -466,22 +524,11 @@
     b = act_ref[:, wide : wide + STATE]
     c = act_ref[:, wide + STATE :]
     aux = aux_ref[...]
-    stat = stat_ref[...]
-    r1m = stat[:, 0:1]
-    coef = stat[:, 1:2]
     r0 = aux[:, LANES - 1 : LANES]
     skip_e = rowp_ref[1:2, :]
-    gain = rowp_ref[2:3, :]
-
     y = y_ref[...]
-    ssd = (y + skip_e * x32).astype(BF16).astype(F32)
-    z = z_ref[...].astype(F32)
-    sig = sigmoid(z)
-    sz = z * sig
-    d_gated = (r1m * gain) * d0_ref[...].astype(F32) - (ssd * sz) * coef
-    dy16 = (d_gated * sz).astype(BF16)
+    dy16 = dy_ref[...]
     dy = dy16.astype(F32)
-    dp_ref[:, :wide] = (r0 * (d_gated * ssd * (sig * (1.0 + z * (1.0 - sig))))).astype(BF16)
 
     causal, dt_e, cum_e, cum_c, cum_t = decays(
         aux, heads, exp_ref[...], rowp_ref[0:1, :], rowp_ref[3:4, :LANES], colp_ref[:, 0:1]
@@ -546,7 +593,7 @@
     sig_v = pltpu.roll(aux, LANES - heads, 1)
     d_pre = jnp.where(lane < heads, d_dt * sig_v, 0.0)
     dt = jnp.where(lane < heads, aux, 0.0)
-    dp_ref[:, wide + chans :] = (r0 * d_pre).astype(BF16)
+    dp_ref[:, chans:] = (r0 * d_pre).astype(BF16)
 
     d_act = jnp.concatenate([skip_e * dy + dt_e * v, d_b, d_c], axis=1)
     d_conv = d_act * slope_ref[...].astype(F32)
@@ -558,19 +605,30 @@
         term = cw_ref[k : k + 1, :] * moved
         d_u = term if d_u is None else d_u + term
         sm_ref[k : k + 1, :] += jnp.sum(u * moved, axis=0, keepdims=True)
-    dp_ref[:, wide : wide + chans] = (r0 * d_u).astype(BF16)
+    dp_ref[:, :chans] = (r0 * d_u).astype(BF16)
     sm_ref[4:5, :] += jnp.sum(d_conv, axis=0, keepdims=True)
     sm_ref[5:6, :wide] += jnp.sum(x32 * dy, axis=0, keepdims=True)
     sm_ref[6:7, :LANES] += jnp.sum(d_pre, axis=0, keepdims=True)
     sm_ref[7:8, :LANES] += jnp.sum(dt * decay_grad, axis=0, keepdims=True)
 
+    @pl.when(step == steps - 1)
+    def _():
+        out_y.wait_recv()
+        out_x.wait_recv()
+        br_o[...] = own_b[...].astype(F32) + y_f[...].astype(F32) + x_f[...].astype(F32)
+        last_copy = pltpu.make_async_copy(br_o, br_ref, b_load.at[3])
+        last_copy.start()
+        for copy in (out_a, out_b, out_y, out_x):
+            copy.wait_send()
+        last_copy.wait()
+
 
 def grads_kernel(
-    dp_ref, w_ref, h_ref, piece_ref, tiny_ref,
-    dn_ref, win_ref, wout_ref,
+    dpg_ref, dp_ref, w_ref, h_ref, gate_ref, piece_ref, tiny_ref,
+    dn_ref, wing_ref, win_ref, wout_ref,
     dpv, wv, hb, far_p, y_p, x_p, far_a, far_b, y_f, x_f, dn_o, sib_s, mine_s, own_s, z_u, z_d, pv,
     load_sem, hb_sem, d_send, d_recv, s_send, s_recv, zu_send, zu_recv, zd_send, zd_recv,
-    g_send, g_recv, p_send, p_recv, w_send, w_recv, out_sem,
+    g_send, g_recv, k_send, k_recv, p_send, p_recv, w_send, w_recv, out_sem,
 ):
     s = lax.axis_index("seq")
     h = lax.axis_index("head")
@@ -613,10 +671,15 @@
 
         closing.append(finish)
 
-    load_dp = pltpu.make_async_copy(dp_ref, dpv, load_sem.at[0])
+    skip = dpv.shape[1] - cols
+    load_dp = pltpu.make_async_copy(dp_ref, dpv.at[:, skip:], load_sem.at[0])
     load_w = pltpu.make_async_copy(w_ref, wv, load_sem.at[1])
+    load_g = pltpu.make_async_copy(dpg_ref, dpv.at[:, :skip], load_sem.at[4])
+    own_gate = pltpu.make_async_copy(gate_ref, wing_ref.at[s], load_sem.at[5])
     load_dp.start()
+    load_g.start()
     load_w.start()
+    own_gate.start()
 
     def chip(i):
         return jnp.where(lax.rem(i, 2) == 0, last - i // 2, i // 2)
@@ -636,6 +699,9 @@
     d_sems = (d_send, d_recv)
     g_sems = (g_send, g_recv)
 
+    k_sems = (k_send, k_recv)
+    k0 = push(gate_ref, wing_ref.at[s], k_sems, 0, to_x)
+    k1 = push(gate_ref, wing_ref.at[s], k_sems, 1, to_y)
     w_sems = (w_send, w_recv)
     own_piece = pltpu.make_async_copy(piece_ref, pv.at[s], load_sem.at[2])
     own_piece.start()
@@ -668,7 +734,7 @@
 
         load_h(i, True).wait()
         for lo, hi in spans:
-            sib_s[slot, :, lo:hi] = t_dot(hb[0], dpv[:, lo:hi]).astype(BF16)
+            sib_s[slot, :, lo:hi] = t_dot(hb[0], dpv[:, skip + lo : skip + hi]).astype(BF16)
         sib_s[slot, :, cols - spare :] = tiny_ref[...]
         swap(i).start()
 
@@ -678,7 +744,7 @@
 
         load_h(i, False).wait()
         for lo, hi in spans:
-            mine_s[:, lo:hi] = t_dot(hb[1], dpv[:, lo:hi]).astype(BF16)
+            mine_s[:, lo:hi] = t_dot(hb[1], dpv[:, skip + lo : skip + hi]).astype(BF16)
         mine_s[:, cols - spare :] = tiny_ref[...]
 
         @pl.when(i < 3)
@@ -725,10 +791,27 @@
         closing.append(finish)
 
     load_dp.wait()
+    pl.loop(0, 2)(rows_of)
+
+    @pl.when(r == 0)
+    def _():
+        up_copy(last).start()
+
+    @pl.when(r == last)
+    def _():
+        down_copy(0).start()
+
+    load_g.wait()
     load_w.wait()
     part(far, far_p)
     d0 = push(far_p.at[:half], far_a, d_sems, 0, to_x)
     d1 = push(far_p.at[half:], far_b, d_sems, 1, to_y)
+    k0.wait_recv()
+    gate_a = wing_ref.at[x_peer, : n // 2]
+    k2 = push(gate_a, gate_a, k_sems, 2, to_y)
+    k1.wait_recv()
+    gate_b = wing_ref.at[y_peer, n // 2 :]
+    k3 = push(gate_b, gate_b, k_sems, 3, to_x)
     own_piece.wait()
     w0.wait_recv()
     piece_a = pv.at[x_peer, 0]
@@ -736,35 +819,26 @@
     w1.wait_recv()
     piece_b = pv.at[y_peer, 1]
     w3 = push(piece_b, piece_b, w_sems, 3, to_x)
-    pl.loop(0, 2)(rows_of)
-    @pl.when(r == 0)
-    def _():
-        up_copy(last).start()
-
-    @pl.when(r == last)
-    def _():
-        down_copy(0).start()
-
-    part(y_peer, y_p)
-    d0.wait_recv()
-    add_to(y_p, slice(0, half), far_a[...])
-    d2 = push(y_p, y_f, d_sems, 2, to_y)
-    part(x_peer, x_p)
-    d1.wait_recv()
-    add_to(x_p, slice(half, q), far_b[...])
-    d3 = push(x_p, x_f, d_sems, 3, to_x)
     pl.loop(2, 4)(rows_of)
 
     follow(2, r == 0, up_copy, last)
     follow(1, r == last, down_copy, 0)
     pass_on(last, (r > 0) & above, up_add, up_copy)
     pass_on(0, (r < last) & below, down_add, down_copy)
+    part(y_peer, y_p)
+    part(x_peer, x_p)
     follow(1, r == 0, up_copy, 2)
     follow(2, r == last, down_copy, 1)
     pass_on(2, r == 1, up_add, up_copy)
     pass_on(1, r == 2, down_add, down_copy)
     finish_later(1, r == 0, up_copy)
     finish_later(2, r == last, down_copy)
+    d0.wait_recv()
+    add_to(y_p, slice(0, half), far_a[...])
+    d2 = push(y_p, y_f, d_sems, 2, to_y)
+    d1.wait_recv()
+    add_to(x_p, slice(half, q), far_b[...])
+    d3 = push(x_p, x_f, d_sems, 3, to_x)
     pl.when(r > 0)(lambda: up_add(r))
     pl.when(r < last)(lambda: down_add(r))
 
@@ -786,38 +860,42 @@
     own_piece = pltpu.make_async_copy(piece_of(h), wout_ref.at[h], load_sem.at[2])
     own_piece.start()
 
-    d2.wait_recv()
-    d3.wait_recv()
-
-    def dn_out(j):
-        to = pl.ds(pl.multiple_of(j * tile, tile), tile)
-        return pltpu.make_async_copy(dn_o.at[lax.rem(j, 2)], dn_ref.at[:, to], out_sem.at[lax.rem(j, 2)])
-
-    own_at = pl.ds(pl.multiple_of(s * q, 16), q)
-    tiles_n = wv.shape[0] // tile
-
-    @pl.loop(0, tiles_n)
-    def _(j):
-        to = pl.ds(pl.multiple_of(j * tile, tile), tile)
-        got = dot_t(dpv[own_at, :], wv[to, :])
-
-        @pl.when(j > 1)
-        def _():
-            dn_out(j - 2).wait()
-
-        dn_o[lax.rem(j, 2)] = got + y_f[:, to].astype(F32) + x_f[:, to].astype(F32)
-        dn_out(j).start()
-
     g0.wait_recv()
     part_a = win_ref.at[x_peer, : n // 2]
     g2 = push(part_a, part_a, g_sems, 2, to_y)
     g1.wait_recv()
     part_b = win_ref.at[y_peer, n // 2 :]
     g3 = push(part_b, part_b, g_sems, 3, to_x)
+
+    d2.wait_recv()
+    d3.wait_recv()
+
+    def dn_out(j):
+        to = pl.ds(pl.multiple_of(j * tile, tile), tile)
+        return pltpu.make_async_copy(dn_o.at[lax.rem(j, 2)], dn_ref.at[:, to], out_sem.at[lax.rem(j, 2)])
+
+    own_at = pl.ds(pl.multiple_of(s * q, 16), q)
+    tiles_n = wv.shape[0] // tile
+
+    @pl.loop(0, tiles_n)
+    def _(j):
+        to = pl.ds(pl.multiple_of(j * tile, tile), tile)
+        got = dot_t(dpv[own_at, :], wv[to, :])
+
+        @pl.when(j > 1)
+        def _():
+            dn_out(j - 2).wait()
+
+        dn_o[lax.rem(j, 2)] = got + y_f[:, to].astype(F32) + x_f[:, to].astype(F32)
+        dn_out(j).start()
+
     dn_out(tiles_n - 2).wait()
     dn_out(tiles_n - 1).wait()
     own_win.wait()
+    own_gate.wait()
     own_piece.wait()
+    k2.wait_recv()
+    k3.wait_recv()
     for copy in pieces:
         copy.wait_recv()
     g2.wait_recv()
@@ -828,6 +906,30 @@
         copy.wait_send()
     for finish in closing:
         finish()
+
+
+def finish_kernel(gate_ref, rest_ref, w_ref, dtw_ref, gain_ref, win_ref, wdt_ref, norm_ref, *, heads, wide):
+    ranks = gate_ref.shape[0]
+    gain = gain_ref[...]
+    norm = None
+
+    def piece(at, raw):
+        to = slice(at, at + raw.shape[1])
+        win_ref[:, to] = raw * gain
+        return jnp.sum(raw * w_ref[:, to].astype(F32), axis=1, keepdims=True)
+
+    shared = None
+    dt_parts = []
+    for k in range(ranks):
+        here = piece(k * wide, gate_ref[k].astype(F32)) + piece(DI + k * wide, rest_ref[k, :, :wide].astype(F32))
+        norm = here if norm is None else norm + here
+        bc = rest_ref[k, :, wide : wide + 2 * STATE].astype(F32)
+        shared = bc if shared is None else shared + bc
+        dt_parts.append(rest_ref[k, :, wide + 2 * STATE : wide + 2 * STATE + heads].astype(F32))
+    norm = norm + piece(2 * DI, shared)
+    raw = jnp.concatenate(dt_parts, axis=1)
+    wdt_ref[...] = raw * gain
+    norm_ref[...] = norm + jnp.sum(raw * dtw_ref[...].astype(F32), axis=1, keepdims=True)
 
 
 def local(hidden, lengths, out_grad, norm_gain, w_in, w_dt, conv_weight, conv_bias, dt_bias, a_log, skip_gain, gate_gain, w_out):
@@ -1016,29 +1118,52 @@
     stat2 = jnp.where(lane == 0, r1m[:, None], jnp.where(lane == 1, coef[:, None], 0.0))
 
     partial = dot(gg, w_o).astype(BF16)
+    dy, dpg = pl.pallas_call(
+        gate_kernel,
+        grid=grid,
+        in_specs=[forth(wide), forth(LANES), forth(wide), forth(wide), forth(wide), forth(LANES), whole(rowp)],
+        out_specs=[forth(wide), forth(wide)],
+        out_shape=[sds((tokens, wide), BF16), sds((tokens, wide), BF16)],
+        compiler_params=params,
+        cost_estimate=pl.CostEstimate(
+            flops=20 * tokens * wide, bytes_accessed=tokens * wide * 14, transcendentals=tokens * wide
+        ),
+        name="gate_back",
+    )(act, aux, z, d0, y, stat2, rowp)
+
     og_scaled = (og_all.astype(F32) * r1m[:, None]).astype(BF16)
     wog = t_dot(gg, og_scaled).astype(BF16)
-    stat2, wog, partial = lax.optimization_barrier((stat2, wog, partial))
-    branch = lax.psum_scatter(partial, "seq", scatter_dimension=0, tiled=True)
-
-    dp, sm = pl.pallas_call(
+    wig_gate = t_dot(h_all, dpg).astype(BF16)
+    dy, wog, wig_gate, partial = lax.optimization_barrier((dy, wog, wig_gate, partial))
+    own_gate = lax.psum_scatter(wig_gate, "head", scatter_dimension=0, tiled=True)
+
+    rest = chans + LANES
+    dp, sm, branch = pl.pallas_call(
         functools.partial(back_kernel, heads=heads, wide=wide),
         grid=grid,
         in_specs=[
-            back(chans), back(LANES), back(wide), back(wide), back(wide),
+            back(chans), back(LANES), back(wide), back(wide),
             pl.BlockSpec((1, STATE, wide), lambda j: (steps - 1 - j, 0, 0)),
-            back(chans), back(chans), back(LANES),
+            back(chans), back(chans), hbm,
             whole(expand), whole(seg), whole(rowp), whole(colp), whole(cw),
         ],
-        out_specs=[back(cols), pl.BlockSpec((8, chans), lambda j: (0, 0))],
-        out_shape=[sds((tokens, cols), BF16), sds((8, chans), F32)],
-        scratch_shapes=[pltpu.VMEM((STATE, wide), F32), pltpu.VMEM((chunk + 8, chans), F32)],
-        compiler_params=params,
+        out_specs=[back(rest), pl.BlockSpec((8, chans), lambda j: (0, 0)), hbm],
+        out_shape=[sds((tokens, rest), BF16), sds((8, chans), F32), sds((local_len, width), F32)],
+        scratch_shapes=[pltpu.VMEM((STATE, wide), F32), pltpu.VMEM((chunk + 8, chans), F32)]
+        + [pltpu.VMEM((local_len, width), BF16)] * 3
+        + [pltpu.VMEM((local_len // 2, width), BF16)] * 2
+        + [pltpu.VMEM((local_len, width), BF16)] * 2
+        + [pltpu.VMEM((local_len, width), F32)]
+        + [dma(4)] * 3,
+        compiler_params=pltpu.CompilerParams(
+            dimension_semantics=("arbitrary",), collective_id=2, has_side_effects=True,
+            vmem_limit_bytes=56 * 1024 * 1024,
+        ),
         cost_estimate=pl.CostEstimate(
             flops=2 * tokens * wide * 12 * chunk, bytes_accessed=tokens * wide * 24, transcendentals=tokens * chunk * heads
         ),
         name="scan_back",
-    )(act, aux, z, d0, y, states, slope, u, stat2, expand, seg, rowp, colp, cw)
+    )(act, aux, dy, y, states, slope, u, partial, expand, seg, rowp, colp, cw)
 
     skip_h = jnp.sum(sm[5, :wide].reshape(heads, HEAD_DIM), axis=1)
     tiny = jnp.concatenate([sm[:5].reshape(-1), sm[6, :heads], sm[7, :heads], skip_h])
@@ -1047,15 +1172,15 @@
         piece = n_own // owners
         pieces = wog.reshape(owners // ranks, owners, piece, width).swapaxes(0, 1)
         pieces = lax.psum_scatter(pieces, "head", scatter_dimension=0, tiled=False)
-        dp, pieces, branch = lax.optimization_barrier((dp, pieces, branch))
         laid = jnp.pad(tiny, (0, shard * spare - tiny.shape[0])).reshape(shard, spare).astype(BF16)
-        dn, rows_in, w_out_grad = pl.pallas_call(
+        dn, gate_rows, rest_rows, w_out_grad = pl.pallas_call(
             grads_kernel,
-            in_specs=[hbm, hbm, hbm, hbm, vmem],
-            out_specs=[hbm] * 3,
+            in_specs=[hbm] * 6 + [vmem],
+            out_specs=[hbm] * 4,
             out_shape=[
                 sds((local_len, width), F32),
-                sds((ranks, shard, cols), BF16),
+                sds((ranks, shard, wide), BF16),
+                sds((ranks, shard, rest), BF16),
                 sds((owners, piece, width), BF16),
             ],
             scratch_shapes=[
@@ -1068,15 +1193,15 @@
             + [pltpu.VMEM((local_len, width), BF16)] * 2
             + [
                 pltpu.VMEM((2, local_len, 256), F32),
-                pltpu.VMEM((2, shard, cols), BF16),
-                pltpu.VMEM((shard, cols), BF16),
-                pltpu.VMEM((4, shard, cols), BF16),
-                pltpu.VMEM((3, shard, cols), BF16),
-                pltpu.VMEM((3, shard, cols), BF16),
+                pltpu.VMEM((2, shard, rest), BF16),
+                pltpu.VMEM((shard, rest), BF16),
+                pltpu.VMEM((4, shard, rest), BF16),
+                pltpu.VMEM((3, shard, rest), BF16),
+                pltpu.VMEM((3, shard, rest), BF16),
                 pltpu.VMEM((ranks, owners // ranks, piece, width), BF16),
             ]
-            + [dma(4), dma(2)]
-            + [dma(4)] * 10
+            + [dma(6), dma(2)]
+            + [dma(4)] * 12
             + [dma(owners)] * 2
             + [dma(4)] * 2
             + [dma(2)],
@@ -1087,35 +1212,43 @@
                 flops=4 * tokens * width * cols, bytes_accessed=8 * tokens * cols, transcendentals=0
             ),
             name="weight_grads",
-        )(dp, w_t, h_all, pieces, laid)
+        )(dpg, dp, w_t, h_all, own_gate, pieces, laid)
         w_out_grad = w_out_grad.reshape(n_own, width).astype(F32)
-        tiny_all = rows_in[:, :, cols - spare :].reshape(ranks, shard * spare)[:, : tiny.shape[0]].astype(F32)
+        tiny_all = rest_rows[:, :, rest - spare :].reshape(ranks, shard * spare)[:, : tiny.shape[0]].astype(F32)
     else:
         full = lax.all_gather(lax.psum(wog, "head"), "seq", axis=0, tiled=True)
         w_out_grad = lax.dynamic_slice_in_dim(full, owner * n_own, n_own, 0).astype(F32)
         wig = t_dot(h_all, dp).astype(BF16)
-        dn = lax.psum_scatter(dot_t(dp, w_t).astype(BF16), "seq", scatter_dimension=0, tiled=True).astype(F32)
-        rows_in = lax.all_gather(lax.psum_scatter(wig, "head", scatter_dimension=0, tiled=True), "seq")
+        dn = (dot_t(dp, w_t[:, wide:]) + dot_t(dpg, w_t[:, :wide])).astype(BF16)
+        dn = lax.psum_scatter(dn, "seq", scatter_dimension=0, tiled=True).astype(F32)
+        gate_rows = lax.all_gather(own_gate, "seq")
+        rest_rows = lax.all_gather(lax.psum_scatter(wig, "head", scatter_dimension=0, tiled=True), "seq")
         tiny_all = lax.all_gather(lax.psum(tiny, "head"), "seq")
     gate_gain_grad = jnp.sum(w_out.astype(F32) * w_out_grad, axis=1) / gate_gain.astype(F32)
 
-    bc_cols = jnp.sum(rows_in[:, :, 2 * wide : wide + chans].astype(F32), axis=0)
-    raw_in = jnp.concatenate(
-        [rows_in[r, :, :wide].astype(F32) for r in range(ranks)]
-        + [rows_in[r, :, wide : 2 * wide].astype(F32) for r in range(ranks)]
-        + [bc_cols],
-        axis=1,
-    )
-    raw_dt = jnp.concatenate(
-        [rows_in[r, :, wide + chans : wide + chans + heads].astype(F32) for r in range(ranks)], axis=1
-    )
-    w_in_grad = raw_in * gain_rows
-    w_dt_grad = raw_dt * gain_rows
-    norm_gain_grad = jnp.sum(raw_in * w_in.astype(F32), axis=1) + jnp.sum(raw_dt * w_dt.astype(F32), axis=1)
+    strip = min(32, shard)
+
+    def rows_spec(size):
+        return pl.BlockSpec((strip, size), lambda j: (j, 0))
+
+    def ranks_spec(size):
+        return pl.BlockSpec((ranks, strip, size), lambda j: (0, j, 0))
+
+    w_in_grad, w_dt_grad, norm_gain_grad = pl.pallas_call(
+        functools.partial(finish_kernel, heads=heads, wide=wide),
+        grid=(shard // strip,),
+        in_specs=[ranks_spec(wide), ranks_spec(rest), rows_spec(PROJ), rows_spec(HEADS), rows_spec(1)],
+        out_specs=[rows_spec(PROJ), rows_spec(HEADS), rows_spec(1)],
+        out_shape=[sds((shard, PROJ), F32), sds((shard, HEADS), F32), sds((shard, 1), F32)],
+        compiler_params=params,
+        cost_estimate=pl.CostEstimate(flops=6 * shard * PROJ, bytes_accessed=8 * shard * PROJ, transcendentals=0),
+        name="w_in_finish",
+    )(gate_rows, rest_rows, w_in, w_dt, gain_rows)
+    norm_gain_grad = norm_gain_grad.reshape(shard)
 
     h32 = hidden[0].astype(F32)
     own_r1m = lax.dynamic_slice_in_dim(r1m, rank * local_len, local_len, 0)[:, None]
-    block_out = (h32 + own_r1m * branch.astype(F32)).astype(BF16)[None]
+    block_out = (h32 + own_r1m * branch).astype(BF16)[None]
     r0 = lax.rsqrt(jnp.mean(h32 * h32, axis=1, keepdims=True) + EPS)
     mixed = jnp.sum(dn * h32, axis=1, keepdims=True) / width
     hidden_grad = (out_grad[0].astype(F32) + dn - h32 * (r0 * r0 * mixed))[None]

time: 671 us -> 606 us (0.903)
  waiting for transfers between devices: 86.5 us -> 32.7 us
  other arithmetic: 40.3 us -> 24.2 us
  matrix products: 27.1 us -> 41.7 us
  Pallas kernels: 457 us -> 444 us
    reduce_scatter x1, waiting for transfers between devices: 85.9 us -> 0.01 us  [local(): lax.psum_scatter(wig_gate, 'head', scatter_dimension=0, tiled=True)]
    reduce_scatter x1, waiting for transfers between devices: 0.01 us -> 32.7 us  [local(): pieces = lax.psum_scatter(pieces, 'head', scatter_dimension=0, tiled=False)]
    pallas_call x1 -> x3, Pallas kernels: 208 us -> 189 us  [the longest x1 163 us: local(): pl.pallas_call(grads_kernel, in_specs=[hbm] * 6 + [vmem], out_specs=[hbm]...]
    dot_general x1 -> x2, matrix products: 13.1 us -> 27.7 us  [t_dot(): lax.dot_general(a, b, (((0,), (0,)), ((), ())), preferred_element_type=F32)]
    unnamed x9 -> x0, other arithmetic: 9.92 us -> none
    mul x2 -> x0, other arithmetic: 8.5 us -> none  [the longest x1 8.35 us: local(): w_in_grad = raw_in * gain_rows]
    pallas_call x1, Pallas kernels: 64.1 us -> 70.9 us  [local(): pl.pallas_call(functools.partial(back_kernel, heads=heads, wide=wide), gr...]
  transfers between devices with their start and end apart: 2 -> 2, of which waited for: 1 -> 1; matrix products, arithmetic and copies ran while one was open for 1% -> 2% of each run, Pallas kernels for 10% -> 12%
where the time goes in v3:
time: 606 us; the launch traced here: 598 us
  Pallas kernels  444 us (73%)
  matrix products  41.7 us (7%)
  waiting for transfers between devices  32.7 us (5%)
  local copies, waits for them, and re-layouts  24.6 us (4%)
  other arithmetic  24.2 us (4%)
  blocking collectives  15.6 us (3%)
  between operations  15.4 us (3%)
    pallas_call x1, Pallas kernels, local(): pl.pallas_call(grads_kernel, in_specs=[hbm] * 6 + [vmem], out_specs=[hbm]...  163 us
    pallas_call x1, Pallas kernels, local(): pl.pallas_call(functools.partial(gather_kernel, ring=ring, wide=wide), in...  146 us
    pallas_call x1, Pallas kernels, local(): pl.pallas_call(functools.partial(back_kernel, heads=heads, wide=wide), gr...  70.9 us
    pallas_call x1, Pallas kernels, local(): pl.pallas_call(functools.partial(scan_kernel, heads=heads, wide=wide), gr...  38.9 us
    reduce_scatter x1, waiting for transfers between devices, local(): pieces = lax.psum_scatter(pieces, 'head', scatter_dimension=0, tiled=False)  32.7 us
    dot_general x2, matrix products, t_dot(): lax.dot_general(a, b, (((0,), (0,)), ((), ())), preferred_element_type=F32)  27.7 us
    pallas_call x1, Pallas kernels, local(): pl.pallas_call(gate_kernel, grid=grid, in_specs=[forth(wide), forth(LANES...  15.8 us
    psum x1, blocking collectives, local(): lax.psum(sums[:2].reshape(2, tokens // LANES, LANES), 'seq')  15.6 us
  transfers between devices with their start and end apart: 2, of which 1 were waited for; matrix products, arithmetic and copies ran while one was open for 2% of the time, Pallas kernels for 12%

profile of v3, /device:TPU:8, one launch (start us, length us, event | category | flops | bytes accessed | tf_op | source)
XLA Modules:
  0.0 598.5 jit_solution(13892874799010919891)
XLA Ops:
  7.2 0.7 convert_element_type.86
  7.9 0.8 copy.48.gain_ref
  8.7 0.8 reshape.184
  9.4 3.5 concatenate.28
  13.0 0.7 multiply_convert_fusion.4
  13.7 0.1 copy.47
  13.9 0.7 pad_maximum_fusion.dtw_ref
  14.7 145.6 %gather_project.1 = (bf16[2048,2048]{1,0:T(8,128)(2,1)}, bf16[2048,2048]{1,0:T(8,128)(2,1)}, bf16[2048,2432]{1,0:T(8,128)(2,1)}, bf16[1024,2048]{1,0:T(8,128)(2,...) custom-call(bf16[512,2048]{1,0:T(8,128)(2,1)} %bitcast.69, ...), custom_call_target="tpu_custom_call" | custom-call | flops 28991029248 | bytes 36700160 | tf_op jit(solution)/shard_map/gather_project/pallas_call | solution.py:994
  160.3 1.2 slice.121
  161.5 0.5 reshape.187
  162.0 0.1 reshape.188
  163.0 0.8 fusion.9.exp_ref
  164.2 0.6 fusion.14.cw_ref
  164.9 0.6 stack.19.rowp_ref
  165.5 0.6 broadcast_in_dim.84.cb_ref
  166.1 0.6 broadcast_in_dim.85.dtb_ref
  166.7 0.7 broadcast_in_dim.88.colp_ref
  167.4 38.9 %scan.1 = (bf16[2048,1280]{1,0:T(8,128)(2,1)}, bf16[2048,1280]{1,0:T(8,128)(2,1)}, f32[2048,128]{1,0:T(8,128)}, f32[2048,1024]{1,0:T(8,128)}, bf16[2048,1024]{1,...) custom-call(bf16[2048,1280]{1,0:T(8,128)(2,1)} %get-tuple-element.43.u_ref, ...), custom_call_target="tpu_custom_call" | custom-call | flops 12884901888 | bytes 33554432 | tf_op jit(solution)/shard_map/scan/pallas_call | solution.py:1083
  206.3 0.8 slice_bitcast_fusion
  207.1 15.6 %psum.7 = f32[2,16,128]{2,1,0:T(8,128)S(1)} all-reduce(f32[2,16,128]{2,1,0:T(8,128)S(1)} %bitcast.75), channel_id=1, replica_groups=mesh['seq'=4,'head'=8] {'seq'}, use_global_device_ids=true, to_apply=%region_0.1 | all-reduce | flops 4096 | bytes 32768 | tf_op jit(solution)/shard_map/psum | solution.py:1112
  223.4 14.1 %convolution_convert_fusion.part_ref = bf16[2048,2048]{1,0:T(8,128)(2,1)} fusion(bf16[2048,1024]{1,0:T(8,128)(2,1)} %get-tuple-element.53, bf16[1024,2048]{1,0:T(8,128)(2,1)} %get-tuple-element.57), kind=kOutput, calls=%fused_computation.3 | convolution fusion | flops 8594128896 | bytes 16777216 | tf_op jit(solution)/shard_map/dot_general | solution.py:26
  237.5 13.6 %fusion.7 = bf16[1024,2048]{1,0:T(8,128)(2,1)} fusion(bf16[2048,1024]{1,0:T(8,128)(2,1)S(1)} %copy-done.4, bf16[2048,2048]{1,0:T(8,128)(2,1)} %get-tuple-element.54, f32[2048]{0:T(1024)S(1)} %get-tuple-element.127), kind=kOutput, calls=%fused_computation.15 | convolution fusion | flops 8604614656 | bytes 16785408 | tf_op jit(solution)/shard_map/dot_general | solution.py:34
  251.0 1.6 select_select_fusion.stat_ref
  252.6 15.8 %gate_back.1 = (bf16[2048,1024]{1,0:T(8,128)(2,1)}, bf16[2048,1024]{1,0:T(8,128)(2,1)}) custom-call(bf16[2048,1280]{1,0:T(8,128)(2,1)} %get-tuple-element.49.x_ref.act_ref, f32[2048,128]{1,0:T(8,128)} %get-tuple-element.50.aux_ref, bf16[2048,1024]{1,0:T(8,128)(2,1)} %get-tuple-element.45.z_ref, bf16[2048,1024]{1,0:T(8,128)(2,1)} %get-tuple-element.46.d0_ref, ...), custom_call_target="tpu_custom_call" | custom-call | flops 41943040 | bytes 29360128 | tf_op jit(solution)/shard_map/gate_back/pallas_call | solution.py:1121
  268.5 14.1 %convolution_convert_fusion.1 = bf16[2048,1024]{1,0:T(8,128)(2,1)} fusion(bf16[2048,2048]{1,0:T(8,128)(2,1)} %get-tuple-element.55.h_ref, bf16[2048,1024]{1,0:T(8,128)(2,1)} %get-tuple-element.56.dpg_ref), kind=kOutput, calls=%fused_computation.16 | convolution fusion | flops 8592031744 | bytes 16777216 | tf_op jit(solution)/shard_map/dot_general | solution.py:34
  282.6 4.7 copy.61
  287.4 0.7 copy-done.2
  288.1 0.7 copy.51.dtw_ref
  288.9 0.9 fusion.10.seg_ref
  289.8 70.9 %scan_back.1 = (bf16[2048,1408]{1,0:T(8,128)(2,1)}, f32[8,1280]{1,0:T(8,128)}, f32[512,2048]{1,0:T(8,128)}) custom-call(bf16[2048,1280]{1,0:T(8,128)(2,1)} %get-tuple-element.49.x_ref.act_ref, f32[2048,128]{1,0:T(8,128)} %get-tuple-element.50.aux_ref, bf16[2048,1024]{1,0:T(8,128)(2,1)} %get-tuple-element.58.dy_ref, f32[2048,1024]{1,0:T(8,128)} %get-tuple-element.51.y_ref, ...), custom_call_target="tpu_custom_call" | custom-call | flops 12884901888 | bytes 50331648 | tf_op jit(solution)/shard_map/scan_back/pallas_call | solution.py:1141
  360.7 0.8 convert.22
  361.5 0.8 slice_reduce_fusion.1
  362.4 0.1 reduce_sum.45
  362.6 0.7 convert_element_type.101.tiny_ref
  363.4 32.7 %reduce-scatter.5.cloned.1.call-done = bf16[1,2,64,2048]{3,2,1,0:T(8,128)(2,1)} async-done(((bf16[8,2,64,2048]{3,2,1,0:T(8,128)(2,1)}), bf16[1,2,64,2048]{3,2,1,0:T(8,128)(2,1)}) %reduce-scatter.5.cloned.1.call-update) | async-done | bytes 524304 | tf_op jit(solution)/shard_map/reduce_scatter | solution.py:1174
  396.1 163.1 %weight_grads.1 = (f32[512,2048]{1,0:T(8,128)}, bf16[4,256,1024]{2,1,0:T(8,128)(2,1)}, bf16[4,256,1408]{2,1,0:T(8,128)(2,1)}, bf16[8,64,2048]{2,1,0:T(8,128)(2,1)}) custom-call(bf16[2048,1024]{1,0:T(8,128)(2,1)} %get-tuple-element.56.dpg_ref, bf16[2048,1408]{1,0:T(8,128)(2,1)} %get-tuple-element.63.dp_ref, bf16[2048,2432]{1,0:T(8,128)(2,1)} %get-tuple-element.47.w_ref, ...), custom_call_target="tpu_custom_call" | custom-call | flops 40802189312 | bytes 39845888 | tf_op jit(solution)/shard_map/weight_grads/pallas_call | solution.py:1176
  559.2 1.1 slice.110
  560.3 0.2 reshape.199
  560.8 0.6 slice.141
  561.4 0.6 slice_reduce_fusion.2
  562.0 3.0 fusion.3
  565.0 9.8 %w_in_finish.1 = (f32[256,8448]{1,0:T(8,128)}, f32[256,64]{1,0:T(8,128)}, f32[256,1]{1,0:T(8,128)}) custom-call(bf16[4,256,1024]{2,1,0:T(8,128)(2,1)} %get-tuple-element.68.gate_ref, bf16[4,256,1408]{2,1,0:T(8,128)(2,1)} %get-tuple-element.69.rest_ref, bf16[256,8448]{1,0:T(8,128)(2,1)} %w_ref.3, bf16[256,64]{1,0:T(8,128)(2,1)} %copy.51.dtw_ref, ...), custom_call_target="tpu_custom_call" | custom-call | flops 12976128 | bytes 17301504 | tf_op jit(solution)/shard_map/w_in_finish/pallas_call | solution.py:1237
  574.8 1.6 copy.54
  576.7 0.5 slice_bitcast_fusion.5
  577.2 4.8 multiply_reduce_fusion
  582.0 0.6 convert_divide_fusion
  582.6 0.7 reduce.1
  583.3 7.9 %fusion.6 = (f32[1,512,2048]{2,1,0:T(8,128)}, bf16[1,512,2048]{2,1,0:T(8,128)(2,1)}) fusion(f32[512,2048]{1,0:T(8,128)} %get-tuple-element.67, f32[512]{0:T(512)S(1)} %multiply_multiply_fusion.1, bf16[1,512,2048]{2,1,0:T(8,128)(2,1)} %param.15, bf16[1,512,2048]{2,1,0:T(8,128)(2,1)S(1)} %copy-done, f32[512,2048]{1,0:T(8,128)} %get-tuple-element.62, ...), kind=kLoop, calls=%fused_computation.12 | loop fusion | flops 8388608 | bytes 18878464 | tf_op jit(solution)/shard_map/broadcast_in_dim | solution.py:1254
  (70 shorter events, 2.3 us)
Async XLA Ops:
  7.2 356.2 %reduce-scatter.3.cloned.1.call-start = ((), (), s32[]{:S(2)}) async-start(), calls=%async_computation.2 | async-start | bytes 4718592 | tf_op jit(solution)/shard_map/reduce_scatter | solution.py:1138
  223.4 14.1 %copy-start.4 = (bf16[2048,1024]{1,0:T(8,128)(2,1)S(1)}, bf16[2048,1024]{1,0:T(8,128)(2,1)}, u32[]{:S(2)}) copy-start(bf16[2048,1024]{1,0:T(8,128)(2,1)} %get-tuple-element.53) | copy-start | bytes 12582916
  282.6 113.5 %reduce-scatter.5.cloned.1.call-start = ((), (), s32[]{:S(2)}) async-start(), calls=%async_computation.3 | async-start | bytes 4718592 | tf_op jit(solution)/shard_map/reduce_scatter | solution.py:1174
  287.4 0.8 copy-start.2
  396.1 165.9 %copy-start = (bf16[1,512,2048]{2,1,0:T(8,128)(2,1)S(1)}, bf16[1,512,2048]{2,1,0:T(8,128)(2,1)}, u32[]{:S(2)}) copy-start(bf16[1,512,2048]{2,1,0:T(8,128)(2,1)} %param.13) | copy-start | bytes 6291460
  577.2 4.8 copy-start.3
  577.2 5.4 copy-start.1
Sparse Core Ops, SparseCore 0:
  282.7 62.7 reduce-scatter.2
  347.8 48.2 reduce-scatter.4

commit v4 on v3

--- a/solution.py
+++ b/solution.py
@@ -35,7 +35,7 @@
 
 
 def sigmoid(v):
-    return 1.0 / (1.0 + jnp.exp(-v))
+    return 0.5 * jnp.tanh(0.5 * v) + 0.5
 
 
 def remote(src, dst, send, recv, target):
@@ -313,9 +313,12 @@
         if ring:
             o_tick(2 + i)
 
+    if ring:
+        o_tick(6)
     o_far = relay(ov, o_sems, o_open)
     if ring:
-        o_tick(6)
+        for t in range(7, chunks + 3):
+            o_tick(t)
         for i in range(chunks):
             o_swap(i).wait_recv()
     o_out.start()
@@ -359,6 +362,22 @@
     return causal, dt_e, cum_e, cum_c, cum_t
 
 
+def shift_matrix(rows, by):
+    r = lax.broadcasted_iota(jnp.int32, (rows, rows), 0)
+    c = lax.broadcasted_iota(jnp.int32, (rows, rows), 1)
+    return jnp.where(c == r + by, 1.0, 0.0).astype(BF16)
+
+
+def lower_parts(cum_c, cum_t, h, causal):
+    mid = causal.shape[0] // 2
+    near = causal[:mid, :mid]
+    col, row = cum_c[:, h : h + 1], cum_t[h : h + 1, :]
+    top = jnp.exp(jnp.where(near, col[:mid] - row[:, :mid], -1e30))
+    low = jnp.exp(col[mid:] - row[:, :mid])
+    right = jnp.exp(jnp.where(near, col[mid:] - row[:, mid:], -1e30))
+    return top, low, right
+
+
 def scan_kernel(
     u_ref, d_ref, z_ref, d0_ref, cw_ref, cb_ref, dtb_ref, exp_ref, rowp_ref, colp_ref,
     act_ref, slope_ref, aux_ref, y_ref, gg_ref, st_ref, sum_ref, state, ext, *, heads, wide,
@@ -370,16 +389,18 @@
     @pl.when(step == 0)
     def _():
         state[...] = jnp.zeros_like(state)
-        ext[0:8, :] = jnp.zeros((8, chans), F32)
-
-    @pl.when(step > 0)
-    def _():
-        ext[0:8, :] = ext[rows : rows + 8, :]
-
-    ext[8 : rows + 8, :] = u_ref[...].astype(F32)
-    pre = cb_ref[0:1, :]
-    for k in range(KERNEL):
-        pre = pre + cw_ref[k : k + 1, :] * ext[pl.ds(8 - (KERNEL - 1) + k, rows), :]
+        ext[...] = jnp.zeros_like(ext)
+
+    u = u_ref[...]
+    u32 = u.astype(F32)
+    pre = cb_ref[0:1, :] + cw_ref[KERNEL - 1 : KERNEL, :] * u32
+    before = jnp.zeros((8, chans), F32)
+    for j in range(1, KERNEL):
+        tap = cw_ref[KERNEL - 1 - j : KERNEL - j, :]
+        pre = pre + tap * dot(shift_matrix(rows, -j), u)
+        before = before + tap * ext[8 - j : 16 - j, :]
+    pre = jnp.concatenate([pre[:8] + before, pre[8:]], axis=0)
+    ext[0:8, :] = u32[rows - 8 :, :]
     sig = sigmoid(pre)
     act = (pre * sig).astype(BF16)
     act_ref[...] = act
@@ -407,15 +428,19 @@
     scores = dot_t(c, b)
     st = state[...]
     st_ref[0] = st
+    mid = rows // 2
     half = lax.broadcasted_iota(jnp.int32, (rows, LANES), 1) < HEAD_DIM
     parts = []
     for pair in range(heads // 2):
         x2 = xdt16[:, LANES * pair : LANES * (pair + 1)]
         got = []
         for h in (2 * pair, 2 * pair + 1):
-            spread = cum_c[:, h : h + 1] - cum_t[h : h + 1, :]
-            m = (scores * jnp.exp(jnp.where(causal, spread, -1e30))).astype(BF16)
-            got.append(dot(m, x2))
+            top, low, right = lower_parts(cum_c, cum_t, h, causal)
+            m_top = (scores[:mid, :mid] * top).astype(BF16)
+            m_low = (scores[mid:, :mid] * low).astype(BF16)
+            m_right = (scores[mid:, mid:] * right).astype(BF16)
+            y_low = dot(jnp.concatenate([m_low, m_right], axis=1), x2)
+            got.append(jnp.concatenate([dot(m_top, x2[:mid]), y_low], axis=0))
         parts.append(jnp.where(half, got[0], got[1]))
     y = jnp.concatenate(parts, axis=1) + dot(c, st.astype(BF16)) * jnp.exp(cum_e)
     last = cum_e[rows - 1 : rows, :]
@@ -442,6 +467,113 @@
     return dot(hi, seg) + dot(mid, seg) + dot(low, seg)
 
 
+def blend_kernel(
+    gg_ref, wo_ref, og_ref, sums_ref, mask_ref,
+    stat_ref, part_ref, wog_ref,
+    ggv, wov, ogv, far_p, y_p, x_p, own_p, far_a, far_b, sv, staged,
+    load_sem, d_send, d_recv, s_send, s_recv, out_sem, w_sem,
+):
+    s = lax.axis_index("seq")
+    q = far_p.shape[0]
+    half = q // 2
+    rows = min(CHUNK, q)
+    x_peer = s + 1 - 2 * lax.rem(s, 2)
+    y_peer = lax.rem(s + 2, 4)
+    far = 3 - s
+    to_x, to_y, to_far = {"seq": x_peer}, {"seq": y_peer}, {"seq": far}
+    loads = [
+        pltpu.make_async_copy(src, dst, load_sem.at[i])
+        for i, (src, dst) in enumerate(((gg_ref, ggv), (wo_ref, wov), (og_ref, ogv)))
+    ]
+    for copy in loads:
+        copy.start()
+    sv[s] = sums_ref[...]
+    greet([to_x, to_y, to_far])
+    sums = [
+        remote(sums_ref, sv.at[s], s_send.at[i], s_recv.at[i], peer) for i, peer in enumerate((to_x, to_y, to_far))
+    ]
+    for copy in sums:
+        copy.start()
+    loads[0].wait()
+    loads[1].wait()
+
+    def part(block, out):
+        @pl.loop(0, q // rows)
+        def _(j):
+            at = pl.ds(pl.multiple_of(block * q + j * rows, 16), rows)
+            to = pl.ds(pl.multiple_of(j * rows, 16), rows)
+            out[to, :] = dot(ggv[at, :], wov[...]).astype(BF16)
+
+    part(far, far_p)
+    d0 = remote(far_p.at[:half], far_a, d_send.at[0], d_recv.at[0], to_x)
+    d1 = remote(far_p.at[half:], far_b, d_send.at[1], d_recv.at[1], to_y)
+    d0.start()
+    d1.start()
+    part(y_peer, y_p)
+    part(x_peer, x_p)
+    part(s, own_p)
+    own_out = pltpu.make_async_copy(own_p, part_ref.at[2], out_sem.at[2])
+    own_out.start()
+
+    for copy in sums:
+        copy.wait_recv()
+    total = (sv[0] + sv[1]) + (sv[2] + sv[3])
+    r1 = lax.rsqrt(total[0:1] / DI + EPS)
+    r1m = r1 * mask_ref[0:1]
+    coef = r1m * r1 * r1 * total[1:2] / DI
+    sub = lax.broadcasted_iota(jnp.int32, (LANES, r1.shape[1]), 0)
+    stat = jnp.where(sub == 0, r1m, jnp.where(sub == 1, coef, 0.0)).T
+    stat_ref[...] = stat
+
+    @pl.loop(0, ggv.shape[0] // rows)
+    def _(j):
+        at = pl.ds(pl.multiple_of(j * rows, 16), rows)
+        ggv[at, :] = (ggv[at, :].astype(F32) * stat_ref[at, 0:1]).astype(BF16)
+
+    loads[2].wait()
+    tile = 256
+    ring = len(wog_ref.shape) == 4
+
+    def w_out(m):
+        slot = lax.rem(m, 2)
+        if ring:
+            per = tile // wog_ref.shape[2]
+            groups = wov.shape[0] // 2 // tile
+            to = wog_ref.at[pl.ds(lax.rem(m, groups) * per, per), m // groups]
+            src = staged.at[slot].reshape(per, wog_ref.shape[2], wog_ref.shape[3])
+        else:
+            to = wog_ref.at[pl.ds(pl.multiple_of(m * tile, tile), tile), :]
+            src = staged.at[slot]
+        return pltpu.make_async_copy(src, to, w_sem.at[slot])
+
+    count = wov.shape[0] // tile
+
+    @pl.loop(0, count)
+    def _(m):
+        @pl.when(m >= 2)
+        def _():
+            w_out(m - 2).wait()
+
+        at = pl.ds(pl.multiple_of(m * tile, tile), tile)
+        staged[lax.rem(m, 2)] = t_dot(ggv[:, at], ogv[...]).astype(BF16)
+        w_out(m).start()
+
+    d0.wait_recv()
+    y_p[:half, :] = (y_p[:half, :].astype(F32) + far_a[...].astype(F32)).astype(BF16)
+    y_out = pltpu.make_async_copy(y_p, part_ref.at[0], out_sem.at[0])
+    y_out.start()
+    d1.wait_recv()
+    x_p[half:, :] = (x_p[half:, :].astype(F32) + far_b[...].astype(F32)).astype(BF16)
+    x_out = pltpu.make_async_copy(x_p, part_ref.at[1], out_sem.at[1])
+    x_out.start()
+    w_out(count - 2).wait()
+    w_out(count - 1).wait()
+    for copy in (own_out, y_out, x_out):
+        copy.wait()
+    for copy in sums + [d0, d1]:
+        copy.wait_send()
+
+
 def gate_kernel(x_ref, aux_ref, z_ref, d0_ref, y_ref, stat_ref, rowp_ref, dy_ref, dpg_ref):
     stat = stat_ref[...]
     r1m = stat[:, 0:1]
@@ -459,7 +591,7 @@
 def back_kernel(
     act_ref, aux_ref, dy_ref, y_ref, st_ref, slope_ref, u_ref, part_ref,
     exp_ref, seg_ref, rowp_ref, colp_ref, cw_ref,
-    dp_ref, sm_ref, br_ref, adj, ext, y_b, x_b, own_b, far_a, far_b, y_f, x_f, br_o,
+    dp_ref, sm_ref, br_ref, adj, ext, own_b, y_f, x_f, br_o,
     b_send, b_recv, b_load, *, heads, wide,
 ):
     step = pl.program_id(0)
@@ -468,56 +600,25 @@
     chans = u_ref.shape[1]
 
     s = lax.axis_index("seq")
-    q = y_b.shape[0]
-    half = q // 2
     x_peer = s + 1 - 2 * lax.rem(s, 2)
     y_peer = lax.rem(s + 2, 4)
     to_x, to_y = {"seq": x_peer}, {"seq": y_peer}
-
-    def at_rows(block, start, size):
-        return part_ref.at[pl.ds(pl.multiple_of(block * q + start, 16), size), :]
-
-    def b_copy(src, dst, i, target):
-        return remote(src, dst, b_send.at[i], b_recv.at[i], target)
-
-    out_a = b_copy(at_rows(3 - s, 0, half), far_a, 0, to_x)
-    out_b = b_copy(at_rows(3 - s, half, half), far_b, 1, to_y)
-    out_y = b_copy(y_b, y_f, 2, to_y)
-    out_x = b_copy(x_b, x_f, 3, to_x)
-    b_loads = [
-        pltpu.make_async_copy(at_rows(y_peer, 0, q), y_b, b_load.at[0]),
-        pltpu.make_async_copy(at_rows(x_peer, 0, q), x_b, b_load.at[1]),
-        pltpu.make_async_copy(at_rows(s, 0, q), own_b, b_load.at[2]),
-    ]
+    out_y = remote(part_ref.at[0], y_f, b_send.at[0], b_recv.at[0], to_y)
+    out_x = remote(part_ref.at[1], x_f, b_send.at[1], b_recv.at[1], to_x)
+    own_load = pltpu.make_async_copy(part_ref.at[2], own_b, b_load.at[0])
 
     @pl.when(step == 0)
     def _():
         greet([to_x, to_y])
-        out_a.start()
-        out_b.start()
-        for copy in b_loads:
-            copy.start()
-
-    @pl.when(step == 3)
-    def _():
-        for copy in b_loads:
-            copy.wait()
-        out_a.wait_recv()
-        y_b[:half, :] = (y_b[:half, :].astype(F32) + far_a[...].astype(F32)).astype(BF16)
         out_y.start()
-        out_b.wait_recv()
-        x_b[half:, :] = (x_b[half:, :].astype(F32) + far_b[...].astype(F32)).astype(BF16)
         out_x.start()
+        own_load.start()
 
     @pl.when(step == 0)
     def _():
         sm_ref[...] = jnp.zeros_like(sm_ref)
         adj[...] = jnp.zeros_like(adj)
-        ext[rows : rows + 8, :] = jnp.zeros((8, chans), F32)
-
-    @pl.when(step > 0)
-    def _():
-        ext[rows : rows + 8, :] = ext[0:8, :]
+        ext[...] = jnp.zeros_like(ext)
 
     x = act_ref[:, :wide]
     x32 = x.astype(F32)
@@ -545,6 +646,7 @@
     tail = jnp.exp(last - cum_e)
     half = lax.broadcasted_iota(jnp.int32, (rows, LANES), 1) < HEAD_DIM
     zero = jnp.zeros((rows, LANES), BF16)
+    mid = rows // 2
     n_sum = None
     parts = []
     for pair in range(heads // 2):
@@ -554,21 +656,28 @@
         got = []
         for side in range(2):
             h = 2 * pair + side
-            spread = cum_c[:, h : h + 1] - cum_t[h : h + 1, :]
-            ell = jnp.exp(jnp.where(causal, spread, -1e30))
-            m = (scores * ell).astype(BF16)
-            got.append(t_dot(m, dy2))
+            top, low, right = lower_parts(cum_c, cum_t, h, causal)
+            m_top = (scores[:mid, :mid] * top).astype(BF16)
+            m_low = (scores[mid:, :mid] * low).astype(BF16)
+            m_right = (scores[mid:, mid:] * right).astype(BF16)
+            v_top = t_dot(jnp.concatenate([m_top, m_low], axis=0), dy2)
+            got.append(jnp.concatenate([v_top, t_dot(m_right, dy2[mid:])], axis=0))
             own = half if side == 0 else jnp.logical_not(half)
-            n = dot_t(jnp.where(own, dy2, zero), x2) * ell
-            n_sum = n if n_sum is None else n_sum + n
+            dy_own = jnp.where(own, dy2, zero)
+            g_top = dot_t(dy_own[:mid], x2[:mid])
+            g_low = dot_t(dy_own[mid:], x2)
+            n = [g_top * top, g_low[:, :mid] * low, g_low[:, mid:] * right]
+            n_sum = n if n_sum is None else [p + v for p, v in zip(n_sum, n)]
         parts.append(jnp.where(half, got[0], got[1]))
+    n_low = jnp.concatenate([n_sum[1], n_sum[2]], axis=1).astype(BF16)
+    n_top = n_sum[0].astype(BF16)
     out_part = dot(b, q16) * tail
     v = jnp.concatenate(parts, axis=1) + out_part
-    n16 = n_sum.astype(BF16)
     dy_e = (dy * ecum).astype(BF16)
     x_tail = (xdt * tail).astype(BF16)
-    d_b = t_dot(n16, c) + dot_t(x_tail, q16)
-    d_c = dot(n16, b) + dot_t(dy_e, st16)
+    d_b = jnp.concatenate([t_dot(jnp.concatenate([n_top, n_low[:, :mid]], axis=0), c), t_dot(n_low[:, mid:], c[mid:])], axis=0)
+    d_b = d_b + dot_t(x_tail, q16)
+    d_c = jnp.concatenate([dot(n_top, b[:mid]), dot(n_low, b)], axis=0) + dot_t(dy_e, st16)
     elast = jnp.exp(last)
     adj[...] = elast * q_in + t_dot(c, dy_e)
 
@@ -597,14 +706,17 @@
 
     d_act = jnp.concatenate([skip_e * dy + dt_e * v, d_b, d_c], axis=1)
     d_conv = d_act * slope_ref[...].astype(F32)
-    ext[0:rows, :] = d_conv
+    d_conv16 = d_conv.astype(BF16)
     u = u_ref[...].astype(F32)
-    d_u = None
-    for k in range(KERNEL):
-        moved = ext[pl.ds(KERNEL - 1 - k, rows), :]
-        term = cw_ref[k : k + 1, :] * moved
-        d_u = term if d_u is None else d_u + term
+    d_u = cw_ref[KERNEL - 1 : KERNEL, :] * d_conv
+    sm_ref[KERNEL - 1 : KERNEL, :] += jnp.sum(u * d_conv, axis=0, keepdims=True)
+    for j in range(1, KERNEL):
+        k = KERNEL - 1 - j
+        moved = dot(shift_matrix(rows, j), d_conv16)
+        moved = jnp.concatenate([moved[: rows - 8], moved[rows - 8 :] + ext[j : j + 8, :]], axis=0)
+        d_u = d_u + cw_ref[k : k + 1, :] * moved
         sm_ref[k : k + 1, :] += jnp.sum(u * moved, axis=0, keepdims=True)
+    ext[8:16, :] = d_conv[0:8, :]
     dp_ref[:, :chans] = (r0 * d_u).astype(BF16)
     sm_ref[4:5, :] += jnp.sum(d_conv, axis=0, keepdims=True)
     sm_ref[5:6, :wide] += jnp.sum(x32 * dy, axis=0, keepdims=True)
@@ -613,12 +725,13 @@
 
     @pl.when(step == steps - 1)
     def _():
+        own_load.wait()
         out_y.wait_recv()
         out_x.wait_recv()
         br_o[...] = own_b[...].astype(F32) + y_f[...].astype(F32) + x_f[...].astype(F32)
-        last_copy = pltpu.make_async_copy(br_o, br_ref, b_load.at[3])
+        last_copy = pltpu.make_async_copy(br_o, br_ref, b_load.at[1])
         last_copy.start()
-        for copy in (out_a, out_b, out_y, out_x):
+        for copy in (out_y, out_x):
             copy.wait_send()
         last_copy.wait()
 
@@ -1016,7 +1129,8 @@
             pltpu.VMEM((tokens, LANES), F32),
             pltpu.VMEM((tokens, wide), BF16),
         ]
-        + [dma(4)] * 14
+        + [dma(4)] * 9
+        + [dma(8)] * 5
         + [dma(6), dma(26)],
         compiler_params=pltpu.CompilerParams(
             collective_id=0, has_side_effects=True, vmem_limit_bytes=56 * 1024 * 1024
@@ -1101,7 +1215,7 @@
             sds((steps, STATE, wide), F32),
             sds((8, tokens), F32),
         ],
-        scratch_shapes=[pltpu.VMEM((STATE, wide), F32), pltpu.VMEM((chunk + 8, chans), F32)],
+        scratch_shapes=[pltpu.VMEM((STATE, wide), F32), pltpu.VMEM((16, chans), F32)],
         compiler_params=params,
         cost_estimate=pl.CostEstimate(
             flops=2 * tokens * wide * 12 * chunk, bytes_accessed=tokens * wide * 16, transcendentals=tokens * chunk * heads
@@ -1109,15 +1223,35 @@
         name="scan",
     )(u, d_raw, z, d0, cw, cb, dtb, expand, rowp, colp)
 
-    sums = lax.psum(sums[:2].reshape(2, tokens // LANES, LANES), "seq").reshape(2, tokens)
     mask = (jnp.arange(tokens, dtype=jnp.int32) < lengths[0]).astype(F32)
-    r1 = lax.rsqrt(sums[0] / DI + EPS)
-    r1m = r1 * mask
-    coef = r1m * r1 * r1 * sums[1] / DI
-    lane = jnp.arange(LANES, dtype=jnp.int32)[None]
-    stat2 = jnp.where(lane == 0, r1m[:, None], jnp.where(lane == 1, coef[:, None], 0.0))
-
-    partial = dot(gg, w_o).astype(BF16)
+    n_own = DI // owners
+    piece = n_own // owners
+    wog_shape = (owners, owners // ranks, piece, width) if ring else (wide, width)
+    stat2, partial, wog = pl.pallas_call(
+        blend_kernel,
+        in_specs=[hbm, hbm, hbm, vmem, vmem],
+        out_specs=[vmem, hbm, hbm],
+        out_shape=[sds((tokens, LANES), F32), sds((3, local_len, width), BF16), sds(wog_shape, BF16)],
+        scratch_shapes=[
+            pltpu.VMEM((tokens, wide), BF16),
+            pltpu.VMEM((wide, width), BF16),
+            pltpu.VMEM((tokens, width), BF16),
+        ]
+        + [pltpu.VMEM((local_len, width), BF16)] * 4
+        + [pltpu.VMEM((local_len // 2, width), BF16)] * 2
+        + [pltpu.VMEM((ranks, 8, tokens), F32), pltpu.VMEM((2, 256, width), BF16)]
+        + [dma(3), dma(2), dma(2), dma(3), dma(3), dma(3), dma(2)],
+        compiler_params=pltpu.CompilerParams(
+            collective_id=3, has_side_effects=True, vmem_limit_bytes=56 * 1024 * 1024
+        ),
+        cost_estimate=pl.CostEstimate(
+            flops=4 * tokens * wide * width, bytes_accessed=4 * tokens * (width + wide), transcendentals=0
+        ),
+        name="blend",
+    )(gg, w_o, og_all, sums, jnp.broadcast_to(mask[None], (8, tokens)))
+
+    if ring:
+        pieces = lax.psum_scatter(wog, "head", scatter_dimension=0, tiled=False)
     dy, dpg = pl.pallas_call(
         gate_kernel,
         grid=grid,
@@ -1131,10 +1265,8 @@
         name="gate_back",
     )(act, aux, z, d0, y, stat2, rowp)
 
-    og_scaled = (og_all.astype(F32) * r1m[:, None]).astype(BF16)
-    wog = t_dot(gg, og_scaled).astype(BF16)
     wig_gate = t_dot(h_all, dpg).astype(BF16)
-    dy, wog, wig_gate, partial = lax.optimization_barrier((dy, wog, wig_gate, partial))
+    dy, wig_gate = lax.optimization_barrier((dy, wig_gate))
     own_gate = lax.psum_scatter(wig_gate, "head", scatter_dimension=0, tiled=True)
 
     rest = chans + LANES
@@ -1149,12 +1281,10 @@
         ],
         out_specs=[back(rest), pl.BlockSpec((8, chans), lambda j: (0, 0)), hbm],
         out_shape=[sds((tokens, rest), BF16), sds((8, chans), F32), sds((local_len, width), F32)],
-        scratch_shapes=[pltpu.VMEM((STATE, wide), F32), pltpu.VMEM((chunk + 8, chans), F32)]
+        scratch_shapes=[pltpu.VMEM((STATE, wide), F32), pltpu.VMEM((16, chans), F32)]
         + [pltpu.VMEM((local_len, width), BF16)] * 3
-        + [pltpu.VMEM((local_len // 2, width), BF16)] * 2
-        + [pltpu.VMEM((local_len, width), BF16)] * 2
         + [pltpu.VMEM((local_len, width), F32)]
-        + [dma(4)] * 3,
+        + [dma(2)] * 3,
         compiler_params=pltpu.CompilerParams(
             dimension_semantics=("arbitrary",), collective_id=2, has_side_effects=True,
             vmem_limit_bytes=56 * 1024 * 1024,
@@ -1167,11 +1297,7 @@
 
     skip_h = jnp.sum(sm[5, :wide].reshape(heads, HEAD_DIM), axis=1)
     tiny = jnp.concatenate([sm[:5].reshape(-1), sm[6, :heads], sm[7, :heads], skip_h])
-    n_own = DI // owners
     if ring:
-        piece = n_own // owners
-        pieces = wog.reshape(owners // ranks, owners, piece, width).swapaxes(0, 1)
-        pieces = lax.psum_scatter(pieces, "head", scatter_dimension=0, tiled=False)
         laid = jnp.pad(tiny, (0, shard * spare - tiny.shape[0])).reshape(shard, spare).astype(BF16)
         dn, gate_rows, rest_rows, w_out_grad = pl.pallas_call(
             grads_kernel,
@@ -1247,7 +1373,7 @@
     norm_gain_grad = norm_gain_grad.reshape(shard)
 
     h32 = hidden[0].astype(F32)
-    own_r1m = lax.dynamic_slice_in_dim(r1m, rank * local_len, local_len, 0)[:, None]
+    own_r1m = lax.dynamic_slice_in_dim(stat2[:, 0:1], rank * local_len, local_len, 0)
     block_out = (h32 + own_r1m * branch).astype(BF16)[None]
     r0 = lax.rsqrt(jnp.mean(h32 * h32, axis=1, keepdims=True) + EPS)
     mixed = jnp.sum(dn * h32, axis=1, keepdims=True) / width

time: 606 us -> 577 us (0.952)
  matrix products: 41.7 us -> 14 us
  blocking collectives: 15.6 us -> 0 us
  waiting for transfers between devices: 32.7 us -> 42.9 us
  Pallas kernels: 444 us -> 453 us
    pallas_call x0 -> x1, Pallas kernels: none -> 32.9 us  [local(): pl.pallas_call(blend_kernel, in_specs=[hbm, hbm, hbm, vmem, vmem], out_sp...]
    pallas_call x1, Pallas kernels: 70.9 us -> 53.7 us  [local(): pl.pallas_call(functools.partial(back_kernel, heads=heads, wide=wide), gr...]
    psum x1 -> x0, blocking collectives: 15.6 us -> none  [local(): lax.psum(sums[:2].reshape(2, tokens // LANES, LANES), 'seq')]
    dot_general x1 -> x0, matrix products: 14.1 us -> none  [dot(): return jnp.dot(a, b, preferred_element_type=F32)]
    dot_general x2 -> x1, matrix products: 27.7 us -> 14 us  [t_dot(): lax.dot_general(a, b, (((0,), (0,)), ((), ())), preferred_element_type=F32)]
    reduce_scatter x1, waiting for transfers between devices: 32.7 us -> 42.1 us  [local(): pieces = lax.psum_scatter(wog, 'head', scatter_dimension=0, tiled=False)]
    pallas_call x1, Pallas kernels: 38.9 us -> 32.1 us  [local(): pl.pallas_call(functools.partial(scan_kernel, heads=heads, wide=wide), gr...]
  transfers between devices with their start and end apart: 2 -> 2, of which waited for: 1 -> 1; matrix products, arithmetic and copies ran while one was open for 2% -> 1% of each run, Pallas kernels for 12% -> 9%
where the time goes in v4:
time: 577 us; the launch traced here: 567 us
  Pallas kernels  453 us (79%)
  waiting for transfers between devices  42.9 us (7%)
  other arithmetic  21.6 us (4%)
  local copies, waits for them, and re-layouts  19.9 us (3%)
  between operations  15.2 us (3%)
  matrix products  14 us (2%)
    pallas_call x1, Pallas kernels, local(): pl.pallas_call(grads_kernel, in_specs=[hbm] * 6 + [vmem], out_specs=[hbm]...  163 us
    pallas_call x1, Pallas kernels, local(): pl.pallas_call(functools.partial(gather_kernel, ring=ring, wide=wide), in...  146 us
    pallas_call x1, Pallas kernels, local(): pl.pallas_call(functools.partial(back_kernel, heads=heads, wide=wide), gr...  53.7 us
    reduce_scatter x1, waiting for transfers between devices, local(): pieces = lax.psum_scatter(wog, 'head', scatter_dimension=0, tiled=False)  42.1 us
    pallas_call x1, Pallas kernels, local(): pl.pallas_call(blend_kernel, in_specs=[hbm, hbm, hbm, vmem, vmem], out_sp...  32.9 us
    pallas_call x1, Pallas kernels, local(): pl.pallas_call(functools.partial(scan_kernel, heads=heads, wide=wide), gr...  32.1 us
    pallas_call x1, Pallas kernels, local(): pl.pallas_call(gate_kernel, grid=grid, in_specs=[forth(wide), forth(LANES...  15.8 us
    dot_general x1, matrix products, t_dot(): lax.dot_general(a, b, (((0,), (0,)), ((), ())), preferred_element_type=F32)  14 us
  transfers between devices with their start and end apart: 2, of which 1 were waited for; matrix products, arithmetic and copies ran while one was open for 1% of the time, Pallas kernels for 9%

profile of v4, /device:TPU:8, one launch (start us, length us, event | category | flops | bytes accessed | tf_op | source)
XLA Modules:
  0.0 566.8 jit_solution(10652234361814759408)
XLA Ops:
  7.2 0.7 convert_element_type.80
  7.9 0.7 multiply_convert_fusion
  8.6 0.1 copy.45
  8.7 0.8 reshape.137
  9.5 3.5 concatenate.28
  13.0 0.1 reshape.138
  13.1 0.8 copy.46.gain_ref
  13.9 0.7 pad_maximum_fusion.dtw_ref
  14.7 145.8 %gather_project.1 = (bf16[2048,2048]{1,0:T(8,128)(2,1)}, bf16[2048,2048]{1,0:T(8,128)(2,1)}, bf16[2048,2432]{1,0:T(8,128)(2,1)}, bf16[1024,2048]{1,0:T(8,128)(2,...) custom-call(bf16[512,2048]{1,0:T(8,128)(2,1)} %bitcast.46, ...), custom_call_target="tpu_custom_call" | custom-call | flops 28991029248 | bytes 36700160 | tf_op jit(solution)/shard_map/gather_project/pallas_call | solution.py:1107
  160.5 1.2 slice.111
  161.8 0.5 reshape.140
  162.4 0.1 reshape.141
  162.5 0.1 reshape.142
  163.7 0.8 fusion.6.exp_ref
  165.1 0.6 fusion.11.cw_ref
  165.7 0.6 stack.19.rowp_ref
  166.4 0.6 broadcast_in_dim.22.cb_ref
  167.0 0.7 broadcast_in_dim.26.colp_ref
  167.7 0.6 broadcast_in_dim.23.dtb_ref
  168.3 32.1 %scan.1 = (bf16[2048,1280]{1,0:T(8,128)(2,1)}, bf16[2048,1280]{1,0:T(8,128)(2,1)}, f32[2048,128]{1,0:T(8,128)}, f32[2048,1024]{1,0:T(8,128)}, bf16[2048,1024]{1,...) custom-call(bf16[2048,1280]{1,0:T(8,128)(2,1)} %get-tuple-element.44.u_ref, ...), custom_call_target="tpu_custom_call" | custom-call | flops 12884901888 | bytes 33554432 | tf_op jit(solution)/shard_map/scan/pallas_call | solution.py:1197
  200.4 0.6 broadcast_in_dim.54.mask_ref
  201.0 32.9 %blend.1 = (f32[2048,128]{1,0:T(8,128)}, bf16[3,512,2048]{2,1,0:T(8,128)(2,1)}, bf16[8,2,64,2048]{3,2,1,0:T(8,128)(2,1)}) custom-call(bf16[2048,1024]{1,0:T(8,128)(2,1)} %get-tuple-element.49.gg_ref, bf16[1024,2048]{1,0:T(8,128)(2,1)} %get-tuple-element.50.wo_ref, bf16[2048,2048]{1,0:T(8,128)(2,1)} %get-tuple-element.51.og_ref, ...), custom_call_target="tpu_custom_call" | custom-call | flops 17179869184 | bytes 25165824 | tf_op jit(solution)/shard_map/blend/pallas_call | solution.py:1230
  234.0 15.8 %gate_back.1 = (bf16[2048,1024]{1,0:T(8,128)(2,1)}, bf16[2048,1024]{1,0:T(8,128)(2,1)}) custom-call(bf16[2048,1280]{1,0:T(8,128)(2,1)} %get-tuple-element.54.x_ref.act_ref, f32[2048,128]{1,0:T(8,128)} %get-tuple-element.55.aux_ref, bf16[2048,1024]{1,0:T(8,128)(2,1)} %get-tuple-element.46.z_ref, bf16[2048,1024]{1,0:T(8,128)(2,1)} %get-tuple-element.47.d0_ref, ...), custom_call_target="tpu_custom_call" | custom-call | flops 41943040 | bytes 29360128 | tf_op jit(solution)/shard_map/gate_back/pallas_call | solution.py:1255
  249.8 14.0 %convolution_convert_fusion = bf16[2048,1024]{1,0:T(8,128)(2,1)} fusion(bf16[2048,2048]{1,0:T(8,128)(2,1)} %get-tuple-element.58.h_ref, bf16[2048,1024]{1,0:T(8,128)(2,1)} %get-tuple-element.59.dpg_ref), kind=kOutput, calls=%fused_computation.10 | convolution fusion | flops 8592031744 | bytes 16777216 | tf_op jit(solution)/shard_map/dot_general | solution.py:34
  263.9 0.7 reduce-scatter.5.cloned.1.call-update
  264.6 0.7 copy.48.dtw_ref
  265.3 0.9 fusion.7.seg_ref
  266.2 53.7 %scan_back.1 = (bf16[2048,1408]{1,0:T(8,128)(2,1)}, f32[8,1280]{1,0:T(8,128)}, f32[512,2048]{1,0:T(8,128)}) custom-call(bf16[2048,1280]{1,0:T(8,128)(2,1)} %get-tuple-element.54.x_ref.act_ref, f32[2048,128]{1,0:T(8,128)} %get-tuple-element.55.aux_ref, bf16[2048,1024]{1,0:T(8,128)(2,1)} %get-tuple-element.60.dy_ref, f32[2048,1024]{1,0:T(8,128)} %get-tuple-element.56.y_ref, ...), custom_call_target="tpu_custom_call" | custom-call | flops 12884901888 | bytes 50331648 | tf_op jit(solution)/shard_map/scan_back/pallas_call | solution.py:1273
  320.0 0.8 convert.22
  320.8 0.8 slice_reduce_fusion.1
  321.6 0.1 reduce_sum.45
  321.8 0.1 concatenate.34
  321.9 0.7 convert_element_type.92.tiny_ref
  322.6 1.1 dynamic-slice_reduce_fusion
  323.7 42.1 %reduce-scatter.5.cloned.1.call-done = bf16[1,2,64,2048]{3,2,1,0:T(8,128)(2,1)} async-done(((bf16[8,2,64,2048]{3,2,1,0:T(8,128)(2,1)}), bf16[1,2,64,2048]{3,2,1,0:T(8,128)(2,1)}) %reduce-scatter.5.cloned.1.call-update) | async-done | bytes 524304 | tf_op jit(solution)/shard_map/reduce_scatter | solution.py:1254
  365.8 162.9 %weight_grads.1 = (f32[512,2048]{1,0:T(8,128)}, bf16[4,256,1024]{2,1,0:T(8,128)(2,1)}, bf16[4,256,1408]{2,1,0:T(8,128)(2,1)}, bf16[8,64,2048]{2,1,0:T(8,128)(2,1)}) custom-call(bf16[2048,1024]{1,0:T(8,128)(2,1)} %get-tuple-element.59.dpg_ref, bf16[2048,1408]{1,0:T(8,128)(2,1)} %get-tuple-element.65.dp_ref, bf16[2048,2432]{1,0:T(8,128)(2,1)} %get-tuple-element.48.w_ref, ...), custom_call_target="tpu_custom_call" | custom-call | flops 40802189312 | bytes 39845888 | tf_op jit(solution)/shard_map/weight_grads/pallas_call | solution.py:1302
  528.7 1.1 slice.100
  529.8 0.2 reshape.150
  530.2 0.1 fusion.12
  530.3 0.6 slice.129
  530.9 0.6 slice_reduce_fusion.2
  531.5 9.9 %w_in_finish.1 = (f32[256,8448]{1,0:T(8,128)}, f32[256,64]{1,0:T(8,128)}, f32[256,1]{1,0:T(8,128)}) custom-call(bf16[4,256,1024]{2,1,0:T(8,128)(2,1)} %get-tuple-element.70.gate_ref, bf16[4,256,1408]{2,1,0:T(8,128)(2,1)} %get-tuple-element.71.rest_ref, bf16[256,8448]{1,0:T(8,128)(2,1)} %w_ref.3, bf16[256,64]{1,0:T(8,128)(2,1)} %copy.48.dtw_ref, ...), custom_call_target="tpu_custom_call" | custom-call | flops 12976128 | bytes 17301504 | tf_op jit(solution)/shard_map/w_in_finish/pallas_call | solution.py:1363
  541.4 1.6 copy.51
  543.1 6.8 %fusion.1 = (f32[512]{0:T(512)S(1)}, f32[512]{0:T(512)S(1)}, f32[512]{0:T(512)S(1)}, f32[512,2048]{1,0:T(8,128)}) fusion(bf16[1,512,2048]{2,1,0:T(8,128)(2,1)S(1)} %copy-done, f32[512,2048]{1,0:T(8,128)} %get-tuple-element.69, bf16[8,64,2048]{2,1,0:T(8,128)(2,1)} %get-tuple-element.75, bf16[512,2048]{1,0:T(8,128)(2,1)} %wo_in_ref.1), kind=kLoop, calls=%fused_computation.5 | loop fusion | flops 9435648 | bytes 14686208 | tf_op jit(solution)/shard_map/reduce_sum | solution.py:1378
  549.9 0.6 convert_divide_fusion
  550.7 0.5 slice_bitcast_fusion.3
  551.2 0.7 reduce.2
  551.9 7.9 %fusion.4 = (f32[1,512,2048]{2,1,0:T(8,128)}, bf16[1,512,2048]{2,1,0:T(8,128)(2,1)}) fusion(f32[512,2048]{1,0:T(8,128)} %get-tuple-element.69, f32[512]{0:T(512)S(1)} %multiply_multiply_fusion, bf16[1,512,2048]{2,1,0:T(8,128)(2,1)} %param.15, bf16[1,512,2048]{2,1,0:T(8,128)(2,1)S(1)} %copy-done, f32[512,2048]{1,0:T(8,128)} %get-tuple-element.64, ...), kind=kLoop, calls=%fused_computation.8 | loop fusion | flops 8388608 | bytes 18878464 | tf_op jit(solution)/shard_map/broadcast_in_dim | solution.py:1380
  (64 shorter events, 1.8 us)
Async XLA Ops:
  7.2 316.5 %reduce-scatter.3.cloned.1.call-start = ((), (), s32[]{:S(2)}) async-start(), calls=%async_computation.2 | async-start | bytes 4718592 | tf_op jit(solution)/shard_map/reduce_scatter | solution.py:1270
  263.8 0.8 copy-start.3
  263.8 102.0 %reduce-scatter.5.cloned.1.call-start = ((), (), s32[]{:S(2)}) async-start(), calls=%async_computation.3 | async-start | bytes 4718592 | tf_op jit(solution)/shard_map/reduce_scatter | solution.py:1254
  530.0 11.4 %copy-start.1 = (f32[4,6448]{1,0:T(4,128)}, f32[4,6448]{1,0:T(4,128)S(1)}, u32[]{:S(2)}) copy-start(f32[4,6448]{1,0:T(4,128)S(1)} %slice_convert_fusion) | copy-start | bytes 309508
  531.5 11.6 %copy-start = (bf16[1,512,2048]{2,1,0:T(8,128)(2,1)S(1)}, bf16[1,512,2048]{2,1,0:T(8,128)(2,1)}, u32[]{:S(2)}) copy-start(bf16[1,512,2048]{2,1,0:T(8,128)(2,1)} %param.13) | copy-start | bytes 6291460
  543.1 6.8 %copy-start.4 = (bf16[512]{0:T(512)(128)(2,1)S(1)}, bf16[512]{0:T(512)(128)(2,1)}, u32[]{:S(2)}) copy-start(bf16[512]{0:T(512)(128)(2,1)} %param.24) | copy-start | bytes 3076
  543.1 7.4 %slice-start = ((f32[4,6448]{1,0:T(4,128)}), f32[4,48]{1,0:T(4,128)S(1)}, s32[]{:S(2)}) async-start(f32[4,6448]{1,0:T(4,128)} %copy-done.1), calls=%async_computation.4 | async-start | bytes 4096 | tf_op jit(solution)/shard_map/slice | solution.py:1387
  543.1 8.2 %copy-start.2 = (f32[256,1]{1,0:T(8,128)S(1)}, f32[256,1]{1,0:T(8,128)}, u32[]{:S(2)}) copy-start(f32[256,1]{1,0:T(8,128)} %get-tuple-element.72) | copy-start | bytes 3076
Sparse Core Ops, SparseCore 0:
  264.0 51.3 reduce-scatter.2
  317.6 48.1 reduce-scatter.4

commit v5 on v4

--- a/solution.py
+++ b/solution.py
@@ -446,8 +446,9 @@
     last = cum_e[rows - 1 : rows, :]
     tail = jnp.exp(last - cum_e)
     state[...] = jnp.exp(last) * st + t_dot(b, (xdt * tail).astype(BF16))
-    y_ref[...] = y
-    ssd = (y + rowp_ref[1:2, :] * x32).astype(BF16).astype(F32)
+    y16 = y.astype(BF16)
+    y_ref[...] = y16
+    ssd = (y16.astype(F32) + rowp_ref[1:2, :] * x32).astype(BF16).astype(F32)
     z = z_ref[...].astype(F32)
     g = ssd * (z * sigmoid(z))
     gg = g * rowp_ref[2:3, :]
@@ -467,35 +468,156 @@
     return dot(hi, seg) + dot(mid, seg) + dot(low, seg)
 
 
-def blend_kernel(
-    gg_ref, wo_ref, og_ref, sums_ref, mask_ref,
-    stat_ref, part_ref, wog_ref,
-    ggv, wov, ogv, far_p, y_p, x_p, own_p, far_a, far_b, sv, staged,
-    load_sem, d_send, d_recv, s_send, s_recv, out_sem, w_sem,
+def line_sum(own, z_u, z_d, sems, r, last, to_up, to_down, join, closing):
+    zu_send, zu_recv, zd_send, zd_recv = sems
+
+    def up_copy(t):
+        return remote(own.at[t], z_u.at[t - 1], zu_send.at[t], zu_recv.at[t], to_up)
+
+    def down_copy(t):
+        return remote(own.at[t], z_d.at[t], zd_send.at[t], zd_recv.at[t], to_down)
+
+    def up_add(t):
+        up_copy(t).wait_recv()
+        join(t, z_u.at[t - 1])
+
+    def down_add(t):
+        down_copy(t).wait_recv()
+        join(t, z_d.at[t])
+
+    def sent_later(t, there, make):
+        closing.append(lambda: pl.when(there)(lambda: make(t).wait_send()))
+
+    def pass_on(t, there, add, make):
+        @pl.when(there)
+        def _():
+            add(t)
+            make(t).start()
+
+        sent_later(t, there, make)
+
+    def follow(t, there, make, before):
+        @pl.when(there)
+        def _():
+            make(before).wait_send()
+            make(t).start()
+
+    def start():
+        pl.when(r == 0)(lambda: up_copy(last).start())
+        pl.when(r == last)(lambda: down_copy(0).start())
+
+    def second():
+        follow(2, r == 0, up_copy, last)
+        follow(1, r == last, down_copy, 0)
+        pass_on(last, r == 1, up_add, up_copy)
+        pass_on(0, r == 2, down_add, down_copy)
+
+    def across():
+        pass_on(last, r == 2, up_add, up_copy)
+        pass_on(0, r == 1, down_add, down_copy)
+
+    def third():
+        follow(1, r == 0, up_copy, 2)
+        follow(2, r == last, down_copy, 1)
+        pass_on(2, r == 1, up_add, up_copy)
+        pass_on(1, r == 2, down_add, down_copy)
+        sent_later(1, r == 0, up_copy)
+        sent_later(2, r == last, down_copy)
+
+    def final():
+        pl.when(r > 0)(lambda: up_add(r))
+        pl.when(r < last)(lambda: down_add(r))
+
+    return start, second, across, third, final
+
+
+def mid_kernel(
+    gg_ref, wo_ref, og_ref, h_ref, act_ref, aux_ref, z_ref, d0_ref, y_ref, sums_ref, mask_ref, rowp_ref,
+    br_ref, wog_ref, dy_ref, dpg_ref, gate_ref,
+    stat_v, ggv, wov, ogv, far_p, y_p, x_p, own_p, far_a, far_b, y_f, x_f, sv,
+    ow, other, other_in, z_u, z_d, part_s, xin, zin, din, yin, ain, dyo, hb, rows_s,
+    load_sem, d_send, d_recv, s_send, s_recv, c_send, c_recv, zu_send, zu_recv, zd_send, zd_recv,
+    in_sem, dy_sem, hb_sem, rows_sem, out_sem, *, ring,
 ):
     s = lax.axis_index("seq")
+    tokens, wide = ggv.shape
+    width = wov.shape[1]
     q = far_p.shape[0]
     half = q // 2
     rows = min(CHUNK, q)
+    tile = 256
     x_peer = s + 1 - 2 * lax.rem(s, 2)
     y_peer = lax.rem(s + 2, 4)
     far = 3 - s
     to_x, to_y, to_far = {"seq": x_peer}, {"seq": y_peer}, {"seq": far}
-    loads = [
-        pltpu.make_async_copy(src, dst, load_sem.at[i])
-        for i, (src, dst) in enumerate(((gg_ref, ggv), (wo_ref, wov), (og_ref, ogv)))
-    ]
-    for copy in loads:
-        copy.start()
+    load_gg = pltpu.make_async_copy(gg_ref, ggv, load_sem.at[0])
+    load_wo = pltpu.make_async_copy(wo_ref, wov, load_sem.at[1])
+    cut = ogv.shape[1]
+
+    def load_og(d):
+        return pltpu.make_async_copy(og_ref.at[:, d * cut : (d + 1) * cut], ogv, load_sem.at[2])
+
+    def load_chunk(i):
+        at = pl.ds(pl.multiple_of(i * rows, 16), rows)
+        slot = lax.rem(i, 2)
+        pairs = ((act_ref.at[at, :wide], xin), (z_ref.at[at, :], zin), (d0_ref.at[at, :], din), (y_ref.at[at, :], yin), (aux_ref.at[at, :], ain))
+        return [pltpu.make_async_copy(src, dst.at[slot], in_sem.at[slot, k]) for k, (src, dst) in enumerate(pairs)]
+
+    def load_h(i):
+        slot = lax.rem(i, 2)
+        return pltpu.make_async_copy(h_ref.at[:, pl.ds(pl.multiple_of(i * tile, tile), tile)], hb.at[slot], hb_sem.at[slot])
+
+    load_gg.start()
+    load_wo.start()
+    load_og(0).start()
+    peers = [to_x, to_y, to_far]
+    extra = []
+    closing = []
+    if ring:
+        h = lax.axis_index("head")
+        owners = lax.axis_size("head")
+        last = owners // 2 - 1
+        core = lax.rem(h, 2)
+        r = h // 2
+        to_sib = {"head": h + 1 - 2 * core}
+        to_up, to_down = {"head": lax.rem(h + 2, owners)}, {"head": lax.rem(h + owners - 2, owners)}
+        peers.append(to_sib)
+        extra = [(r < last, to_up), (r > 0, to_down)]
+
+        def join(t, more):
+            ow[t] = (ow[t].astype(F32) + more[...].astype(F32)).astype(BF16)
+
+        start, second, across, third, final = line_sum(
+            ow, z_u, z_d, (zu_send, zu_recv, zd_send, zd_recv), r, last, to_up, to_down, join, closing
+        )
     sv[s] = sums_ref[...]
-    greet([to_x, to_y, to_far])
+    greet(peers, extra)
     sums = [
         remote(sums_ref, sv.at[s], s_send.at[i], s_recv.at[i], peer) for i, peer in enumerate((to_x, to_y, to_far))
     ]
     for copy in sums:
         copy.start()
-    loads[0].wait()
-    loads[1].wait()
+    for i in (0, 1):
+        for copy in load_chunk(i):
+            copy.start()
+    load_h(0).start()
+    load_h(1).start()
+    load_gg.wait()
+    for copy in sums:
+        copy.wait_recv()
+    total = (sv[0] + sv[1]) + (sv[2] + sv[3])
+    r1 = lax.rsqrt(total[0:1] / DI + EPS)
+    r1m = r1 * mask_ref[0:1]
+    coef = r1m * r1 * r1 * total[1:2] / DI
+    sub = lax.broadcasted_iota(jnp.int32, (LANES, tokens), 0)
+    stat_v[...] = jnp.where(sub == 0, r1m, jnp.where(sub == 1, coef, 0.0)).T
+
+    @pl.loop(0, tokens // rows)
+    def _(j):
+        at = pl.ds(pl.multiple_of(j * rows, 16), rows)
+        ggv[at, :] = (ggv[at, :].astype(F32) * stat_v[at, 0:1]).astype(BF16)
+
+    load_wo.wait()
 
     def part(block, out):
         @pl.loop(0, q // rows)
@@ -504,115 +626,190 @@
             to = pl.ds(pl.multiple_of(j * rows, 16), rows)
             out[to, :] = dot(ggv[at, :], wov[...]).astype(BF16)
 
+    def d_copy(src, dst, i, target):
+        copy = remote(src, dst, d_send.at[i], d_recv.at[i], target)
+        copy.start()
+        return copy
+
     part(far, far_p)
-    d0 = remote(far_p.at[:half], far_a, d_send.at[0], d_recv.at[0], to_x)
-    d1 = remote(far_p.at[half:], far_b, d_send.at[1], d_recv.at[1], to_y)
-    d0.start()
-    d1.start()
+    d0 = d_copy(far_p.at[:half], far_a, 0, to_x)
+    d1 = d_copy(far_p.at[half:], far_b, 1, to_y)
     part(y_peer, y_p)
+    d2 = d_copy(y_p.at[half:], y_f.at[half:], 2, to_y)
     part(x_peer, x_p)
+    d3 = d_copy(x_p.at[:half], x_f.at[:half], 3, to_x)
     part(s, own_p)
-    own_out = pltpu.make_async_copy(own_p, part_ref.at[2], out_sem.at[2])
-    own_out.start()
-
-    for copy in sums:
-        copy.wait_recv()
-    total = (sv[0] + sv[1]) + (sv[2] + sv[3])
-    r1 = lax.rsqrt(total[0:1] / DI + EPS)
-    r1m = r1 * mask_ref[0:1]
-    coef = r1m * r1 * r1 * total[1:2] / DI
-    sub = lax.broadcasted_iota(jnp.int32, (LANES, r1.shape[1]), 0)
-    stat = jnp.where(sub == 0, r1m, jnp.where(sub == 1, coef, 0.0)).T
-    stat_ref[...] = stat
-
-    @pl.loop(0, ggv.shape[0] // rows)
-    def _(j):
-        at = pl.ds(pl.multiple_of(j * rows, 16), rows)
-        ggv[at, :] = (ggv[at, :].astype(F32) * stat_ref[at, 0:1]).astype(BF16)
-
-    loads[2].wait()
-    tile = 256
-    ring = len(wog_ref.shape) == 4
-
-    def w_out(m):
-        slot = lax.rem(m, 2)
-        if ring:
-            per = tile // wog_ref.shape[2]
-            groups = wov.shape[0] // 2 // tile
-            to = wog_ref.at[pl.ds(lax.rem(m, groups) * per, per), m // groups]
-            src = staged.at[slot].reshape(per, wog_ref.shape[2], wog_ref.shape[3])
-        else:
-            to = wog_ref.at[pl.ds(pl.multiple_of(m * tile, tile), tile), :]
-            src = staged.at[slot]
-        return pltpu.make_async_copy(src, to, w_sem.at[slot])
-
-    count = wov.shape[0] // tile
-
-    @pl.loop(0, count)
-    def _(m):
-        @pl.when(m >= 2)
-        def _():
-            w_out(m - 2).wait()
-
-        at = pl.ds(pl.multiple_of(m * tile, tile), tile)
-        staged[lax.rem(m, 2)] = t_dot(ggv[:, at], ogv[...]).astype(BF16)
-        w_out(m).start()
-
+
+    def w_rows(d):
+        to = slice(d * cut, (d + 1) * cut)
+
+        @pl.loop(0, wide // tile)
+        def _(m):
+            at = pl.ds(pl.multiple_of(m * tile, tile), tile)
+            got = t_dot(ggv[:, at], ogv[...]).astype(BF16)
+            if ring:
+                piece = ow.shape[2]
+                chips = tile // (2 * piece)
+                groups = wide // 2 // tile
+                part_s[...] = got.reshape(part_s.shape)
+                first = pl.ds(lax.rem(m, groups) * chips, chips)
+                ow[first, m // groups, :, to] = part_s[:, core]
+                other[first, m // groups, :, to] = part_s[:, 1 - core]
+            else:
+                rows_s[0, :, : got.shape[1]] = got
+                copy = pltpu.make_async_copy(rows_s.at[0], wog_ref.at[at, to], out_sem.at[0])
+                copy.start()
+                copy.wait()
+
+    load_og(0).wait()
+    w_rows(0)
+    load_og(1).start()
+    load_og(1).wait()
+    w_rows(1)
+    if ring:
+        swap = remote(other, other_in, c_send.at[0], c_recv.at[0], to_sib)
+        swap.start()
+        swap.wait_recv()
+
+        @pl.loop(0, 4)
+        def _(t):
+            join(t, other_in.at[t])
+
+        start()
     d0.wait_recv()
     y_p[:half, :] = (y_p[:half, :].astype(F32) + far_a[...].astype(F32)).astype(BF16)
-    y_out = pltpu.make_async_copy(y_p, part_ref.at[0], out_sem.at[0])
-    y_out.start()
+    d4 = d_copy(y_p.at[:half], y_f.at[:half], 4, to_y)
     d1.wait_recv()
     x_p[half:, :] = (x_p[half:, :].astype(F32) + far_b[...].astype(F32)).astype(BF16)
-    x_out = pltpu.make_async_copy(x_p, part_ref.at[1], out_sem.at[1])
-    x_out.start()
-    w_out(count - 2).wait()
-    w_out(count - 1).wait()
-    for copy in (own_out, y_out, x_out):
-        copy.wait()
-    for copy in sums + [d0, d1]:
+    d5 = d_copy(x_p.at[half:], x_f.at[half:], 5, to_x)
+
+    def dy_out(i):
+        at = pl.ds(pl.multiple_of(i * rows, 16), rows)
+        return pltpu.make_async_copy(dyo.at[lax.rem(i, 2)], dy_ref.at[at, :], dy_sem.at[lax.rem(i, 2)])
+
+    chunks = tokens // rows
+
+    def gate_chunk(i):
+        slot = lax.rem(i, 2)
+        at = pl.ds(pl.multiple_of(i * rows, 16), rows)
+        for copy in load_chunk(i):
+            copy.wait()
+        r0 = ain[slot, :, LANES - 1 : LANES]
+        ssd = (yin[slot].astype(F32) + rowp_ref[1:2, :] * xin[slot].astype(F32)).astype(BF16).astype(F32)
+        z = zin[slot].astype(F32)
+        sig = sigmoid(z)
+        sz = z * sig
+        d_gated = (stat_v[at, 0:1] * rowp_ref[2:3, :]) * din[slot].astype(F32) - (ssd * sz) * stat_v[at, 1:2]
+
+        @pl.when(i >= 2)
+        def _():
+            dy_out(i - 2).wait()
+
+        dyo[slot] = (d_gated * sz).astype(BF16)
+        dy_out(i).start()
+        ggv[at, :] = (r0 * (d_gated * ssd * (sig * (1.0 + z * (1.0 - sig))))).astype(BF16)
+
+        @pl.when(i + 2 < chunks)
+        def _():
+            for copy in load_chunk(i + 2):
+                copy.start()
+
+    pl.loop(0, chunks - 1)(gate_chunk)
+    if ring:
+        second()
+    pl.loop(chunks - 1, chunks)(gate_chunk)
+    dpg_out = pltpu.make_async_copy(ggv, dpg_ref, out_sem.at[1])
+    dpg_out.start()
+
+    def rows_out(i):
+        slot = lax.rem(i, 2)
+        at = pl.ds(pl.multiple_of(i * tile, tile), tile)
+        return pltpu.make_async_copy(rows_s.at[slot], gate_ref.at[at, :], rows_sem.at[slot])
+
+    blocks = width // tile
+
+    def gate_rows(i):
+        slot = lax.rem(i, 2)
+        load_h(i).wait()
+        got = t_dot(hb[slot], ggv[...]).astype(BF16)
+
+        @pl.when(i >= 2)
+        def _():
+            rows_out(i - 2).wait()
+
+        rows_s[slot] = got
+        rows_out(i).start()
+
+        @pl.when(i + 2 < blocks)
+        def _():
+            load_h(i + 2).start()
+
+    pl.loop(0, blocks // 2)(gate_rows)
+    if ring:
+        across()
+        third()
+    pl.loop(blocks // 2, blocks)(gate_rows)
+    if ring:
+        final()
+        wog_out = pltpu.make_async_copy(ow.at[r], wog_ref, out_sem.at[0])
+        wog_out.start()
+    for copy in (d2, d3, d4, d5):
+        copy.wait_recv()
+    own_p[...] = (own_p[...].astype(F32) + y_f[...].astype(F32) + x_f[...].astype(F32)).astype(BF16)
+    br_out = pltpu.make_async_copy(own_p, br_ref, out_sem.at[2])
+    br_out.start()
+    for i in (chunks - 2, chunks - 1):
+        dy_out(i).wait()
+    for i in (blocks - 2, blocks - 1):
+        rows_out(i).wait()
+    dpg_out.wait()
+    br_out.wait()
+    for copy in sums + [d0, d1, d2, d3, d4, d5]:
         copy.wait_send()
-
-
-def gate_kernel(x_ref, aux_ref, z_ref, d0_ref, y_ref, stat_ref, rowp_ref, dy_ref, dpg_ref):
-    stat = stat_ref[...]
-    r1m = stat[:, 0:1]
-    coef = stat[:, 1:2]
-    r0 = aux_ref[:, LANES - 1 : LANES]
-    ssd = (y_ref[...] + rowp_ref[1:2, :] * x_ref[...].astype(F32)).astype(BF16).astype(F32)
-    z = z_ref[...].astype(F32)
-    sig = sigmoid(z)
-    sz = z * sig
-    d_gated = (r1m * rowp_ref[2:3, :]) * d0_ref[...].astype(F32) - (ssd * sz) * coef
-    dy_ref[...] = (d_gated * sz).astype(BF16)
-    dpg_ref[...] = (r0 * (d_gated * ssd * (sig * (1.0 + z * (1.0 - sig))))).astype(BF16)
+    if ring:
+        wog_out.wait()
+        swap.wait_send()
+    for finish in closing:
+        finish()
 
 
 def back_kernel(
-    act_ref, aux_ref, dy_ref, y_ref, st_ref, slope_ref, u_ref, part_ref,
+    act_ref, aux_ref, dy_ref, y_ref, st_ref, slope_ref, u_ref, piece_ref,
     exp_ref, seg_ref, rowp_ref, colp_ref, cw_ref,
-    dp_ref, sm_ref, br_ref, adj, ext, own_b, y_f, x_f, br_o,
-    b_send, b_recv, b_load, *, heads, wide,
+    dp_ref, sm_ref, all_ref, adj, ext, b_send, b_recv, b_load, *, heads, wide, ring,
 ):
     step = pl.program_id(0)
     steps = pl.num_programs(0)
     rows = act_ref.shape[0]
     chans = u_ref.shape[1]
 
-    s = lax.axis_index("seq")
-    x_peer = s + 1 - 2 * lax.rem(s, 2)
-    y_peer = lax.rem(s + 2, 4)
-    to_x, to_y = {"seq": x_peer}, {"seq": y_peer}
-    out_y = remote(part_ref.at[0], y_f, b_send.at[0], b_recv.at[0], to_y)
-    out_x = remote(part_ref.at[1], x_f, b_send.at[1], b_recv.at[1], to_x)
-    own_load = pltpu.make_async_copy(part_ref.at[2], own_b, b_load.at[0])
-
-    @pl.when(step == 0)
-    def _():
-        greet([to_x, to_y])
-        out_y.start()
-        out_x.start()
-        own_load.start()
+    if ring:
+        s = lax.axis_index("seq")
+        x_peer = s + 1 - 2 * lax.rem(s, 2)
+        y_peer = lax.rem(s + 2, 4)
+        to_x, to_y = {"seq": x_peer}, {"seq": y_peer}
+        from_x, from_y = all_ref.at[x_peer, 0], all_ref.at[y_peer, 1]
+        moves = [
+            remote(piece_ref, all_ref.at[s], b_send.at[0], b_recv.at[0], to_x),
+            remote(piece_ref, all_ref.at[s], b_send.at[1], b_recv.at[1], to_y),
+            remote(from_x, from_x, b_send.at[2], b_recv.at[2], to_y),
+            remote(from_y, from_y, b_send.at[3], b_recv.at[3], to_x),
+        ]
+        own_piece = pltpu.make_async_copy(piece_ref, all_ref.at[s], b_load.at[0])
+
+        @pl.when(step == 0)
+        def _():
+            greet([to_x, to_y])
+            moves[0].start()
+            moves[1].start()
+            own_piece.start()
+
+        @pl.when(step == 3)
+        def _():
+            moves[0].wait_recv()
+            moves[2].start()
+            moves[1].wait_recv()
+            moves[3].start()
 
     @pl.when(step == 0)
     def _():
@@ -627,7 +824,7 @@
     aux = aux_ref[...]
     r0 = aux[:, LANES - 1 : LANES]
     skip_e = rowp_ref[1:2, :]
-    y = y_ref[...]
+    y = y_ref[...].astype(F32)
     dy16 = dy_ref[...]
     dy = dy16.astype(F32)
 
@@ -723,25 +920,22 @@
     sm_ref[6:7, :LANES] += jnp.sum(d_pre, axis=0, keepdims=True)
     sm_ref[7:8, :LANES] += jnp.sum(dt * decay_grad, axis=0, keepdims=True)
 
-    @pl.when(step == steps - 1)
-    def _():
-        own_load.wait()
-        out_y.wait_recv()
-        out_x.wait_recv()
-        br_o[...] = own_b[...].astype(F32) + y_f[...].astype(F32) + x_f[...].astype(F32)
-        last_copy = pltpu.make_async_copy(br_o, br_ref, b_load.at[1])
-        last_copy.start()
-        for copy in (out_y, out_x):
-            copy.wait_send()
-        last_copy.wait()
+    if ring:
+        @pl.when(step == steps - 1)
+        def _():
+            moves[2].wait_recv()
+            moves[3].wait_recv()
+            for copy in moves:
+                copy.wait_send()
+            own_piece.wait()
 
 
 def grads_kernel(
     dpg_ref, dp_ref, w_ref, h_ref, gate_ref, piece_ref, tiny_ref,
     dn_ref, wing_ref, win_ref, wout_ref,
-    dpv, wv, hb, far_p, y_p, x_p, far_a, far_b, y_f, x_f, dn_o, sib_s, mine_s, own_s, z_u, z_d, pv,
+    dpv, wv, hb, far_p, y_p, x_p, far_a, far_b, y_f, x_f, sib_s, mine_s, own_s, z_u, z_d,
     load_sem, hb_sem, d_send, d_recv, s_send, s_recv, zu_send, zu_recv, zd_send, zd_recv,
-    g_send, g_recv, k_send, k_recv, p_send, p_recv, w_send, w_recv, out_sem,
+    g_send, g_recv, k_send, k_recv, p_send, p_recv, out_sem,
 ):
     s = lax.axis_index("seq")
     h = lax.axis_index("head")
@@ -815,11 +1009,6 @@
     k_sems = (k_send, k_recv)
     k0 = push(gate_ref, wing_ref.at[s], k_sems, 0, to_x)
     k1 = push(gate_ref, wing_ref.at[s], k_sems, 1, to_y)
-    w_sems = (w_send, w_recv)
-    own_piece = pltpu.make_async_copy(piece_ref, pv.at[s], load_sem.at[2])
-    own_piece.start()
-    w0 = push(piece_ref, pv.at[s], w_sems, 0, to_x)
-    w1 = push(piece_ref, pv.at[s], w_sems, 1, to_y)
     tile = 256
 
     def part(block, out):
@@ -871,101 +1060,52 @@
         for lo, hi in spans:
             own_s[t, :, lo:hi] = (own_s[t, :, lo:hi].astype(F32) + extra[:, lo:hi].astype(F32)).astype(BF16)
 
-    def up_copy(t):
-        return remote(own_s.at[t], z_u.at[t - 1], zu_send.at[t], zu_recv.at[t], to_up)
-
-    def down_copy(t):
-        return remote(own_s.at[t], z_d.at[t], zd_send.at[t], zd_recv.at[t], to_down)
-
-    def up_add(t):
-        up_copy(t).wait_recv()
-        join(t, z_u.at[t - 1])
-
-    def down_add(t):
-        down_copy(t).wait_recv()
-        join(t, z_d.at[t])
-
-    def pass_on(t, there, add, make):
-        pl.when(there)(functools.partial(add, t))
-        launch(there, lambda: make(t))
-
-    def follow(t, there, make, before):
-        @pl.when(there)
-        def _():
-            make(before).wait_send()
-            make(t).start()
-
-    def finish_later(t, there, make):
-        def finish():
-            @pl.when(there)
-            def _():
-                make(t).wait_send()
-
-        closing.append(finish)
+    start, second, across, third, final = line_sum(
+        own_s, z_u, z_d, (zu_send, zu_recv, zd_send, zd_recv), r, last, to_up, to_down, join, closing
+    )
 
     load_dp.wait()
-    pl.loop(0, 2)(rows_of)
-
-    @pl.when(r == 0)
-    def _():
-        up_copy(last).start()
-
-    @pl.when(r == last)
-    def _():
-        down_copy(0).start()
-
     load_g.wait()
     load_w.wait()
     part(far, far_p)
     d0 = push(far_p.at[:half], far_a, d_sems, 0, to_x)
     d1 = push(far_p.at[half:], far_b, d_sems, 1, to_y)
+    pl.loop(0, 2)(rows_of)
+    start()
     k0.wait_recv()
     gate_a = wing_ref.at[x_peer, : n // 2]
     k2 = push(gate_a, gate_a, k_sems, 2, to_y)
     k1.wait_recv()
     gate_b = wing_ref.at[y_peer, n // 2 :]
     k3 = push(gate_b, gate_b, k_sems, 3, to_x)
-    own_piece.wait()
-    w0.wait_recv()
-    piece_a = pv.at[x_peer, 0]
-    w2 = push(piece_a, piece_a, w_sems, 2, to_y)
-    w1.wait_recv()
-    piece_b = pv.at[y_peer, 1]
-    w3 = push(piece_b, piece_b, w_sems, 3, to_x)
     pl.loop(2, 4)(rows_of)
-
-    follow(2, r == 0, up_copy, last)
-    follow(1, r == last, down_copy, 0)
-    pass_on(last, (r > 0) & above, up_add, up_copy)
-    pass_on(0, (r < last) & below, down_add, down_copy)
     part(y_peer, y_p)
+    d2 = push(y_p.at[half:], y_f.at[half:], d_sems, 2, to_y)
+    second()
     part(x_peer, x_p)
-    follow(1, r == 0, up_copy, 2)
-    follow(2, r == last, down_copy, 1)
-    pass_on(2, r == 1, up_add, up_copy)
-    pass_on(1, r == 2, down_add, down_copy)
-    finish_later(1, r == 0, up_copy)
-    finish_later(2, r == last, down_copy)
+    d3 = push(x_p.at[:half], x_f.at[:half], d_sems, 3, to_x)
     d0.wait_recv()
     add_to(y_p, slice(0, half), far_a[...])
-    d2 = push(y_p, y_f, d_sems, 2, to_y)
+    d4 = push(y_p.at[:half], y_f.at[:half], d_sems, 4, to_y)
     d1.wait_recv()
     add_to(x_p, slice(half, q), far_b[...])
-    d3 = push(x_p, x_f, d_sems, 3, to_x)
-    pl.when(r > 0)(lambda: up_add(r))
-    pl.when(r < last)(lambda: down_add(r))
+    d5 = push(x_p.at[half:], x_f.at[half:], d_sems, 5, to_x)
+    across()
+    third()
+    d0.wait_send()
+    d1.wait_send()
+    part(s, far_p)
+    final()
 
     red = own_s.at[r]
     g0 = push(red, win_ref.at[s], g_sems, 0, to_x)
     g1 = push(red, win_ref.at[s], g_sems, 1, to_y)
     own_win = pltpu.make_async_copy(red, win_ref.at[s], load_sem.at[3])
     own_win.start()
-    w2.wait_recv()
-    w3.wait_recv()
     per = owners // 4
 
     def piece_of(head):
-        return pv.at[head // per, lax.rem(head, per)]
+        return piece_ref.at[head // per, lax.rem(head, per)]
 
     pieces = []
     for k, peer in enumerate(to_heads):
@@ -980,30 +1120,12 @@
     part_b = win_ref.at[y_peer, n // 2 :]
     g3 = push(part_b, part_b, g_sems, 3, to_x)
 
-    d2.wait_recv()
-    d3.wait_recv()
-
-    def dn_out(j):
-        to = pl.ds(pl.multiple_of(j * tile, tile), tile)
-        return pltpu.make_async_copy(dn_o.at[lax.rem(j, 2)], dn_ref.at[:, to], out_sem.at[lax.rem(j, 2)])
-
-    own_at = pl.ds(pl.multiple_of(s * q, 16), q)
-    tiles_n = wv.shape[0] // tile
-
-    @pl.loop(0, tiles_n)
-    def _(j):
-        to = pl.ds(pl.multiple_of(j * tile, tile), tile)
-        got = dot_t(dpv[own_at, :], wv[to, :])
-
-        @pl.when(j > 1)
-        def _():
-            dn_out(j - 2).wait()
-
-        dn_o[lax.rem(j, 2)] = got + y_f[:, to].astype(F32) + x_f[:, to].astype(F32)
-        dn_out(j).start()
-
-    dn_out(tiles_n - 2).wait()
-    dn_out(tiles_n - 1).wait()
+    for copy in (d2, d3, d4, d5):
+        copy.wait_recv()
+    far_p[...] = (far_p[...].astype(F32) + y_f[...].astype(F32) + x_f[...].astype(F32)).astype(BF16)
+    dn_out = pltpu.make_async_copy(far_p, dn_ref, out_sem.at[0])
+    dn_out.start()
+    dn_out.wait()
     own_win.wait()
     own_gate.wait()
     own_piece.wait()
@@ -1016,13 +1138,28 @@
     for i in (2, 3):
         swap(i).wait_send()
     for copy in sent:
-        copy.wait_send()
+        if copy is not d0 and copy is not d1:
+            copy.wait_send()
     for finish in closing:
         finish()
 
 
-def finish_kernel(gate_ref, rest_ref, w_ref, dtw_ref, gain_ref, win_ref, wdt_ref, norm_ref, *, heads, wide):
+def finish_kernel(
+    gate_ref, rest_ref, w_ref, dtw_ref, gain_ref, wog_ref, wo_ref, ggain_ref, hid_ref, og_ref, dn_ref, br_ref,
+    win_ref, wdt_ref, norm_ref, wout_ref, gg_ref, blk_ref, hg_ref, *, heads, wide,
+):
     ranks = gate_ref.shape[0]
+    wog = wog_ref[...].astype(F32)
+    wout_ref[...] = wog
+    gg_ref[...] = jnp.sum(wog * wo_ref[...].astype(F32), axis=1, keepdims=True) / ggain_ref[...]
+    h32 = hid_ref[...].astype(F32)
+    blk_ref[...] = (h32 + br_ref[...].astype(F32)).astype(BF16)
+    dn = dn_ref[...].astype(F32)
+    count = h32.shape[1]
+    r0 = lax.rsqrt(jnp.sum(h32 * h32, axis=1, keepdims=True) / count + EPS)
+    mixed = jnp.sum(dn * h32, axis=1, keepdims=True) / count
+    hg_ref[...] = og_ref[...].astype(F32) + dn - h32 * (r0 * r0 * mixed)
+
     gain = gain_ref[...]
     norm = None
 
@@ -1210,7 +1347,7 @@
             sds((tokens, chans), BF16),
             sds((tokens, chans), BF16),
             sds((tokens, LANES), F32),
-            sds((tokens, wide), F32),
+            sds((tokens, wide), BF16),
             sds((tokens, wide), BF16),
             sds((steps, STATE, wide), F32),
             sds((8, tokens), F32),
@@ -1226,52 +1363,60 @@
     mask = (jnp.arange(tokens, dtype=jnp.int32) < lengths[0]).astype(F32)
     n_own = DI // owners
     piece = n_own // owners
-    wog_shape = (owners, owners // ranks, piece, width) if ring else (wide, width)
-    stat2, partial, wog = pl.pallas_call(
-        blend_kernel,
-        in_specs=[hbm, hbm, hbm, vmem, vmem],
-        out_specs=[vmem, hbm, hbm],
-        out_shape=[sds((tokens, LANES), F32), sds((3, local_len, width), BF16), sds(wog_shape, BF16)],
+    per = owners // ranks
+    wog_shape = (per, piece, width) if ring else (wide, width)
+    line_shape = (4, per, piece, width) if ring else (1, 1, 16, LANES)
+    in_chunk = min(CHUNK, local_len)
+    branch, wog, dy, dpg, wig_gate = pl.pallas_call(
+        functools.partial(mid_kernel, ring=ring),
+        in_specs=[hbm] * 9 + [vmem] * 3,
+        out_specs=[hbm] * 5,
+        out_shape=[
+            sds((local_len, width), BF16),
+            sds(wog_shape, BF16),
+            sds((tokens, wide), BF16),
+            sds((tokens, wide), BF16),
+            sds((width, wide), BF16),
+        ],
         scratch_shapes=[
+            pltpu.VMEM((tokens, LANES), F32),
             pltpu.VMEM((tokens, wide), BF16),
             pltpu.VMEM((wide, width), BF16),
-            pltpu.VMEM((tokens, width), BF16),
+            pltpu.VMEM((tokens, width // 2), BF16),
         ]
         + [pltpu.VMEM((local_len, width), BF16)] * 4
         + [pltpu.VMEM((local_len // 2, width), BF16)] * 2
-        + [pltpu.VMEM((ranks, 8, tokens), F32), pltpu.VMEM((2, 256, width), BF16)]
-        + [dma(3), dma(2), dma(2), dma(3), dma(3), dma(3), dma(2)],
+        + [pltpu.VMEM((local_len, width), BF16)] * 2
+        + [pltpu.VMEM((ranks, 8, tokens), F32)]
+        + [pltpu.VMEM(line_shape, BF16)] * 3
+        + [pltpu.VMEM((3,) + line_shape[1:], BF16)] * 2
+        + [pltpu.VMEM((256 // (2 * piece), 2, piece, width // 2) if ring else (16, LANES), BF16)]
+        + [pltpu.VMEM((2, in_chunk, wide), BF16)] * 4
+        + [
+            pltpu.VMEM((2, in_chunk, LANES), F32),
+            pltpu.VMEM((2, in_chunk, wide), BF16),
+            pltpu.VMEM((2, tokens, 256), BF16),
+            pltpu.VMEM((2, 256, wide), BF16),
+        ]
+        + [dma(3)]
+        + [dma(6)] * 2
+        + [dma(3)] * 2
+        + [dma(1)] * 2
+        + [dma(4)] * 4
+        + [pltpu.SemaphoreType.DMA((2, 5)), dma(2), dma(2), dma(2), dma(3)],
         compiler_params=pltpu.CompilerParams(
             collective_id=3, has_side_effects=True, vmem_limit_bytes=56 * 1024 * 1024
         ),
         cost_estimate=pl.CostEstimate(
-            flops=4 * tokens * wide * width, bytes_accessed=4 * tokens * (width + wide), transcendentals=0
+            flops=6 * tokens * wide * width, bytes_accessed=4 * tokens * (width + 5 * wide), transcendentals=0
         ),
-        name="blend",
-    )(gg, w_o, og_all, sums, jnp.broadcast_to(mask[None], (8, tokens)))
-
-    if ring:
-        pieces = lax.psum_scatter(wog, "head", scatter_dimension=0, tiled=False)
-    dy, dpg = pl.pallas_call(
-        gate_kernel,
-        grid=grid,
-        in_specs=[forth(wide), forth(LANES), forth(wide), forth(wide), forth(wide), forth(LANES), whole(rowp)],
-        out_specs=[forth(wide), forth(wide)],
-        out_shape=[sds((tokens, wide), BF16), sds((tokens, wide), BF16)],
-        compiler_params=params,
-        cost_estimate=pl.CostEstimate(
-            flops=20 * tokens * wide, bytes_accessed=tokens * wide * 14, transcendentals=tokens * wide
-        ),
-        name="gate_back",
-    )(act, aux, z, d0, y, stat2, rowp)
-
-    wig_gate = t_dot(h_all, dpg).astype(BF16)
-    dy, wig_gate = lax.optimization_barrier((dy, wig_gate))
+        name="mid",
+    )(gg, w_o, og_all, h_all, act, aux, z, d0, y, sums, jnp.broadcast_to(mask[None], (8, tokens)), rowp)
     own_gate = lax.psum_scatter(wig_gate, "head", scatter_dimension=0, tiled=True)
 
     rest = chans + LANES
-    dp, sm, branch = pl.pallas_call(
-        functools.partial(back_kernel, heads=heads, wide=wide),
+    dp, sm, pieces = pl.pallas_call(
+        functools.partial(back_kernel, heads=heads, wide=wide, ring=ring),
         grid=grid,
         in_specs=[
             back(chans), back(LANES), back(wide), back(wide),
@@ -1280,20 +1425,21 @@
             whole(expand), whole(seg), whole(rowp), whole(colp), whole(cw),
         ],
         out_specs=[back(rest), pl.BlockSpec((8, chans), lambda j: (0, 0)), hbm],
-        out_shape=[sds((tokens, rest), BF16), sds((8, chans), F32), sds((local_len, width), F32)],
+        out_shape=[sds((tokens, rest), BF16), sds((8, chans), F32), sds((ranks,) + wog_shape, BF16)],
         scratch_shapes=[pltpu.VMEM((STATE, wide), F32), pltpu.VMEM((16, chans), F32)]
-        + [pltpu.VMEM((local_len, width), BF16)] * 3
-        + [pltpu.VMEM((local_len, width), F32)]
-        + [dma(2)] * 3,
+        + [dma(4)] * 2
+        + [dma(1)],
         compiler_params=pltpu.CompilerParams(
             dimension_semantics=("arbitrary",), collective_id=2, has_side_effects=True,
             vmem_limit_bytes=56 * 1024 * 1024,
-        ),
+        )
+        if ring
+        else params,
         cost_estimate=pl.CostEstimate(
             flops=2 * tokens * wide * 12 * chunk, bytes_accessed=tokens * wide * 24, transcendentals=tokens * chunk * heads
         ),
         name="scan_back",
-    )(act, aux, dy, y, states, slope, u, partial, expand, seg, rowp, colp, cw)
+    )(act, aux, dy, y, states, slope, u, wog, expand, seg, rowp, colp, cw)
 
     skip_h = jnp.sum(sm[5, :wide].reshape(heads, HEAD_DIM), axis=1)
     tiny = jnp.concatenate([sm[:5].reshape(-1), sm[6, :heads], sm[7, :heads], skip_h])
@@ -1304,7 +1450,7 @@
             in_specs=[hbm] * 6 + [vmem],
             out_specs=[hbm] * 4,
             out_shape=[
-                sds((local_len, width), F32),
+                sds((local_len, width), BF16),
                 sds((ranks, shard, wide), BF16),
                 sds((ranks, shard, rest), BF16),
                 sds((owners, piece, width), BF16),
@@ -1318,18 +1464,16 @@
             + [pltpu.VMEM((local_len // 2, width), BF16)] * 2
             + [pltpu.VMEM((local_len, width), BF16)] * 2
             + [
-                pltpu.VMEM((2, local_len, 256), F32),
                 pltpu.VMEM((2, shard, rest), BF16),
                 pltpu.VMEM((shard, rest), BF16),
                 pltpu.VMEM((4, shard, rest), BF16),
                 pltpu.VMEM((3, shard, rest), BF16),
                 pltpu.VMEM((3, shard, rest), BF16),
-                pltpu.VMEM((ranks, owners // ranks, piece, width), BF16),
             ]
             + [dma(6), dma(2)]
-            + [dma(4)] * 12
+            + [dma(6)] * 2
+            + [dma(4)] * 10
             + [dma(owners)] * 2
-            + [dma(4)] * 2
             + [dma(2)],
             compiler_params=pltpu.CompilerParams(
                 collective_id=1, has_side_effects=True, vmem_limit_bytes=56 * 1024 * 1024
@@ -1339,45 +1483,53 @@
             ),
             name="weight_grads",
         )(dpg, dp, w_t, h_all, own_gate, pieces, laid)
-        w_out_grad = w_out_grad.reshape(n_own, width).astype(F32)
+        w_out_grad = w_out_grad.reshape(n_own, width)
         tiny_all = rest_rows[:, :, rest - spare :].reshape(ranks, shard * spare)[:, : tiny.shape[0]].astype(F32)
     else:
         full = lax.all_gather(lax.psum(wog, "head"), "seq", axis=0, tiled=True)
-        w_out_grad = lax.dynamic_slice_in_dim(full, owner * n_own, n_own, 0).astype(F32)
+        w_out_grad = lax.dynamic_slice_in_dim(full, owner * n_own, n_own, 0)
         wig = t_dot(h_all, dp).astype(BF16)
         dn = (dot_t(dp, w_t[:, wide:]) + dot_t(dpg, w_t[:, :wide])).astype(BF16)
-        dn = lax.psum_scatter(dn, "seq", scatter_dimension=0, tiled=True).astype(F32)
+        dn = lax.psum_scatter(dn, "seq", scatter_dimension=0, tiled=True)
         gate_rows = lax.all_gather(own_gate, "seq")
         rest_rows = lax.all_gather(lax.psum_scatter(wig, "head", scatter_dimension=0, tiled=True), "seq")
         tiny_all = lax.all_gather(lax.psum(tiny, "head"), "seq")
-    gate_gain_grad = jnp.sum(w_out.astype(F32) * w_out_grad, axis=1) / gate_gain.astype(F32)
-
-    strip = min(32, shard)
-
-    def rows_spec(size):
-        return pl.BlockSpec((strip, size), lambda j: (j, 0))
-
-    def ranks_spec(size):
-        return pl.BlockSpec((ranks, strip, size), lambda j: (0, j, 0))
-
-    w_in_grad, w_dt_grad, norm_gain_grad = pl.pallas_call(
+    strips = min(8, shard // 16)
+
+    def strip(total, size):
+        return pl.BlockSpec((total // strips, size), lambda j: (j, 0))
+
+    def ranks_strip(size):
+        return pl.BlockSpec((ranks, shard // strips, size), lambda j: (0, j, 0))
+
+    w_in_grad, w_dt_grad, norm_gain_grad, w_out_grad, gate_gain_grad, block_out, hidden_grad = pl.pallas_call(
         functools.partial(finish_kernel, heads=heads, wide=wide),
-        grid=(shard // strip,),
-        in_specs=[ranks_spec(wide), ranks_spec(rest), rows_spec(PROJ), rows_spec(HEADS), rows_spec(1)],
-        out_specs=[rows_spec(PROJ), rows_spec(HEADS), rows_spec(1)],
-        out_shape=[sds((shard, PROJ), F32), sds((shard, HEADS), F32), sds((shard, 1), F32)],
+        grid=(strips,),
+        in_specs=[
+            ranks_strip(wide), ranks_strip(rest), strip(shard, PROJ), strip(shard, HEADS), strip(shard, 1),
+            strip(n_own, width), strip(n_own, width), strip(n_own, 1),
+            strip(local_len, width), strip(local_len, width), strip(local_len, width), strip(local_len, width),
+        ],
+        out_specs=[
+            strip(shard, PROJ), strip(shard, HEADS), strip(shard, 1), strip(n_own, width), strip(n_own, 1),
+            strip(local_len, width), strip(local_len, width),
+        ],
+        out_shape=[
+            sds((shard, PROJ), F32),
+            sds((shard, HEADS), F32),
+            sds((shard, 1), F32),
+            sds((n_own, width), F32),
+            sds((n_own, 1), F32),
+            sds((local_len, width), BF16),
+            sds((local_len, width), F32),
+        ],
         compiler_params=params,
-        cost_estimate=pl.CostEstimate(flops=6 * shard * PROJ, bytes_accessed=8 * shard * PROJ, transcendentals=0),
-        name="w_in_finish",
-    )(gate_rows, rest_rows, w_in, w_dt, gain_rows)
-    norm_gain_grad = norm_gain_grad.reshape(shard)
-
-    h32 = hidden[0].astype(F32)
-    own_r1m = lax.dynamic_slice_in_dim(stat2[:, 0:1], rank * local_len, local_len, 0)
-    block_out = (h32 + own_r1m * branch).astype(BF16)[None]
-    r0 = lax.rsqrt(jnp.mean(h32 * h32, axis=1, keepdims=True) + EPS)
-    mixed = jnp.sum(dn * h32, axis=1, keepdims=True) / width
-    hidden_grad = (out_grad[0].astype(F32) + dn - h32 * (r0 * r0 * mixed))[None]
+        cost_estimate=pl.CostEstimate(flops=6 * shard * PROJ, bytes_accessed=16 * shard * PROJ, transcendentals=0),
+        name="finish",
+    )(
+        gate_rows, rest_rows, w_in, w_dt, gain_rows, w_out_grad, w_out, gate_gain.astype(F32)[:, None],
+        hidden[0], out_grad[0], dn, branch,
+    )
 
     n_conv = 5 * chans
     conv_all = tiny_all[:, :n_conv].reshape(ranks, 5, chans)
@@ -1389,9 +1541,9 @@
     vec_own = lax.dynamic_slice_in_dim(vec, owner * hs, hs, 1)
 
     return (
-        block_out,
-        hidden_grad,
-        norm_gain_grad,
+        block_out[None],
+        hidden_grad[None],
+        norm_gain_grad.reshape(shard),
         w_in_grad,
         w_dt_grad,
         conv_own[:KERNEL],
@@ -1399,7 +1551,7 @@
         vec_own[0],
         vec_own[1],
         vec_own[2],
-        gate_gain_grad,
+        gate_gain_grad.reshape(n_own),
         w_out_grad,
     )
 

time: 577 us -> 508 us (0.88)
  waiting for transfers between devices: 42.9 us -> 0.02 us
  matrix products: 14 us -> 0 us
  other arithmetic: 21.6 us -> 8.83 us
    pallas_call x1, Pallas kernels: 163 us -> 120 us  [local(): pl.pallas_call(grads_kernel, in_specs=[hbm] * 6 + [vmem], out_specs=[hbm]...]
    reduce_scatter x1 -> x0, waiting for transfers between devices: 42.1 us -> none  [local(): pieces = lax.psum_scatter(wog, 'head', scatter_dimension=0, tiled=False)]
    pallas_call x3 -> x2, Pallas kernels: 103 us -> 139 us  [the longest x1 87.2 us: local(): pl.pallas_call(functools.partial(mid_kernel, ring=ring), in_specs=[hbm] *...]
    dot_general x1 -> x0, matrix products: 14 us -> none  [t_dot(): lax.dot_general(a, b, (((0,), (0,)), ((), ())), preferred_element_type=F32)]
    broadcast_in_dim x1, other arithmetic: 7.89 us -> 0.01 us  [local(): gate_gain.astype(F32)[:, None]]
    pallas_call x1, Pallas kernels: 9.94 us -> 16.9 us  [local(): pl.pallas_call(functools.partial(finish_kernel, heads=heads, wide=wide),...]
    reduce_sum x1 -> x0, other arithmetic: 6.81 us -> none  [local(): r0 = lax.rsqrt(jnp.mean(h32 * h32, axis=1, keepdims=True) + EPS)]
  transfers between devices with their start and end apart: 2 -> 1, of which waited for: 1 -> 0; matrix products, arithmetic and copies ran while one was open for 1% -> 1% of each run, Pallas kernels for 9% -> 10%
where the time goes in v5:
time: 508 us; the launch traced here: 498 us
  Pallas kernels  454 us (89%)
  local copies, waits for them, and re-layouts  20.4 us (4%)
  between operations  15.4 us (3%)
  other arithmetic  8.83 us (2%)
    pallas_call x1, Pallas kernels, local(): pl.pallas_call(functools.partial(gather_kernel, ring=ring, wide=wide), in...  146 us
    pallas_call x1, Pallas kernels, local(): pl.pallas_call(grads_kernel, in_specs=[hbm] * 6 + [vmem], out_specs=[hbm]...  120 us
    pallas_call x1, Pallas kernels, local(): pl.pallas_call(functools.partial(mid_kernel, ring=ring), in_specs=[hbm] *...  87.2 us
    pallas_call x1, Pallas kernels, local(): pl.pallas_call(functools.partial(back_kernel, heads=heads, wide=wide, rin...  51.3 us
    pallas_call x1, Pallas kernels, local(): pl.pallas_call(functools.partial(scan_kernel, heads=heads, wide=wide), gr...  32 us
    pallas_call x1, Pallas kernels, local(): pl.pallas_call(functools.partial(finish_kernel, heads=heads, wide=wide),...  16.9 us
  transfers between devices with their start and end apart: 1, of which 0 were waited for; matrix products, arithmetic and copies ran while one was open for 1% of the time, Pallas kernels for 10%

profile of v5, /device:TPU:8, one launch (start us, length us, event | category | flops | bytes accessed | tf_op | source)
XLA Modules:
  0.0 498.4 jit_solution(14483615135368917576)
XLA Ops:
  7.2 0.7 convert_element_type.56
  7.9 0.7 multiply_convert_fusion
  8.6 0.1 copy.47
  8.7 0.8 reshape.124
  9.5 3.5 concatenate.28
  13.0 0.1 reshape.125
  13.1 0.8 copy.48.gain_ref
  13.9 0.7 pad_maximum_fusion.dtw_ref
  14.7 145.8 %gather_project.1 = (bf16[2048,2048]{1,0:T(8,128)(2,1)}, bf16[2048,2048]{1,0:T(8,128)(2,1)}, bf16[2048,2432]{1,0:T(8,128)(2,1)}, bf16[1024,2048]{1,0:T(8,128)(2,...) custom-call(bf16[512,2048]{1,0:T(8,128)(2,1)} %bitcast.33, ...), custom_call_target="tpu_custom_call" | custom-call | flops 28991029248 | bytes 36700160 | tf_op jit(solution)/shard_map/gather_project/pallas_call | solution.py:1244
  160.5 1.2 slice.107
  161.7 0.5 reshape.127
  162.3 0.1 reshape.128
  162.5 0.1 reshape.129
  162.6 0.1 reshape.130
  162.8 0.1 reshape.132
  163.5 0.1 reshape.131
  163.6 0.8 fusion.exp_ref
  165.1 0.6 fusion.5.cw_ref
  165.7 0.7 stack.19.rowp_ref
  166.4 0.6 broadcast_in_dim.52.cb_ref
  167.0 0.7 broadcast_in_dim.56.colp_ref
  167.7 0.6 broadcast_in_dim.53.dtb_ref
  168.3 32.0 %scan.1 = (bf16[2048,1280]{1,0:T(8,128)(2,1)}, bf16[2048,1280]{1,0:T(8,128)(2,1)}, f32[2048,128]{1,0:T(8,128)}, bf16[2048,1024]{1,0:T(8,128)(2,1)}, bf16[2048,10...) custom-call(bf16[2048,1280]{1,0:T(8,128)(2,1)} %get-tuple-element.46.u_ref, ...), custom_call_target="tpu_custom_call" | custom-call | flops 12884901888 | bytes 33554432 | tf_op jit(solution)/shard_map/scan/pallas_call | solution.py:1334
  200.3 0.6 broadcast_in_dim.57.mask_ref
  200.9 87.2 %mid.1 = (bf16[512,2048]{1,0:T(8,128)(2,1)}, bf16[2,64,2048]{2,1,0:T(8,128)(2,1)}, bf16[2048,1024]{1,0:T(8,128)(2,1)}, bf16[2048,1024]{1,0:T(8,128)(2,1)}, bf16[2048,1024]{1,0:T(8,128)(2,1)}) custom-call(bf16[2048,1024]{1,0:T(8,128)(2,1)} %get-tuple-element.51.gg_ref, bf16[1024,2048]{1,0:T(8,128)(2,1)} %get-tuple-element.52.wo_ref, ...), custom_call_target="tpu_custom_call" | custom-call | flops 25769803776 | bytes 58720256 | tf_op jit(solution)/shard_map/mid/pallas_call | solution.py:1370
  288.2 0.6 copy-done.1
  288.8 0.1 copy-done
  288.9 0.7 copy.50.dtw_ref
  289.6 0.9 fusion.1.seg_ref
  290.5 51.3 %scan_back.1 = (bf16[2048,1408]{1,0:T(8,128)(2,1)}, f32[8,1280]{1,0:T(8,128)}, bf16[4,2,64,2048]{3,2,1,0:T(8,128)(2,1)}) custom-call(bf16[2048,1280]{1,0:T(8,128)(2,1)} %get-tuple-element.55.act_ref, f32[2048,128]{1,0:T(8,128)} %get-tuple-element.56.aux_ref, bf16[2048,1024]{1,0:T(8,128)(2,1)} %get-tuple-element.60.dy_ref, ...), custom_call_target="tpu_custom_call" | custom-call | flops 12884901888 | bytes 50331648 | tf_op jit(solution)/shard_map/scan_back/pallas_call | solution.py:1418
  341.9 0.8 convert.22
  342.7 0.8 slice_reduce_fusion.1
  343.6 0.1 reduce_sum.18
  343.7 0.1 concatenate.34
  343.8 0.7 convert_element_type.65.tiny_ref
  344.5 0.9 copy.52.ggain_ref
  345.4 120.5 %weight_grads.1 = (bf16[512,2048]{1,0:T(8,128)(2,1)}, bf16[4,256,1024]{2,1,0:T(8,128)(2,1)}, bf16[4,256,1408]{2,1,0:T(8,128)(2,1)}, bf16[8,64,2048]{2,1,0:T(8,128)(2,1)}) custom-call(bf16[2048,1024]{1,0:T(8,128)(2,1)} %get-tuple-element.59.dpg_ref, bf16[2048,1408]{1,0:T(8,128)(2,1)} %get-tuple-element.64.dp_ref, bf16[2048,2432]{1,0:T(8,128)(2,1)} %get-tuple-element.50.w_ref, ...), custom_call_target="tpu_custom_call" | custom-call | flops 40802189312 | bytes 39845888 | tf_op jit(solution)/shard_map/weight_grads/pallas_call | solution.py:1448
  465.9 1.1 slice.96
  466.9 0.2 reshape.138
  467.3 0.1 fusion.6
  467.4 0.6 slice.125
  468.0 0.6 slice_reduce_fusion.2
  468.6 16.9 %finish.1 = (f32[256,8448]{1,0:T(8,128)}, f32[256,64]{1,0:T(8,128)}, f32[256,1]{1,0:T(8,128)}, f32[512,2048]{1,0:T(8,128)}, f32[512,1]{1,0:T(8,128)}, /*index=5*/bf16[512,2048]{1,0:T(8,128)(2,1)}, f32[512,2048]{1,0:T(8,128)}) custom-call(bf16[4,256,1024]{2,1,0:T(8,128)(2,1)} %get-tuple-element.68.gate_ref, bf16[4,256,1408]{2,1,0:T(8,128)(2,1)} %get-tuple-element.69.rest_ref, ...), custom_call_target="tpu_custom_call" | custom-call | flops 12976128 | bytes 34603008 | tf_op jit(solution)/shard_map/finish/pallas_call | solution.py:1505
  485.5 1.6 copy.54
  487.1 1.7 reduce.3
  488.8 1.6 reduce.1
  490.4 0.1 reshape.142
  490.6 0.5 slice_bitcast_fusion.3
  (50 shorter events, 1.4 us)
Async XLA Ops:
  7.2 338.2 %reduce-scatter.2.cloned.1.call-start = ((), (), s32[]{:S(2)}) async-start(), calls=%async_computation.1 | async-start | bytes 4718592 | tf_op jit(solution)/shard_map/reduce_scatter | solution.py:1415
  288.1 0.7 copy-start.1
  288.2 0.8 copy-start
Sparse Core Ops, SparseCore 0:
  288.3 46.1 reduce-scatter.1

commit v6 on v5

--- a/solution.py
+++ b/solution.py
@@ -59,294 +59,6 @@
     pl.semaphore_wait(barrier, count)
 
 
-def gather_kernel(
-    hid_ref, og_ref, w_ref, wo_in_ref, gain_ref, dtw_ref,
-    hall_ref, ogall_ref, wt_ref, wo_ref, z_ref, u_ref, d_ref, d0_ref,
-    hv, ov, wv, wov, stage, zv, uv, dv, d0v,
-    h_send, h_recv, o_send, o_recv, z_up, z_dn, z_recv, s_send, s_recv,
-    c_up, c_dn, c_recv, t_send, t_recv, local_sem, out_sem, *, ring, wide,
-):
-    s = lax.axis_index("seq")
-    q = hid_ref.shape[0]
-    half = q // 2
-    x_peer = s + 1 - 2 * lax.rem(s, 2)
-    y_peer = lax.rem(s + 2, 4)
-    far = 3 - s
-    to_x, to_y = {"seq": x_peer}, {"seq": y_peer}
-    chans = uv.shape[1]
-    n_main = stage.shape[1]
-    n = stage.shape[0]
-    peers = [to_x, to_y]
-    extra = []
-
-    def block(ref, at, start, size):
-        return ref.at[pl.ds(pl.multiple_of(at * q + start, 16), size), :]
-
-    if ring:
-        h = lax.axis_index("head")
-        core = lax.rem(h, 2)
-        r = h // 2
-        last = lax.axis_size("head") // 2 - 1
-        to_sib, to_up, to_down = {"head": h + 1 - 2 * core}, {"head": lax.rem(h + 2, 2 * last + 2)}, {"head": lax.rem(h + 2 * last, 2 * last + 2)}
-        above, below = r < last, r > 0
-        peers.append(to_sib)
-        extra = [(above, to_up), (below, to_down)]
-        first = pl.multiple_of(s * wide, LANES)
-        second = pl.multiple_of(DI + s * wide, LANES)
-        loads = [
-            pltpu.make_async_copy(w_ref.at[:, pl.ds(first, wide)], stage.at[:, :wide], local_sem.at[0]),
-            pltpu.make_async_copy(w_ref.at[:, pl.ds(second, wide)], stage.at[:, wide : 2 * wide], local_sem.at[1]),
-            pltpu.make_async_copy(w_ref.at[:, 2 * DI :], stage.at[:, 2 * wide :], local_sem.at[2]),
-        ]
-        is_root = r == s
-        n_o = wov.shape[0] // 2
-        load_o = pltpu.make_async_copy(
-            wo_in_ref, wov.at[pl.ds(pl.multiple_of(core * n_o, 16), n_o), :], local_sem.at[5]
-        )
-        pl.when(is_root)(load_o.start)
-    else:
-        loads = [
-            pltpu.make_async_copy(w_ref, wv, local_sem.at[0]),
-            pltpu.make_async_copy(wo_in_ref, wov, local_sem.at[5]),
-        ]
-    for copy in loads:
-        copy.start()
-    own_h = pltpu.make_async_copy(hid_ref, block(hv, s, 0, q), local_sem.at[3])
-    own_o = pltpu.make_async_copy(og_ref, block(ov, s, 0, q), local_sem.at[4])
-    own_h.start()
-    own_o.start()
-    greet(peers, extra)
-
-    sent = []
-
-    def send(src, dst, sems, i, target):
-        copy = remote(src, dst, sems[0].at[i], sems[1].at[i], target)
-        copy.start()
-        sent.append(copy)
-        return copy
-
-    def open_exchange(src, buf, sems):
-        return (
-            send(src, block(buf, s, 0, q), sems, 0, to_x),
-            send(src, block(buf, s, 0, q), sems, 1, to_y),
-        )
-
-    def relay(buf, sems, heads_in):
-        heads_in[0].wait_recv()
-        a = block(buf, x_peer, 0, half)
-        first = send(a, a, sems, 2, to_y)
-        heads_in[1].wait_recv()
-        b = block(buf, y_peer, half, half)
-        return first, send(b, b, sems, 3, to_x)
-
-    h_sems, o_sems = (h_send, h_recv), (o_send, o_recv)
-    h_open = open_exchange(hid_ref, hv, h_sems)
-
-    closing = []
-    if ring:
-        def w_block(at):
-            return wv.at[pl.ds(pl.multiple_of((2 * at + core) * n, 16), n), :]
-
-        def w_copy(at, sems, target):
-            return remote(w_block(at), w_block(at), sems.at[at], z_recv.at[at], target)
-
-        def w_swap(at):
-            return remote(w_block(at), w_block(at), s_send.at[at], s_recv.at[at], to_sib)
-
-        def launch(there, make):
-            @pl.when(there)
-            def _():
-                make().start()
-
-            def finish():
-                @pl.when(there)
-                def _():
-                    make().wait_send()
-
-            closing.append(finish)
-
-        always = r >= 0
-
-        def w_step(k):
-            lower, upper = r - k, r + k
-            has_lower, has_upper = lower >= 0, upper <= last
-
-            @pl.when(has_lower)
-            def _():
-                w_copy(lower, z_up, to_up).wait_recv()
-
-            launch(has_lower & above, lambda: w_copy(lower, z_up, to_up))
-            launch(has_lower, lambda: w_swap(lower))
-
-            @pl.when(has_upper)
-            def _():
-                w_copy(upper, z_dn, to_down).wait_recv()
-
-            launch(has_upper & below, lambda: w_copy(upper, z_dn, to_down))
-            launch(has_upper, lambda: w_swap(upper))
-
-        chunks = c_recv.shape[0]
-        n_c = n_o // chunks
-        dist = jnp.where(r > s, r - s, s - r)
-
-        def o_block(i):
-            return wov.at[pl.ds(pl.multiple_of(core * n_o + i * n_c, 16), n_c), :]
-
-        def o_copy(i, sems, target):
-            return remote(o_block(i), o_block(i), sems.at[i], c_recv.at[i], target)
-
-        def o_swap(i):
-            return remote(o_block(i), o_block(i), t_send.at[i], t_recv.at[i], to_sib)
-
-        def o_root():
-            @pl.when(is_root)
-            def _():
-                load_o.wait()
-
-            for i in range(chunks):
-                launch(is_root & above, lambda i=i: o_copy(i, c_up, to_up))
-                launch(is_root & below, lambda i=i: o_copy(i, c_dn, to_down))
-                launch(is_root, lambda i=i: o_swap(i))
-
-        def o_tick(t):
-            i = t - dist
-            live = (dist >= 1) & (i >= 0) & (i < chunks)
-
-            @pl.when(live)
-            def _():
-                o_copy(i, c_up, to_up).wait_recv()
-
-            pl.when(live & (r > s) & above)(lambda: o_copy(i, c_up, to_up).start())
-            pl.when(live & (r < s) & below)(lambda: o_copy(i, c_dn, to_down).start())
-            pl.when(live)(lambda: o_swap(i).start())
-
-        def o_finish():
-            for i in range(chunks):
-                pl.when((r > s) & above)(lambda: o_copy(i, c_up, to_up).wait_send())
-                pl.when((r < s) & below)(lambda: o_copy(i, c_dn, to_down).wait_send())
-                pl.when(dist >= 1)(lambda: o_swap(i).wait_send())
-
-        closing.append(o_finish)
-        for copy in loads:
-            copy.wait()
-        own = pl.ds(pl.multiple_of(h * n, 16), n)
-        wv[own, :n_main] = (stage[...].astype(F32) * gain_ref[...]).astype(BF16)
-        wv[own, n_main:] = dtw_ref[...]
-        launch(above, lambda: w_copy(r, z_up, to_up))
-        launch(below, lambda: w_copy(r, z_dn, to_down))
-        launch(always, lambda: w_swap(r))
-        w_step(1)
-    else:
-        for copy in loads:
-            copy.wait()
-
-    h_far = relay(hv, h_sems, h_open)
-    if ring:
-        w_step(2)
-        o_root()
-    for copy in h_far:
-        copy.wait_recv()
-    o_open = open_exchange(og_ref, ov, o_sems)
-    if ring:
-        o_tick(1)
-        w_step(3)
-        for at in range(4):
-            w_swap(at).wait_recv()
-    own_h.wait()
-    own_o.wait()
-
-    rows = min(CHUNK, q)
-
-    def cut(at_block):
-        return pl.ds(pl.multiple_of(at_block * q, 16), q)
-
-    def project_outs(at_block, i):
-        at = cut(at_block)
-        pairs = ((hv, hall_ref), (zv, z_ref), (uv, u_ref), (dv, d_ref))
-        return [
-            pltpu.make_async_copy(src.at[at, :], dst.at[at, :], out_sem.at[4 * i + k])
-            for k, (src, dst) in enumerate(pairs)
-        ]
-
-    def pull_outs(at_block, i):
-        at = cut(at_block)
-        pairs = ((ov, ogall_ref), (d0v, d0_ref))
-        return [
-            pltpu.make_async_copy(src.at[at, :], dst.at[at, :], out_sem.at[16 + 2 * i + k])
-            for k, (src, dst) in enumerate(pairs)
-        ]
-
-    def nth(i):
-        return jnp.where(i == 0, s, jnp.where(i == 1, x_peer, jnp.where(i == 2, y_peer, far)))
-
-    w_out = pltpu.make_async_copy(wv, wt_ref, out_sem.at[24])
-    o_out = pltpu.make_async_copy(wov, wo_ref, out_sem.at[25])
-    w_out.start()
-
-    def project(at_block):
-        @pl.loop(0, q // rows)
-        def _(j):
-            at = pl.ds(pl.multiple_of(at_block * q + j * rows, 16), rows)
-            hb = hv[at, :]
-            h32 = hb.astype(F32)
-            r0 = lax.rsqrt(jnp.mean(h32 * h32, axis=1, keepdims=True) + EPS)
-            zv[at, :] = (dot(hb, wv[:, :wide]) * r0).astype(BF16)
-            uv[at, :] = (dot(hb, wv[:, wide : wide + chans]) * r0).astype(BF16)
-            raw = dot(hb, wv[:, wide + chans :]) * r0
-            lane = lax.broadcasted_iota(jnp.int32, raw.shape, 1)
-            dv[at, :] = jnp.where(lane == LANES - 1, r0, raw)
-
-    def pull(at_block):
-        at = cut(at_block)
-
-        @pl.loop(0, wide // 256)
-        def _(j):
-            to = pl.ds(pl.multiple_of(j * 256, 256), 256)
-            d0v[at, to] = dot_t(ov[at, :], wov[to, :]).astype(BF16)
-
-    @pl.loop(0, 4)
-    def _(i):
-        at_block = nth(i)
-        project(at_block)
-        for copy in project_outs(at_block, i):
-            copy.start()
-        if ring:
-            o_tick(2 + i)
-
-    if ring:
-        o_tick(6)
-    o_far = relay(ov, o_sems, o_open)
-    if ring:
-        for t in range(7, chunks + 3):
-            o_tick(t)
-        for i in range(chunks):
-            o_swap(i).wait_recv()
-    o_out.start()
-
-    @pl.loop(0, 4)
-    def _(i):
-        at_block = nth(i)
-
-        @pl.when(i == 3)
-        def _():
-            for copy in o_far:
-                copy.wait_recv()
-
-        pull(at_block)
-        for copy in pull_outs(at_block, i):
-            copy.start()
-
-    for i, at_block in enumerate((s, x_peer, y_peer, far)):
-        for copy in project_outs(at_block, i) + pull_outs(at_block, i):
-            copy.wait()
-    w_out.wait()
-    o_out.wait()
-    for copy in sent:
-        copy.wait_send()
-    for finish in closing:
-        finish()
-
-
 def decays(aux, heads, expand, rate_e, rate_row, rate_col):
     rows = aux.shape[0]
     lane = lax.broadcasted_iota(jnp.int32, aux.shape, 1)
@@ -362,6 +74,13 @@
     return causal, dt_e, cum_e, cum_c, cum_t
 
 
+def head_matrix(wide, turned=False):
+    shape = (wide, LANES) if turned else (LANES, wide)
+    channel = lax.broadcasted_iota(jnp.int32, shape, 0 if turned else 1)
+    head = lax.broadcasted_iota(jnp.int32, shape, 1 if turned else 0)
+    return jnp.where(channel // HEAD_DIM == head, 1.0, 0.0).astype(BF16)
+
+
 def shift_matrix(rows, by):
     r = lax.broadcasted_iota(jnp.int32, (rows, rows), 0)
     c = lax.broadcasted_iota(jnp.int32, (rows, rows), 1)
@@ -378,35 +97,22 @@
     return top, low, right
 
 
-def scan_kernel(
-    u_ref, d_ref, z_ref, d0_ref, cw_ref, cb_ref, dtb_ref, exp_ref, rowp_ref, colp_ref,
-    act_ref, slope_ref, aux_ref, y_ref, gg_ref, st_ref, sum_ref, state, ext, *, heads, wide,
-):
-    step = pl.program_id(0)
-    rows = u_ref.shape[0]
-    chans = u_ref.shape[1]
-
-    @pl.when(step == 0)
-    def _():
-        state[...] = jnp.zeros_like(state)
-        ext[...] = jnp.zeros_like(ext)
-
-    u = u_ref[...]
+def scan_chunk(u, raw, z, taps, bias, dtb, expand, rowp, rate_col, state, ext, st_out, heads):
+    rows, chans = u.shape
+    wide = expand.shape[1]
     u32 = u.astype(F32)
-    pre = cb_ref[0:1, :] + cw_ref[KERNEL - 1 : KERNEL, :] * u32
+    pre = bias + taps[KERNEL - 1 : KERNEL] * u32
     before = jnp.zeros((8, chans), F32)
     for j in range(1, KERNEL):
-        tap = cw_ref[KERNEL - 1 - j : KERNEL - j, :]
+        tap = taps[KERNEL - 1 - j : KERNEL - j]
         pre = pre + tap * dot(shift_matrix(rows, -j), u)
         before = before + tap * ext[8 - j : 16 - j, :]
     pre = jnp.concatenate([pre[:8] + before, pre[8:]], axis=0)
     ext[0:8, :] = u32[rows - 8 :, :]
     sig = sigmoid(pre)
     act = (pre * sig).astype(BF16)
-    act_ref[...] = act
-    slope_ref[...] = (sig * (1.0 + pre * (1.0 - sig))).astype(BF16)
-    raw = d_ref[...]
-    v = raw + dtb_ref[0:1, :]
+    slope = (sig * (1.0 + pre * (1.0 - sig))).astype(BF16)
+    v = raw + dtb
     soft = jnp.maximum(v, 0.0) + jnp.log1p(jnp.exp(-jnp.abs(v)))
     soft = soft.astype(BF16).astype(F32)
     lane = lax.broadcasted_iota(jnp.int32, v.shape, 1)
@@ -414,20 +120,16 @@
     sig_v = pltpu.roll(sigmoid(v), heads, 1)
     aux = jnp.where((lane >= heads) & (lane < 2 * heads), sig_v, aux)
     aux = jnp.where(lane == LANES - 1, raw, aux)
-    aux_ref[...] = aux
-
-    x = act[:, :wide]
-    x32 = x.astype(F32)
+
+    x32 = act[:, :wide].astype(F32)
     b = act[:, wide : wide + STATE]
     c = act[:, wide + STATE :]
-    causal, dt_e, cum_e, cum_c, cum_t = decays(
-        aux, heads, exp_ref[...], rowp_ref[0:1, :], rowp_ref[3:4, :LANES], colp_ref[:, 0:1]
-    )
+    causal, dt_e, cum_e, cum_c, cum_t = decays(aux, heads, expand, rowp[0:1], rowp[3:4, :LANES], rate_col)
     xdt = x32 * dt_e
     xdt16 = xdt.astype(BF16)
     scores = dot_t(c, b)
     st = state[...]
-    st_ref[0] = st
+    st_out[...] = st
     mid = rows // 2
     half = lax.broadcasted_iota(jnp.int32, (rows, LANES), 1) < HEAD_DIM
     parts = []
@@ -447,25 +149,497 @@
     tail = jnp.exp(last - cum_e)
     state[...] = jnp.exp(last) * st + t_dot(b, (xdt * tail).astype(BF16))
     y16 = y.astype(BF16)
+    ssd = (y16.astype(F32) + rowp[1:2] * x32).astype(BF16).astype(F32)
+    z = z.astype(F32)
+    g = ssd * (z * sigmoid(z))
+    gg = (g * rowp[2:3]).astype(BF16)
+    ssq = dot_t(jnp.ones((8, wide), BF16), (g * g).astype(BF16))
+    return act, slope, aux, y16, gg, ssq
+
+
+def with_cross(ssq, gg, d0):
+    cross = dot_t(jnp.ones((8, gg.shape[1]), BF16), (gg.astype(F32) * d0.astype(F32)).astype(BF16))
+    return jnp.where(lax.broadcasted_iota(jnp.int32, ssq.shape, 0) == 0, ssq, cross)
+
+
+def scan_kernel(
+    u_ref, d_ref, z_ref, d0_ref, cw_ref, dtb_ref, rowp_ref, colp_ref,
+    act_ref, slope_ref, aux_ref, y_ref, gg_ref, st_ref, sum_ref, state, ext, *, heads,
+):
+    @pl.when(pl.program_id(0) == 0)
+    def _():
+        state[...] = jnp.zeros_like(state)
+        ext[...] = jnp.zeros_like(ext)
+
+    act, slope, aux, y16, gg, ssq = scan_chunk(
+        u_ref[...], d_ref[...], z_ref[...], cw_ref[0:KERNEL, :], cw_ref[KERNEL : KERNEL + 1, :], dtb_ref[0:1, :],
+        head_matrix(z_ref.shape[1]), rowp_ref[...], colp_ref[:, 0:1], state, ext, st_ref.at[0], heads,
+    )
+    act_ref[...] = act
+    slope_ref[...] = slope
+    aux_ref[...] = aux
     y_ref[...] = y16
-    ssd = (y16.astype(F32) + rowp_ref[1:2, :] * x32).astype(BF16).astype(F32)
-    z = z_ref[...].astype(F32)
-    g = ssd * (z * sigmoid(z))
-    gg = g * rowp_ref[2:3, :]
-    gg_ref[...] = gg.astype(BF16)
-    ones = jnp.ones((8, wide), BF16)
-    ssq = dot_t(ones, (g * g).astype(BF16))
-    cross = dot_t(ones, (gg * d0_ref[...].astype(F32)).astype(BF16))
-    sub = lax.broadcasted_iota(jnp.int32, ssq.shape, 0)
-    sum_ref[...] = jnp.where(sub == 0, ssq, cross)
+    gg_ref[...] = gg
+    sum_ref[...] = with_cross(ssq, gg, d0_ref[...])
 
 
 def seg_dot(v, seg):
     hi = v.astype(BF16)
-    rest = v - hi.astype(F32)
-    mid = rest.astype(BF16)
-    low = (rest - mid.astype(F32)).astype(BF16)
-    return dot(hi, seg) + dot(mid, seg) + dot(low, seg)
+    return dot(hi, seg) + dot((v - hi.astype(F32)).astype(BF16), seg)
+
+
+def rank_params(par, s, cw_ref, dtb_ref, rowp_ref, colp_ref, heads, wide):
+    owners, _, lanes = par.shape
+    chans = cw_ref.shape[1]
+    share = CHANNELS // owners
+    gains = DI // owners
+    per = HEADS // owners
+
+    def iota(shape, dim):
+        return lax.broadcasted_iota(jnp.int32, shape, dim)
+
+    def chosen(there):
+        return jnp.where(there, 1.0, 0.0).astype(BF16)
+
+    cw_ref[...] = jnp.zeros_like(cw_ref)
+    at = iota((1, chans), 1)
+    wanted = jnp.where(at < wide, s * wide + at, DI + at - wide)
+
+    @pl.loop(0, owners)
+    def _(j):
+        i = iota((lanes, chans), 0)
+        cw_ref[...] += dot(par[j], chosen((i + j * share == wanted) & (i < share)))
+
+    count = heads // per
+    a_e, skip_e, a_row, dt_row, a_col, gain = 0.0, 0.0, 0.0, 0.0, 0.0, []
+    head_of = iota((LANES, wide), 1) // HEAD_DIM
+    lane_e = iota((LANES, wide), 0)
+    lane = iota((LANES, LANES), 0)
+    to = iota((LANES, LANES), 1)
+    for k in range(count):
+        block = par[s * count + k]
+        few = block[:, :LANES]
+        gain.append(block[5:6, :gains].astype(F32))
+
+        def spread(first):
+            return chosen((lane_e - first + per * k == head_of) & (lane_e >= first) & (lane_e < first + per))
+
+        def placed(first):
+            return chosen((lane - first + per * k == to) & (lane >= first) & (lane < first + per))
+
+        a_e = a_e + dot(few, spread(per))
+        skip_e = skip_e + dot(few, spread(2 * per))
+        dt_row = dt_row + dot(few, placed(0))
+        a_row = a_row + dot(few, placed(per))
+        a_col = a_col + lax.dot_general(placed(per), few, (((0,), (1,)), ((), ())), preferred_element_type=F32)
+    rowp_ref[0:1, :] = -jnp.exp(a_e[6:7])
+    rowp_ref[1:2, :] = skip_e[6:7]
+    rowp_ref[2:3, :] = jnp.concatenate(gain, axis=1)
+    rowp_ref[3:8, :] = jnp.zeros((5, wide), F32)
+    rowp_ref[3:4, :LANES] = jnp.where(iota((1, LANES), 1) < heads, -jnp.exp(a_row[6:7]), 0.0)
+    dtb_ref[...] = jnp.broadcast_to(dt_row[6:7], dtb_ref.shape)
+    col = jnp.where(iota((LANES, 1), 0) < heads, -jnp.exp(a_col[:, 6:7]), 0.0)
+    colp_ref[...] = jnp.broadcast_to(col, colp_ref.shape)
+
+
+def gather_kernel(
+    hid_ref, og_ref, w_ref, wo_in_ref, gain_ref, dtw_ref, cwt_ref, cbi_ref, ggn_ref, hds_ref,
+    hall_ref, ogall_ref, wt_ref, wo_ref, z_ref, u_ref, d0_ref, act_ref, slope_ref, aux_ref, y_ref, gg_ref, st_ref,
+    sum_ref, cw_ref, dtb_ref, rowp_ref, colp_ref,
+    hv, ov, wv, wov, stage, zv, uv, dv, par, par_f, state, ext, st_v,
+    h_send, h_recv, o_send, o_recv, z_up, z_dn, z_recv, s_send, s_recv,
+    c_up, c_dn, c_recv, t_send, t_recv, a_send, a_recv, local_sem, out_sem, scan_sem, st_sem, *, heads, wide,
+):
+    ring = True
+    s = lax.axis_index("seq")
+    q = hid_ref.shape[0]
+    half = q // 2
+    x_peer = s + 1 - 2 * lax.rem(s, 2)
+    y_peer = lax.rem(s + 2, 4)
+    far = 3 - s
+    to_x, to_y = {"seq": x_peer}, {"seq": y_peer}
+    chans = uv.shape[1]
+    n_main = stage.shape[1]
+    n = stage.shape[0]
+    peers = [to_x, to_y]
+
+    def block(ref, at, start, size):
+        return ref.at[pl.ds(pl.multiple_of(at * q + start, 16), size), :]
+
+    if ring:
+        h = lax.axis_index("head")
+        core = lax.rem(h, 2)
+        r = h // 2
+        last = lax.axis_size("head") // 2 - 1
+        to_sib, to_up, to_down = {"head": h + 1 - 2 * core}, {"head": lax.rem(h + 2, 2 * last + 2)}, {"head": lax.rem(h + 2 * last, 2 * last + 2)}
+        above, below = r < last, r > 0
+        owners = lax.axis_size("head")
+        to_heads = [{"head": lax.rem(h + k, owners)} for k in range(1, owners)]
+        peers += to_heads
+        first = pl.multiple_of(s * wide, LANES)
+        second = pl.multiple_of(DI + s * wide, LANES)
+        loads = [
+            pltpu.make_async_copy(w_ref.at[:, pl.ds(first, wide)], stage.at[:, :wide], local_sem.at[0]),
+            pltpu.make_async_copy(w_ref.at[:, pl.ds(second, wide)], stage.at[:, wide : 2 * wide], local_sem.at[1]),
+            pltpu.make_async_copy(w_ref.at[:, 2 * DI :], stage.at[:, 2 * wide :], local_sem.at[2]),
+        ]
+        is_root = r == s
+        n_o = wov.shape[0] // 2
+        load_o = pltpu.make_async_copy(
+            wo_in_ref, wov.at[pl.ds(pl.multiple_of(core * n_o, 16), n_o), :], local_sem.at[5]
+        )
+        pl.when(is_root)(load_o.start)
+    for copy in loads:
+        copy.start()
+    own_h = pltpu.make_async_copy(hid_ref, block(hv, s, 0, q), local_sem.at[3])
+    own_o = pltpu.make_async_copy(og_ref, block(ov, s, 0, q), local_sem.at[4])
+    own_h.start()
+    own_o.start()
+    par_f[...] = jnp.zeros_like(par_f)
+    par_f[0:KERNEL, : cwt_ref.shape[1]] = cwt_ref[...].astype(F32)
+    for k, row in enumerate((cbi_ref, ggn_ref, hds_ref)):
+        par_f[KERNEL + k : KERNEL + k + 1, : row.shape[1]] = row[...].astype(F32)
+    par[h] = par_f[...].astype(BF16)
+    greet(peers)
+
+    sent = []
+
+    def send(src, dst, sems, i, target):
+        copy = remote(src, dst, sems[0].at[i], sems[1].at[i], target)
+        copy.start()
+        sent.append(copy)
+        return copy
+
+    def open_exchange(src, buf, sems):
+        return (
+            send(src, block(buf, s, 0, q), sems, 0, to_x),
+            send(src, block(buf, s, 0, q), sems, 1, to_y),
+        )
+
+    def relay(buf, sems, heads_in):
+        heads_in[0].wait_recv()
+        a = block(buf, x_peer, 0, half)
+        first = send(a, a, sems, 2, to_y)
+        heads_in[1].wait_recv()
+        b = block(buf, y_peer, half, half)
+        return first, send(b, b, sems, 3, to_x)
+
+    h_sems, o_sems = (h_send, h_recv), (o_send, o_recv)
+    h_open = open_exchange(hid_ref, hv, h_sems)
+    pars = [send(par.at[h], par.at[h], (a_send, a_recv), k, peer) for k, peer in enumerate(to_heads)]
+
+    closing = []
+    if ring:
+        def w_block(at):
+            return wv.at[pl.ds(pl.multiple_of((2 * at + core) * n, 16), n), :]
+
+        def w_copy(at, sems, target):
+            return remote(w_block(at), w_block(at), sems.at[at], z_recv.at[at], target)
+
+        def w_swap(at):
+            return remote(w_block(at), w_block(at), s_send.at[at], s_recv.at[at], to_sib)
+
+        def launch(there, make):
+            @pl.when(there)
+            def _():
+                make().start()
+
+            def finish():
+                @pl.when(there)
+                def _():
+                    make().wait_send()
+
+            closing.append(finish)
+
+        always = r >= 0
+
+        def w_step(k):
+            lower, upper = r - k, r + k
+            has_lower, has_upper = lower >= 0, upper <= last
+
+            @pl.when(has_lower)
+            def _():
+                w_copy(lower, z_up, to_up).wait_recv()
+
+            launch(has_lower & above, lambda: w_copy(lower, z_up, to_up))
+            launch(has_lower, lambda: w_swap(lower))
+
+            @pl.when(has_upper)
+            def _():
+                w_copy(upper, z_dn, to_down).wait_recv()
+
+            launch(has_upper & below, lambda: w_copy(upper, z_dn, to_down))
+            launch(has_upper, lambda: w_swap(upper))
+
+        chunks = c_recv.shape[0]
+        n_c = n_o // chunks
+        dist = jnp.where(r > s, r - s, s - r)
+        ending = (r == 0) | (r == last)
+
+        def o_block(i):
+            return wov.at[pl.ds(pl.multiple_of(core * n_o + i * n_c, 16), n_c), :]
+
+        def o_copy(i, sems, target):
+            return remote(o_block(i), o_block(i), sems.at[i], c_recv.at[i], target)
+
+        def o_swap(i):
+            return remote(o_block(i), o_block(i), t_send.at[i], t_recv.at[i], to_sib)
+
+        def o_root():
+            @pl.when(is_root)
+            def _():
+                load_o.wait()
+
+            for i in range(chunks):
+                pl.when(is_root & above & (r != 2))(lambda i=i: o_copy(i, c_up, to_up).start())
+                pl.when(is_root & below & (r != 1))(lambda i=i: o_copy(i, c_dn, to_down).start())
+                pl.when(is_root)(lambda i=i: o_swap(i).start())
+
+        def o_root_late():
+            for i in range(chunks):
+                pl.when(is_root & (r == 2))(lambda i=i: o_copy(i, c_up, to_up).start())
+                pl.when(is_root & (r == 1))(lambda i=i: o_copy(i, c_dn, to_down).start())
+
+        def o_tick(t):
+            i = t - dist
+            live = (dist >= 1) & (i >= 0) & (i < chunks) & jnp.logical_not(ending)
+
+            @pl.when(live)
+            def _():
+                o_copy(i, c_up, to_up).wait_recv()
+
+            pl.when(live & (r > s) & above)(lambda: o_copy(i, c_up, to_up).start())
+            pl.when(live & (r < s) & below)(lambda: o_copy(i, c_dn, to_down).start())
+            pl.when(live)(lambda: o_swap(i).start())
+
+        def o_rest():
+            @pl.when(ending & (dist >= 1))
+            def _():
+                for i in range(chunks):
+                    o_copy(i, c_up, to_up).wait_recv()
+                    o_swap(i).start()
+
+        def o_finish():
+            for i in range(chunks):
+                pl.when((r >= s) & above)(lambda: o_copy(i, c_up, to_up).wait_send())
+                pl.when((r <= s) & below)(lambda: o_copy(i, c_dn, to_down).wait_send())
+                o_swap(i).wait_send()
+
+        for copy in loads:
+            copy.wait()
+        own = pl.ds(pl.multiple_of(h * n, 16), n)
+        wv[own, :n_main] = (stage[...].astype(F32) * gain_ref[...].astype(F32)).astype(BF16)
+        shape = (dtw_ref.shape[1], LANES)
+        place = lax.broadcasted_iota(jnp.int32, shape, 1)
+        taken = (lax.broadcasted_iota(jnp.int32, shape, 0) == place + s * heads) & (place < heads)
+        own_dt = dot(dtw_ref[...], jnp.where(taken, 1.0, 0.0).astype(BF16))
+        wv[own, n_main:] = (own_dt * gain_ref[...].astype(F32)).astype(BF16)
+        launch(above, lambda: w_copy(r, z_up, to_up))
+        launch(below, lambda: w_copy(r, z_dn, to_down))
+        launch(always, lambda: w_swap(r))
+        w_step(1)
+
+    rows = min(CHUNK, q)
+
+    def cut(at_block):
+        return pl.ds(pl.multiple_of(at_block * q, 16), q)
+
+    def project_outs(at_block, i):
+        at = cut(at_block)
+        pairs = ((hv, hall_ref), (zv, z_ref), (uv, u_ref))
+        return [
+            pltpu.make_async_copy(src.at[at, :], dst.at[at, :], out_sem.at[3 * i + k])
+            for k, (src, dst) in enumerate(pairs)
+        ]
+
+    act_at, y_at = slice(0, chans), slice(chans, chans + wide)
+    gg_at, d0_at = slice(0, wide), slice(wide, 2 * wide)
+
+    def scan_outs(j):
+        at = pl.ds(pl.multiple_of(j * rows, 16), rows)
+        slot = lax.rem(j, 2)
+        pairs = (
+            (wv.at[at, act_at], act_ref), (wv.at[at, y_at], y_ref), (uv.at[at, :], slope_ref),
+            (dv.at[at, :], aux_ref), (hv.at[at, gg_at], gg_ref),
+        )
+        copies = [pltpu.make_async_copy(src, dst.at[at, :], scan_sem.at[j, k]) for k, (src, dst) in enumerate(pairs)]
+        return copies, pltpu.make_async_copy(st_v.at[slot], st_ref.at[j], st_sem.at[slot])
+
+    def pull_outs(at_block, i):
+        at = cut(at_block)
+        pairs = ((ov.at[at, :], ogall_ref), (hv.at[at, d0_at], d0_ref))
+        return [
+            pltpu.make_async_copy(src, dst.at[at, :], out_sem.at[12 + 2 * i + k])
+            for k, (src, dst) in enumerate(pairs)
+        ]
+
+    def nth(i):
+        return jnp.where(i == 0, s, jnp.where(i == 1, x_peer, jnp.where(i == 2, y_peer, far)))
+
+    w_out = pltpu.make_async_copy(wv, wt_ref, out_sem.at[20])
+    o_out = pltpu.make_async_copy(wov, wo_ref, out_sem.at[21])
+
+    width = wv.shape[0]
+    strip = width // 4
+    late_chip = jnp.where(r < 2, last, 0)
+    early_k = pl.ds(pl.multiple_of(jnp.where(late_chip == 0, strip, 0), strip), 3 * strip)
+    late_k = pl.ds(pl.multiple_of(late_chip * strip, strip), strip)
+
+    def project(at_block, k, ahead):
+        @pl.loop(0, q // rows)
+        def _(j):
+            at = pl.ds(pl.multiple_of(at_block * q + j * rows, 16), rows)
+            hb = hv[at, k]
+            z = dot(hb, wv[k, :wide])
+            u = dot(hb, wv[k, wide : wide + chans])
+            raw = dot(hb, wv[k, wide + chans :])
+            if ahead:
+                zv[at, :] = z.astype(BF16)
+                uv[at, :] = u.astype(BF16)
+                dv[at, :] = raw
+            else:
+                h32 = hv[at, :].astype(F32)
+                r0 = lax.rsqrt(jnp.mean(h32 * h32, axis=1, keepdims=True) + EPS)
+                zv[at, :] = ((z + zv[at, :].astype(F32)) * r0).astype(BF16)
+                uv[at, :] = ((u + uv[at, :].astype(F32)) * r0).astype(BF16)
+                raw = (raw + dv[at, :]) * r0
+                lane = lax.broadcasted_iota(jnp.int32, raw.shape, 1)
+                dv[at, :] = jnp.where(lane == LANES - 1, r0, raw)
+
+    def pull(at_block):
+        at = cut(at_block)
+
+        @pl.loop(0, wide // 256)
+        def _(j):
+            from_o = pl.ds(pl.multiple_of(j * 256, 256), 256)
+            to = pl.ds(pl.multiple_of(wide + j * 256, 256), 256)
+            hv[at, to] = dot_t(ov[at, :], wov[from_o, :]).astype(BF16)
+
+        @pl.loop(0, q // rows)
+        def _(j):
+            some = pl.ds(pl.multiple_of(at_block * q + j * rows, 16), rows)
+            lanes = pl.ds(pl.multiple_of(at_block * q + j * rows, LANES), rows)
+            sum_ref[:, lanes] = with_cross(sum_ref[:, lanes], hv[some, gg_at], hv[some, d0_at])
+
+    h_far = relay(hv, h_sems, h_open)
+    own_h.wait()
+    own_o.wait()
+    for copy in pars:
+        copy.wait_recv()
+    rank_params(par, s, cw_ref, dtb_ref, rowp_ref, colp_ref, heads, wide)
+    w_step(2)
+    o_root()
+    for k in range(1, 4):
+        w_swap(lax.rem(late_chip + k, 4)).wait_recv()
+    project(s, early_k, True)
+    project(x_peer, early_k, True)
+    for copy in h_far:
+        copy.wait_recv()
+    o_open = open_exchange(og_ref, ov, o_sems)
+    o_tick(1)
+
+    @pl.loop(2, 4)
+    def _(i):
+        project(nth(i), early_k, True)
+        o_tick(i)
+
+    o_root_late()
+    w_step(3)
+    w_swap(late_chip).wait_recv()
+    w_out.start()
+
+    @pl.loop(0, 4)
+    def _(i):
+        at_block = nth(i)
+        project(at_block, late_k, False)
+        for copy in project_outs(at_block, i):
+            copy.start()
+        pl.when(i < 3)(lambda: o_tick(4 + i))
+
+    for i, at_block in enumerate((s, x_peer, y_peer, far)):
+        for copy in project_outs(at_block, i):
+            copy.wait()
+    w_out.wait()
+    for copy in h_far:
+        copy.wait_send()
+    sent[:] = [copy for copy in sent if copy is not h_far[0] and copy is not h_far[1]]
+    for finish in closing:
+        finish()
+    o_a, o_b = block(ov, x_peer, 0, half), block(ov, y_peer, half, half)
+    o_far = [
+        remote(o_a, o_a, o_send.at[2], o_recv.at[2], to_y),
+        remote(o_b, o_b, o_send.at[3], o_recv.at[3], to_x),
+    ]
+    sent += o_far
+    state[...] = jnp.zeros_like(state)
+    ext[...] = jnp.zeros_like(ext)
+    expand = head_matrix(wide)
+    steps = 4 * q // rows
+
+    @pl.loop(0, steps)
+    def _(j):
+        at = pl.ds(pl.multiple_of(j * rows, 16), rows)
+        slot = lax.rem(j, 2)
+
+        @pl.when(j >= 2)
+        def _():
+            scan_outs(j - 2)[1].wait()
+
+        @pl.when(j == steps - 2)
+        def _():
+            for opened, copy in zip(o_open, o_far):
+                opened.wait_recv()
+                copy.start()
+
+        act, slope, aux, y16, gg, ssq = scan_chunk(
+            uv[at, :], dv[at, :], zv[at, :], cw_ref[0:KERNEL, :], cw_ref[KERNEL : KERNEL + 1, :], dtb_ref[0:1, :],
+            expand, rowp_ref[...], colp_ref[:, 0:1], state, ext, st_v.at[slot], heads,
+        )
+        wv[at, act_at] = act
+        wv[at, y_at] = y16
+        uv[at, :] = slope
+        dv[at, :] = aux
+        hv[at, gg_at] = gg
+        sum_ref[:, pl.ds(pl.multiple_of(j * rows, LANES), rows)] = ssq
+        copies, st_copy = scan_outs(j)
+        for copy in copies:
+            copy.start()
+        st_copy.start()
+        pl.when(lax.rem(j, 2) == 0)(lambda: o_tick(7 + j // 2))
+
+    o_rest()
+    for i in range(chunks):
+        o_swap(i).wait_recv()
+    o_out.start()
+
+    @pl.loop(0, 4)
+    def _(i):
+        at_block = nth(i)
+
+        @pl.when(i == 3)
+        def _():
+            for copy in o_far:
+                copy.wait_recv()
+
+        pull(at_block)
+        for copy in pull_outs(at_block, i):
+            copy.start()
+
+    for i, at_block in enumerate((s, x_peer, y_peer, far)):
+        for copy in pull_outs(at_block, i):
+            copy.wait()
+
+    @pl.loop(0, steps)
+    def _(j):
+        for copy in scan_outs(j)[0]:
+            copy.wait()
+
+    for j in (steps - 2, steps - 1):
+        scan_outs(j)[1].wait()
+    o_out.wait()
+    for copy in sent:
+        copy.wait_send()
+    o_finish()
 
 
 def line_sum(own, z_u, z_d, sems, r, last, to_up, to_down, join, closing):
@@ -603,6 +777,29 @@
     load_h(0).start()
     load_h(1).start()
     load_gg.wait()
+    load_wo.wait()
+
+    def part(block, out):
+        @pl.loop(0, q // rows)
+        def _(j):
+            at = pl.ds(pl.multiple_of(block * q + j * rows, 16), rows)
+            to = pl.ds(pl.multiple_of(j * rows, 16), rows)
+            out[to, :] = dot(ggv[at, :], wov[...]).astype(BF16)
+
+    def d_copy(src, dst, i, target):
+        copy = remote(src, dst, d_send.at[i], d_recv.at[i], target)
+        copy.start()
+        return copy
+
+    part(far, far_p)
+    d0 = d_copy(far_p.at[:half], far_a, 0, to_x)
+    d1 = d_copy(far_p.at[half:], far_b, 1, to_y)
+    part(y_peer, y_p)
+    d2 = d_copy(y_p.at[half:], y_f.at[half:], 2, to_y)
+    part(x_peer, x_p)
+    d3 = d_copy(x_p.at[:half], x_f.at[:half], 3, to_x)
+    part(s, own_p)
+
     for copy in sums:
         copy.wait_recv()
     total = (sv[0] + sv[1]) + (sv[2] + sv[3])
@@ -616,29 +813,6 @@
     def _(j):
         at = pl.ds(pl.multiple_of(j * rows, 16), rows)
         ggv[at, :] = (ggv[at, :].astype(F32) * stat_v[at, 0:1]).astype(BF16)
-
-    load_wo.wait()
-
-    def part(block, out):
-        @pl.loop(0, q // rows)
-        def _(j):
-            at = pl.ds(pl.multiple_of(block * q + j * rows, 16), rows)
-            to = pl.ds(pl.multiple_of(j * rows, 16), rows)
-            out[to, :] = dot(ggv[at, :], wov[...]).astype(BF16)
-
-    def d_copy(src, dst, i, target):
-        copy = remote(src, dst, d_send.at[i], d_recv.at[i], target)
-        copy.start()
-        return copy
-
-    part(far, far_p)
-    d0 = d_copy(far_p.at[:half], far_a, 0, to_x)
-    d1 = d_copy(far_p.at[half:], far_b, 1, to_y)
-    part(y_peer, y_p)
-    d2 = d_copy(y_p.at[half:], y_f.at[half:], 2, to_y)
-    part(x_peer, x_p)
-    d3 = d_copy(x_p.at[:half], x_f.at[:half], 3, to_x)
-    part(s, own_p)
 
     def w_rows(d):
         to = slice(d * cut, (d + 1) * cut)
@@ -755,7 +929,13 @@
         wog_out.start()
     for copy in (d2, d3, d4, d5):
         copy.wait_recv()
-    own_p[...] = (own_p[...].astype(F32) + y_f[...].astype(F32) + x_f[...].astype(F32)).astype(BF16)
+
+    @pl.loop(0, q // 128)
+    def _(j):
+        at = pl.ds(pl.multiple_of(j * 128, 128), 128)
+        whole = own_p[at, :].astype(F32) + y_f[at, :].astype(F32) + x_f[at, :].astype(F32)
+        own_p[at, :] = (whole * stat_v[pl.ds(pl.multiple_of(s * q + j * 128, 128), 128), 0:1]).astype(BF16)
+
     br_out = pltpu.make_async_copy(own_p, br_ref, out_sem.at[2])
     br_out.start()
     for i in (chunks - 2, chunks - 1):
@@ -775,8 +955,8 @@
 
 def back_kernel(
     act_ref, aux_ref, dy_ref, y_ref, st_ref, slope_ref, u_ref, piece_ref,
-    exp_ref, seg_ref, rowp_ref, colp_ref, cw_ref,
-    dp_ref, sm_ref, all_ref, adj, ext, b_send, b_recv, b_load, *, heads, wide, ring,
+    rowp_ref, colp_ref, cw_ref,
+    dp_ref, sm_ref, all_ref, adj, ext, exp_v, seg_v, b_send, b_recv, b_load, *, heads, wide, ring,
 ):
     step = pl.program_id(0)
     steps = pl.num_programs(0)
@@ -815,6 +995,8 @@
     def _():
         sm_ref[...] = jnp.zeros_like(sm_ref)
         adj[...] = jnp.zeros_like(adj)
+        exp_v[...] = head_matrix(wide)
+        seg_v[...] = head_matrix(wide, True)
         ext[...] = jnp.zeros_like(ext)
 
     x = act_ref[:, :wide]
@@ -829,7 +1011,7 @@
     dy = dy16.astype(F32)
 
     causal, dt_e, cum_e, cum_c, cum_t = decays(
-        aux, heads, exp_ref[...], rowp_ref[0:1, :], rowp_ref[3:4, :LANES], colp_ref[:, 0:1]
+        aux, heads, exp_v[...], rowp_ref[0:1, :], rowp_ref[3:4, :LANES], colp_ref[:, 0:1]
     )
     xdt = x32 * dt_e
     xdt16 = xdt.astype(BF16)
@@ -878,7 +1060,7 @@
     elast = jnp.exp(last)
     adj[...] = elast * q_in + t_dot(c, dy_e)
 
-    seg = seg_ref[...]
+    seg = seg_v[...]
     flow = dy * y - xdt16.astype(F32) * v
     passed = jnp.sum(xdt16.astype(F32) * out_part, axis=0, keepdims=True)
     passed = passed + elast * jnp.sum(q_in * st, axis=0, keepdims=True)
@@ -894,7 +1076,7 @@
     crossing = dot(upper, hi) + dot(upper, mid) + dot(upper, low) + passed_h
     rate_row = rowp_ref[3:4, :LANES]
     decay_grad = rate_row * crossing
-    d_dt = seg_dot(x32 * v, seg) + decay_grad
+    d_dt = dot((x32 * v).astype(BF16), seg) + decay_grad
     lane = lax.broadcasted_iota(jnp.int32, (rows, LANES), 1)
     sig_v = pltpu.roll(aux, LANES - heads, 1)
     d_pre = jnp.where(lane < heads, d_dt * sig_v, 0.0)
@@ -931,9 +1113,9 @@
 
 
 def grads_kernel(
-    dpg_ref, dp_ref, w_ref, h_ref, gate_ref, piece_ref, tiny_ref,
+    dpg_ref, dp_ref, w_ref, h_ref, gate_ref, piece_ref, sm_ref,
     dn_ref, wing_ref, win_ref, wout_ref,
-    dpv, wv, hb, far_p, y_p, x_p, far_a, far_b, y_f, x_f, sib_s, mine_s, own_s, z_u, z_d,
+    dpv, wv, hb, tiny_f, tiny_v, far_p, y_p, x_p, far_a, far_b, y_f, x_f, sib_s, mine_s, own_s, z_u, z_d,
     load_sem, hb_sem, d_send, d_recv, s_send, s_recv, zu_send, zu_recv, zd_send, zd_recv,
     g_send, g_recv, k_send, k_recv, p_send, p_recv, out_sem,
 ):
@@ -1000,6 +1182,11 @@
 
     load_h(0, True).start()
     load_h(0, False).start()
+
+    tiny_f[...] = jnp.zeros_like(tiny_f)
+    for k in range(sm_ref.shape[1] // spare):
+        tiny_f[8 * k : 8 * k + 8, :] = sm_ref[:, spare * k : spare * (k + 1)]
+    tiny_v[...] = tiny_f[...].astype(BF16)
     to_heads = [{"head": lax.rem(h + k, owners)} for k in range(1, owners)]
     greet([to_x, to_y] + to_heads)
 
@@ -1037,7 +1224,7 @@
         load_h(i, True).wait()
         for lo, hi in spans:
             sib_s[slot, :, lo:hi] = t_dot(hb[0], dpv[:, skip + lo : skip + hi]).astype(BF16)
-        sib_s[slot, :, cols - spare :] = tiny_ref[...]
+        sib_s[slot, :, cols - spare :] = tiny_v[...]
         swap(i).start()
 
         @pl.when(i < 3)
@@ -1047,7 +1234,7 @@
         load_h(i, False).wait()
         for lo, hi in spans:
             mine_s[:, lo:hi] = t_dot(hb[1], dpv[:, skip + lo : skip + hi]).astype(BF16)
-        mine_s[:, cols - spare :] = tiny_ref[...]
+        mine_s[:, cols - spare :] = tiny_v[...]
 
         @pl.when(i < 3)
         def _():
@@ -1145,13 +1332,26 @@
 
 
 def finish_kernel(
-    gate_ref, rest_ref, w_ref, dtw_ref, gain_ref, wog_ref, wo_ref, ggain_ref, hid_ref, og_ref, dn_ref, br_ref,
+    gate_ref, rest_ref, w_ref, dtw_ref, gain_ref, wog_ref, wo_ref, hid_ref, og_ref, dn_ref, br_ref,
     win_ref, wdt_ref, norm_ref, wout_ref, gg_ref, blk_ref, hg_ref, *, heads, wide,
 ):
     ranks = gate_ref.shape[0]
     wog = wog_ref[...].astype(F32)
     wout_ref[...] = wog
-    gg_ref[...] = jnp.sum(wog * wo_ref[...].astype(F32), axis=1, keepdims=True) / ggain_ref[...]
+    step = pl.program_id(0)
+
+    @pl.when(step == 0)
+    def _():
+        gg_ref[...] = jnp.zeros_like(gg_ref)
+        norm_ref[...] = jnp.zeros_like(norm_ref)
+
+    def lay(ref, col):
+        shape = (col.shape[0], ref.shape[1])
+        place = lax.broadcasted_iota(jnp.int32, shape, 0) + step * col.shape[0]
+        there = lax.broadcasted_iota(jnp.int32, shape, 1) == place
+        ref[...] += jnp.sum(jnp.where(there, col, 0.0), axis=0, keepdims=True)
+
+    lay(gg_ref, jnp.sum(wog * wo_ref[...].astype(F32), axis=1, keepdims=True))
     h32 = hid_ref[...].astype(F32)
     blk_ref[...] = (h32 + br_ref[...].astype(F32)).astype(BF16)
     dn = dn_ref[...].astype(F32)
@@ -1160,7 +1360,7 @@
     mixed = jnp.sum(dn * h32, axis=1, keepdims=True) / count
     hg_ref[...] = og_ref[...].astype(F32) + dn - h32 * (r0 * r0 * mixed)
 
-    gain = gain_ref[...]
+    gain = gain_ref[...].astype(F32)
     norm = None
 
     def piece(at, raw):
@@ -1179,7 +1379,7 @@
     norm = norm + piece(2 * DI, shared)
     raw = jnp.concatenate(dt_parts, axis=1)
     wdt_ref[...] = raw * gain
-    norm_ref[...] = norm + jnp.sum(raw * dtw_ref[...].astype(F32), axis=1, keepdims=True)
+    lay(norm_ref, norm + jnp.sum(raw * dtw_ref[...].astype(F32), axis=1, keepdims=True))
 
 
 def local(hidden, lengths, out_grad, norm_gain, w_in, w_dt, conv_weight, conv_bias, dt_bias, a_log, skip_gain, gate_gain, w_out):
@@ -1197,168 +1397,161 @@
     steps = tokens // chunk
     shard = w_in.shape[0]
 
-    gain_rows = norm_gain.astype(F32)[:, None]
+    gain_rows = norm_gain[:, None]
 
     def scaled(v):
-        return (v.astype(F32) * gain_rows).astype(BF16)
+        return (v.astype(F32) * gain_rows.astype(F32)).astype(BF16)
 
     spare = LANES // 2
-    small = jnp.concatenate([conv_weight.reshape(-1), conv_bias, dt_bias, a_log, skip_gain, gate_gain])
-    n_small = small.shape[0]
-    small = jnp.pad(small, (0, shard * spare - n_small)).reshape(shard, spare)
-    last_block = jnp.concatenate(
-        [
-            scaled(lax.dynamic_slice_in_dim(w_dt, rank * heads, heads, 1)),
-            jnp.zeros((shard, LANES - spare - heads), BF16),
-            small,
-        ],
-        axis=1,
+    ring = owners == 2 * ranks
+
+    def sds(shape, kind):
+        return jax.ShapeDtypeStruct(shape, kind)
+
+    hbm = pl.BlockSpec(memory_space=pl.ANY)
+    vmem = pl.BlockSpec(memory_space=pltpu.VMEM)
+
+    def dma(count):
+        return pltpu.SemaphoreType.DMA((count,))
+
+    def forth(size):
+        return pl.BlockSpec((chunk, size), lambda j: (j, 0))
+
+    def back(size):
+        return pl.BlockSpec((chunk, size), lambda j: (steps - 1 - j, 0))
+
+    def whole(a):
+        return pl.BlockSpec(a.shape, lambda j: (0,) * a.ndim, pipeline_mode=pl.Buffered(1))
+
+    params = pltpu.CompilerParams(
+        dimension_semantics=("arbitrary",), vmem_limit_bytes=56 * 1024 * 1024
     )
-    ring = owners == 2 * ranks
+    grid = (steps,)
+    cs = CHANNELS // owners
+    hs = HEADS // owners
+    scan_out = [
+        sds((tokens, chans), BF16),
+        sds((tokens, chans), BF16),
+        sds((tokens, LANES), F32),
+        sds((tokens, wide), BF16),
+        sds((tokens, wide), BF16),
+        sds((steps, STATE, wide), F32),
+        sds((8, tokens), F32),
+    ]
+
     if ring:
-        w_given, o_given = w_in, w_out
+        lanes = -(-max(cs, DI // owners) // LANES) * LANES
+
+        (
+            h_all, og_all, w_t, w_o, z, u, d0, act, slope, aux, y, gg, states, sums, cw, dtb, rowp, colp,
+        ) = pl.pallas_call(
+            functools.partial(gather_kernel, heads=heads, wide=wide),
+            in_specs=[hbm] * 4 + [vmem] * 6,
+            out_specs=[hbm] * 13 + [vmem] * 5,
+            out_shape=[
+                sds((tokens, width), BF16),
+                sds((tokens, width), BF16),
+                sds((width, cols), BF16),
+                sds((wide, width), BF16),
+                sds((tokens, wide), BF16),
+                sds((tokens, chans), BF16),
+                sds((tokens, wide), BF16),
+            ]
+            + scan_out
+            + [sds((16, chans), F32), sds((8, LANES), F32), sds((8, wide), F32), sds((LANES, LANES), F32)],
+            scratch_shapes=[
+                pltpu.VMEM((tokens, width), BF16),
+                pltpu.VMEM((tokens, width), BF16),
+                pltpu.VMEM((width, cols), BF16),
+                pltpu.VMEM((wide, width), BF16),
+                pltpu.VMEM((shard, cols - LANES), BF16),
+                pltpu.VMEM((tokens, wide), BF16),
+                pltpu.VMEM((tokens, chans), BF16),
+                pltpu.VMEM((tokens, LANES), F32),
+                pltpu.VMEM((owners, 16, lanes), BF16),
+                pltpu.VMEM((16, lanes), F32),
+                pltpu.VMEM((STATE, wide), F32),
+                pltpu.VMEM((16, chans), F32),
+                pltpu.VMEM((2, STATE, wide), F32),
+            ]
+            + [dma(4)] * 9
+            + [dma(8)] * 5
+            + [dma(owners)] * 2
+            + [dma(6), dma(22), pltpu.SemaphoreType.DMA((steps, 5)), dma(2)],
+            compiler_params=pltpu.CompilerParams(
+                collective_id=0, has_side_effects=True, vmem_limit_bytes=56 * 1024 * 1024
+            ),
+            cost_estimate=pl.CostEstimate(
+                flops=2 * tokens * width * (cols + wide), bytes_accessed=4 * tokens * (width + cols), transcendentals=0
+            ),
+            name="gather_scan",
+        )(
+            hidden[0], out_grad[0], w_in, w_out, gain_rows, w_dt, conv_weight, conv_bias[None], gate_gain[None],
+            jnp.concatenate([dt_bias, a_log, skip_gain])[None],
+        )
     else:
-        w_given = lax.all_gather(
+        dt_block = jnp.pad(scaled(lax.dynamic_slice_in_dim(w_dt, rank * heads, heads, 1)), ((0, 0), (0, LANES - heads)))
+        w_t = lax.all_gather(
             jnp.concatenate(
                 [
                     scaled(lax.dynamic_slice_in_dim(w_in, rank * wide, wide, 1)),
                     scaled(lax.dynamic_slice_in_dim(w_in, DI + rank * wide, wide, 1)),
                     scaled(w_in[:, 2 * DI :]),
-                    last_block,
+                    dt_block,
                 ],
                 axis=1,
             ),
             "head", axis=0, tiled=True,
         )
-        o_given = lax.dynamic_slice_in_dim(lax.all_gather(w_out, "head", axis=0, tiled=True), rank * wide, wide, 0)
-
-    def sds(shape, kind):
-        return jax.ShapeDtypeStruct(shape, kind)
-
-    hbm = pl.BlockSpec(memory_space=pl.ANY)
-    vmem = pl.BlockSpec(memory_space=pltpu.VMEM)
-
-    def dma(count):
-        return pltpu.SemaphoreType.DMA((count,))
-
-    h_all, og_all, w_t, w_o, z, u, d_raw, d0 = pl.pallas_call(
-        functools.partial(gather_kernel, ring=ring, wide=wide),
-        in_specs=[hbm, hbm, hbm, hbm, vmem, vmem],
-        out_specs=[hbm] * 8,
-        out_shape=[
-            sds((tokens, width), BF16),
-            sds((tokens, width), BF16),
-            sds((width, cols), BF16),
-            sds((wide, width), BF16),
-            sds((tokens, wide), BF16),
-            sds((tokens, chans), BF16),
-            sds((tokens, LANES), F32),
-            sds((tokens, wide), BF16),
-        ],
-        scratch_shapes=[
-            pltpu.VMEM((tokens, width), BF16),
-            pltpu.VMEM((tokens, width), BF16),
-            pltpu.VMEM((width, cols), BF16),
-            pltpu.VMEM((wide, width), BF16),
-            pltpu.VMEM((shard, cols - LANES), BF16),
-            pltpu.VMEM((tokens, wide), BF16),
-            pltpu.VMEM((tokens, chans), BF16),
-            pltpu.VMEM((tokens, LANES), F32),
-            pltpu.VMEM((tokens, wide), BF16),
-        ]
-        + [dma(4)] * 9
-        + [dma(8)] * 5
-        + [dma(6), dma(26)],
-        compiler_params=pltpu.CompilerParams(
-            collective_id=0, has_side_effects=True, vmem_limit_bytes=56 * 1024 * 1024
-        ),
-        cost_estimate=pl.CostEstimate(
-            flops=2 * tokens * width * (cols + wide), bytes_accessed=4 * tokens * (width + cols), transcendentals=0
-        ),
-        name="gather_project",
-    )(hidden[0], out_grad[0], w_given, o_given, gain_rows, last_block)
-
-    small = w_t.reshape(owners, shard, cols)[:, :, cols - spare :].reshape(owners, shard * spare)
-    cs = CHANNELS // owners
-    hs = HEADS // owners
-    gs = DI // owners
-    conv_w = small[:, : KERNEL * cs].reshape(owners, KERNEL, cs).swapaxes(0, 1).reshape(KERNEL, CHANNELS)
-    at = KERNEL * cs
-    conv_b = small[:, at : at + cs].reshape(CHANNELS)
-    at += cs
-    dt_b = small[:, at : at + hs].reshape(HEADS)
-    at += hs
-    a_all = small[:, at : at + hs].reshape(HEADS)
-    at += hs
-    skip_all = small[:, at : at + hs].reshape(HEADS)
-    at += hs
-    gain_all = small[:, at : at + gs].reshape(DI)
-
-    def mine(v, size):
-        return lax.dynamic_slice_in_dim(v, rank * size, size, v.ndim - 1)
-
-    cw = jnp.concatenate([mine(conv_w[:, :DI], wide), conv_w[:, DI:]], axis=1).astype(F32)
-    cb = jnp.concatenate([mine(conv_b[:DI], wide), conv_b[DI:]])[None].astype(F32)
-    cw = jnp.concatenate([cw, jnp.zeros((8 - KERNEL, chans), F32)], axis=0)
-    cb = jnp.broadcast_to(cb, (8, chans))
-    dtb = jnp.broadcast_to(jnp.pad(mine(dt_b, heads).astype(F32), (0, LANES - heads))[None], (8, LANES))
-    rate = -jnp.exp(mine(a_all, heads).astype(F32))
-    rowp = jnp.stack(
-        [
-            jnp.repeat(rate, HEAD_DIM),
-            jnp.repeat(mine(skip_all, heads).astype(F32), HEAD_DIM),
-            mine(gain_all, wide).astype(F32),
-            jnp.pad(rate, (0, wide - heads)),
-        ]
-        + [jnp.zeros((wide,), F32)] * 4
-    )
-    colp = jnp.broadcast_to(jnp.pad(rate, (0, LANES - heads))[:, None], (LANES, LANES))
-    head_of = jnp.arange(wide, dtype=jnp.int32) // HEAD_DIM
-    expand = (jnp.arange(LANES, dtype=jnp.int32)[:, None] == head_of[None]).astype(BF16)
-    seg = expand.T
-
-    def forth(size):
-        return pl.BlockSpec((chunk, size), lambda j: (j, 0))
-
-    def back(size):
-        return pl.BlockSpec((chunk, size), lambda j: (steps - 1 - j, 0))
-
-    def whole(a):
-        return pl.BlockSpec(a.shape, lambda j: (0,) * a.ndim, pipeline_mode=pl.Buffered(1))
-
-    params = pltpu.CompilerParams(
-        dimension_semantics=("arbitrary",), vmem_limit_bytes=56 * 1024 * 1024
-    )
-    grid = (steps,)
-
-    act, slope, aux, y, gg, states, sums = pl.pallas_call(
-        functools.partial(scan_kernel, heads=heads, wide=wide),
-        grid=grid,
-        in_specs=[
-            forth(chans), forth(LANES), forth(wide), forth(wide),
-            whole(cw), whole(cb), whole(dtb), whole(expand), whole(rowp), whole(colp),
-        ],
-        out_specs=[
-            forth(chans), forth(chans), forth(LANES), forth(wide), forth(wide),
-            pl.BlockSpec((1, STATE, wide), lambda j: (j, 0, 0)),
-            pl.BlockSpec((8, chunk), lambda j: (0, j)),
-        ],
-        out_shape=[
-            sds((tokens, chans), BF16),
-            sds((tokens, chans), BF16),
-            sds((tokens, LANES), F32),
-            sds((tokens, wide), BF16),
-            sds((tokens, wide), BF16),
-            sds((steps, STATE, wide), F32),
-            sds((8, tokens), F32),
-        ],
-        scratch_shapes=[pltpu.VMEM((STATE, wide), F32), pltpu.VMEM((16, chans), F32)],
-        compiler_params=params,
-        cost_estimate=pl.CostEstimate(
-            flops=2 * tokens * wide * 12 * chunk, bytes_accessed=tokens * wide * 16, transcendentals=tokens * chunk * heads
-        ),
-        name="scan",
-    )(u, d_raw, z, d0, cw, cb, dtb, expand, rowp, colp)
+        w_o = lax.dynamic_slice_in_dim(lax.all_gather(w_out, "head", axis=0, tiled=True), rank * wide, wide, 0)
+        h_all = lax.all_gather(hidden[0], "seq", axis=0, tiled=True)
+        og_all = lax.all_gather(out_grad[0], "seq", axis=0, tiled=True)
+        h32 = h_all.astype(F32)
+        r0 = lax.rsqrt(jnp.mean(h32 * h32, axis=1, keepdims=True) + EPS)
+        projected = dot(h_all, w_t) * r0
+        z = projected[:, :wide].astype(BF16)
+        u = projected[:, wide : wide + chans].astype(BF16)
+        d_raw = jnp.concatenate([projected[:, wide + chans : cols - 1], r0], axis=1)
+        d0 = dot_t(og_all, w_o).astype(BF16)
+
+        def mine(v, size):
+            return lax.dynamic_slice_in_dim(v, rank * size, size, v.ndim - 1)
+
+        conv_w = lax.all_gather(conv_weight, "head", axis=1, tiled=True)
+        conv_b = lax.all_gather(conv_bias, "head", axis=0, tiled=True)
+        cw = jnp.concatenate([conv_w, conv_b[None]], axis=0)
+        cw = jnp.concatenate([mine(cw[:, :DI], wide), cw[:, DI:]], axis=1).astype(F32)
+        cw = jnp.pad(cw, ((0, 16 - KERNEL - 1), (0, 0)))
+        rate = -jnp.exp(mine(lax.all_gather(a_log, "head", axis=0, tiled=True), heads).astype(F32))
+        dtb = jnp.pad(mine(lax.all_gather(dt_bias, "head", axis=0, tiled=True), heads).astype(F32), (0, LANES - heads))
+        dtb = jnp.broadcast_to(dtb[None], (8, LANES))
+        rowp = jnp.stack(
+            [
+                jnp.repeat(rate, HEAD_DIM),
+                jnp.repeat(mine(lax.all_gather(skip_gain, "head", axis=0, tiled=True), heads).astype(F32), HEAD_DIM),
+                mine(lax.all_gather(gate_gain, "head", axis=0, tiled=True), wide).astype(F32),
+                jnp.pad(rate, (0, wide - heads)),
+            ]
+            + [jnp.zeros((wide,), F32)] * 4
+        )
+        colp = jnp.broadcast_to(jnp.pad(rate, (0, LANES - heads))[:, None], (LANES, LANES))
+        act, slope, aux, y, gg, states, sums = pl.pallas_call(
+            functools.partial(scan_kernel, heads=heads),
+            grid=grid,
+            in_specs=[
+                forth(chans), forth(LANES), forth(wide), forth(wide),
+                whole(cw), whole(dtb), whole(rowp), whole(colp),
+            ],
+            out_specs=[
+                forth(chans), forth(chans), forth(LANES), forth(wide), forth(wide),
+                pl.BlockSpec((1, STATE, wide), lambda j: (j, 0, 0)),
+                pl.BlockSpec((8, chunk), lambda j: (0, j)),
+            ],
+            out_shape=scan_out,
+            scratch_shapes=[pltpu.VMEM((STATE, wide), F32), pltpu.VMEM((16, chans), F32)],
+            compiler_params=params,
+            name="scan",
+        )(u, d_raw, z, d0, cw, dtb, rowp, colp)
 
     mask = (jnp.arange(tokens, dtype=jnp.int32) < lengths[0]).astype(F32)
     n_own = DI // owners
@@ -1422,11 +1615,16 @@
             back(chans), back(LANES), back(wide), back(wide),
             pl.BlockSpec((1, STATE, wide), lambda j: (steps - 1 - j, 0, 0)),
             back(chans), back(chans), hbm,
-            whole(expand), whole(seg), whole(rowp), whole(colp), whole(cw),
+            whole(rowp), whole(colp), whole(cw),
         ],
         out_specs=[back(rest), pl.BlockSpec((8, chans), lambda j: (0, 0)), hbm],
         out_shape=[sds((tokens, rest), BF16), sds((8, chans), F32), sds((ranks,) + wog_shape, BF16)],
-        scratch_shapes=[pltpu.VMEM((STATE, wide), F32), pltpu.VMEM((16, chans), F32)]
+        scratch_shapes=[
+            pltpu.VMEM((STATE, wide), F32),
+            pltpu.VMEM((16, chans), F32),
+            pltpu.VMEM((LANES, wide), BF16),
+            pltpu.VMEM((wide, LANES), BF16),
+        ]
         + [dma(4)] * 2
         + [dma(1)],
         compiler_params=pltpu.CompilerParams(
@@ -1439,12 +1637,9 @@
             flops=2 * tokens * wide * 12 * chunk, bytes_accessed=tokens * wide * 24, transcendentals=tokens * chunk * heads
         ),
         name="scan_back",
-    )(act, aux, dy, y, states, slope, u, wog, expand, seg, rowp, colp, cw)
-
-    skip_h = jnp.sum(sm[5, :wide].reshape(heads, HEAD_DIM), axis=1)
-    tiny = jnp.concatenate([sm[:5].reshape(-1), sm[6, :heads], sm[7, :heads], skip_h])
+    )(act, aux, dy, y, states, slope, u, wog, rowp, colp, cw)
+
     if ring:
-        laid = jnp.pad(tiny, (0, shard * spare - tiny.shape[0])).reshape(shard, spare).astype(BF16)
         dn, gate_rows, rest_rows, w_out_grad = pl.pallas_call(
             grads_kernel,
             in_specs=[hbm] * 6 + [vmem],
@@ -1459,6 +1654,8 @@
                 pltpu.VMEM((tokens, cols), BF16),
                 pltpu.VMEM((width, cols), BF16),
                 pltpu.VMEM((2, tokens, shard), BF16),
+                pltpu.VMEM((shard, spare), F32),
+                pltpu.VMEM((shard, spare), BF16),
             ]
             + [pltpu.VMEM((local_len, width), BF16)] * 3
             + [pltpu.VMEM((local_len // 2, width), BF16)] * 2
@@ -1482,9 +1679,11 @@
                 flops=4 * tokens * width * cols, bytes_accessed=8 * tokens * cols, transcendentals=0
             ),
             name="weight_grads",
-        )(dpg, dp, w_t, h_all, own_gate, pieces, laid)
+        )(dpg, dp, w_t, h_all, own_gate, pieces, sm)
         w_out_grad = w_out_grad.reshape(n_own, width)
-        tiny_all = rest_rows[:, :, rest - spare :].reshape(ranks, shard * spare)[:, : tiny.shape[0]].astype(F32)
+        groups = chans // spare
+        tiny_all = rest_rows[:, : 8 * groups, rest - spare :].astype(F32).reshape(ranks, groups, 8, spare)
+        tiny_all = tiny_all.swapaxes(1, 2).reshape(ranks, 8, chans)
     else:
         full = lax.all_gather(lax.psum(wog, "head"), "seq", axis=0, tiled=True)
         w_out_grad = lax.dynamic_slice_in_dim(full, owner * n_own, n_own, 0)
@@ -1493,7 +1692,7 @@
         dn = lax.psum_scatter(dn, "seq", scatter_dimension=0, tiled=True)
         gate_rows = lax.all_gather(own_gate, "seq")
         rest_rows = lax.all_gather(lax.psum_scatter(wig, "head", scatter_dimension=0, tiled=True), "seq")
-        tiny_all = lax.all_gather(lax.psum(tiny, "head"), "seq")
+        tiny_all = lax.all_gather(lax.psum(sm, "head"), "seq")
     strips = min(8, shard // 16)
 
     def strip(total, size):
@@ -1507,19 +1706,20 @@
         grid=(strips,),
         in_specs=[
             ranks_strip(wide), ranks_strip(rest), strip(shard, PROJ), strip(shard, HEADS), strip(shard, 1),
-            strip(n_own, width), strip(n_own, width), strip(n_own, 1),
+            strip(n_own, width), strip(n_own, width),
             strip(local_len, width), strip(local_len, width), strip(local_len, width), strip(local_len, width),
         ],
         out_specs=[
-            strip(shard, PROJ), strip(shard, HEADS), strip(shard, 1), strip(n_own, width), strip(n_own, 1),
+            strip(shard, PROJ), strip(shard, HEADS), pl.BlockSpec((1, shard), lambda j: (0, 0)),
+            strip(n_own, width), pl.BlockSpec((1, n_own), lambda j: (0, 0)),
             strip(local_len, width), strip(local_len, width),
         ],
         out_shape=[
             sds((shard, PROJ), F32),
             sds((shard, HEADS), F32),
-            sds((shard, 1), F32),
+            sds((1, shard), F32),
             sds((n_own, width), F32),
-            sds((n_own, 1), F32),
+            sds((1, n_own), F32),
             sds((local_len, width), BF16),
             sds((local_len, width), F32),
         ],
@@ -1527,16 +1727,15 @@
         cost_estimate=pl.CostEstimate(flops=6 * shard * PROJ, bytes_accessed=16 * shard * PROJ, transcendentals=0),
         name="finish",
     )(
-        gate_rows, rest_rows, w_in, w_dt, gain_rows, w_out_grad, w_out, gate_gain.astype(F32)[:, None],
+        gate_rows, rest_rows, w_in, w_dt, gain_rows, w_out_grad, w_out,
         hidden[0], out_grad[0], dn, branch,
     )
 
-    n_conv = 5 * chans
-    conv_all = tiny_all[:, :n_conv].reshape(ranks, 5, chans)
     conv_all = jnp.concatenate(
-        [conv_all[:, :, :wide].swapaxes(0, 1).reshape(5, DI), jnp.sum(conv_all[:, :, wide:], axis=0)], axis=1
+        [tiny_all[:, :5, :wide].swapaxes(0, 1).reshape(5, DI), jnp.sum(tiny_all[:, :5, wide:], axis=0)], axis=1
     )
-    vec = tiny_all[:, n_conv:].reshape(ranks, 3, heads).swapaxes(0, 1).reshape(3, HEADS)
+    skip_all = jnp.sum(tiny_all[:, 5, :wide].reshape(ranks, heads, HEAD_DIM), axis=2)
+    vec = jnp.stack([tiny_all[:, 6, :heads], tiny_all[:, 7, :heads], skip_all]).reshape(3, HEADS)
     conv_own = lax.dynamic_slice_in_dim(conv_all, owner * cs, cs, 1)
     vec_own = lax.dynamic_slice_in_dim(vec, owner * hs, hs, 1)
 
@@ -1551,7 +1750,7 @@
         vec_own[0],
         vec_own[1],
         vec_own[2],
-        gate_gain_grad.reshape(n_own),
+        gate_gain_grad.reshape(n_own) / gate_gain.astype(F32),
         w_out_grad,
     )
 

time: 508 us -> 463 us (0.911)
  the two profiles are of different devices: /device:TPU:8 before, /device:TPU:0 now
where the time goes in v6:
time: 463 us; the launch traced here: 454 us
  Pallas kernels  422 us (91%)
  between operations  15.2 us (3%)
  local copies, waits for them, and re-layouts  10.1 us (2%)
    pallas_call x1, Pallas kernels, local(): pl.pallas_call(functools.partial(gather_kernel, heads=heads, wide=wide),...  157 us
    pallas_call x1, Pallas kernels, local(): pl.pallas_call(grads_kernel, in_specs=[hbm] * 6 + [vmem], out_specs=[hbm]...  120 us
    pallas_call x1, Pallas kernels, local(): pl.pallas_call(functools.partial(mid_kernel, ring=ring), in_specs=[hbm] *...  82.6 us
    pallas_call x1, Pallas kernels, local(): pl.pallas_call(functools.partial(back_kernel, heads=heads, wide=wide, rin...  46.5 us
    pallas_call x1, Pallas kernels, local(): pl.pallas_call(functools.partial(finish_kernel, heads=heads, wide=wide),...  16.7 us
  transfers between devices with their start and end apart: 1, of which 1 were waited for; matrix products, arithmetic and copies ran while one was open for 0% of the time, Pallas kernels for 10%

profile of v6, /device:TPU:0, one launch (start us, length us, event | category | flops | bytes accessed | tf_op | source)
XLA Modules:
  0.0 454.4 jit_solution(17680722760324045396)
XLA Ops:
  7.2 0.0 reduce-scatter.2.cloned.1.call-start
  7.2 1.4 broadcast_in_dim.31.gain_ref
  8.6 1.5 copy.30.dtw_ref
  10.1 1.3 broadcast_in_dim.25.cbi_ref
  11.4 1.3 broadcast_in_dim.26.ggn_ref
  13.3 1.3 maximum_bitcast_fusion.hds_ref
  14.6 156.5 %gather_scan.1 = (bf16[2048,2048]{1,0:T(8,128)(2,1)}, bf16[2048,2048]{1,0:T(8,128)(2,1)}, bf16[2048,2432]{1,0:T(8,128)(2,1)}, bf16[1024,2048]{1,0:T(8,128)(2,1)}...) custom-call(bf16[512,2048]{1,0:T(8,128)(2,1)} %bitcast.26, ...), custom_call_target="tpu_custom_call" | custom-call | flops 28991029248 | bytes 36700160 | tf_op jit(solution)/shard_map/gather_scan/pallas_call | solution.py:1447
  171.1 0.6 broadcast_in_dim.28.mask_ref
  171.7 82.6 %mid.1 = (bf16[512,2048]{1,0:T(8,128)(2,1)}, bf16[2,64,2048]{2,1,0:T(8,128)(2,1)}, bf16[2048,1024]{1,0:T(8,128)(2,1)}, bf16[2048,1024]{1,0:T(8,128)(2,1)}, bf16[2048,1024]{1,0:T(8,128)(2,1)}) custom-call(bf16[2048,1024]{1,0:T(8,128)(2,1)} %get-tuple-element.48.gg_ref, bf16[1024,2048]{1,0:T(8,128)(2,1)} %get-tuple-element.49.wo_ref, ...), custom_call_target="tpu_custom_call" | custom-call | flops 25769803776 | bytes 58720256 | tf_op jit(solution)/shard_map/mid/pallas_call | solution.py:1563
  254.3 0.0 reduce-scatter.2.cloned.1.call-update
  254.3 46.5 %scan_back.1 = (bf16[2048,1408]{1,0:T(8,128)(2,1)}, f32[8,1280]{1,0:T(8,128)}, bf16[4,2,64,2048]{3,2,1,0:T(8,128)(2,1)}) custom-call(bf16[2048,1280]{1,0:T(8,128)(2,1)} %get-tuple-element.52.act_ref, f32[2048,128]{1,0:T(8,128)} %get-tuple-element.53.aux_ref, bf16[2048,1024]{1,0:T(8,128)(2,1)} %get-tuple-element.60.dy_ref, ...), custom_call_target="tpu_custom_call" | custom-call | flops 12884901888 | bytes 50331648 | tf_op jit(solution)/shard_map/scan_back/pallas_call | solution.py:1611
  300.8 2.9 reduce-scatter.2.cloned.1.call-done.gate_ref
  303.7 120.0 %weight_grads.1 = (bf16[512,2048]{1,0:T(8,128)(2,1)}, bf16[4,256,1024]{2,1,0:T(8,128)(2,1)}, bf16[4,256,1408]{2,1,0:T(8,128)(2,1)}, bf16[8,64,2048]{2,1,0:T(8,128)(2,1)}) custom-call(bf16[2048,1024]{1,0:T(8,128)(2,1)} %get-tuple-element.59.dpg_ref, bf16[2048,1408]{1,0:T(8,128)(2,1)} %get-tuple-element.67.dp_ref, bf16[2048,2432]{1,0:T(8,128)(2,1)} %get-tuple-element.68.w_ref, ...), custom_call_target="tpu_custom_call" | custom-call | flops 40802189312 | bytes 39845888 | tf_op jit(solution)/shard_map/weight_grads/pallas_call | solution.py:1643
  423.7 1.0 bitcast_convert_fusion
  424.8 0.1 copy.36
  424.9 0.1 reshape.66
  425.0 0.1 slice_reduce_fusion.1
  425.1 0.1 fusion
  425.2 0.6 slice.46
  425.8 0.6 slice_reduce_fusion.2
  426.4 0.1 reshape_squeeze.3
  426.5 0.1 reduce_sum.19
  426.6 0.1 stack.12
  426.7 0.1 stack.10
  426.8 0.1 stack.11
  426.9 0.1 constant_dynamic-slice_fusion
  426.9 0.5 slice_bitcast_fusion
  427.5 0.0 copy-start
  427.5 16.7 %finish.1 = (f32[256,8448]{1,0:T(8,128)}, f32[256,64]{1,0:T(8,128)}, f32[1,256]{1,0:T(1,128)}, f32[512,2048]{1,0:T(8,128)}, f32[1,512]{1,0:T(1,128)}, /*index=5*/bf16[512,2048]{1,0:T(8,128)(2,1)}, f32[512,2048]{1,0:T(8,128)}) custom-call(bf16[4,256,1024]{2,1,0:T(8,128)(2,1)} %get-tuple-element.72.gate_ref, bf16[4,256,1408]{2,1,0:T(8,128)(2,1)} %get-tuple-element.73.rest_ref, ...), custom_call_target="tpu_custom_call" | custom-call | flops 12976128 | bytes 34603008 | tf_op jit(solution)/shard_map/finish/pallas_call | solution.py:1704
  444.2 1.6 copy.34
  445.8 0.0 copy-done
  445.8 1.3 convert_divide_fusion
  (5 shorter events, 0.1 us)
Async XLA Ops:
  7.2 296.5 %reduce-scatter.2.cloned.1.call-start = ((), (), s32[]{:S(2)}) async-start(), calls=%async_computation.1 | async-start | bytes 4718592 | tf_op jit(solution)/shard_map/reduce_scatter | solution.py:1608
  427.5 18.4 %copy-start = (bf16[512]{0:T(512)(128)(2,1)S(1)}, bf16[512]{0:T(512)(128)(2,1)}, u32[]{:S(2)}) copy-start(bf16[512]{0:T(512)(128)(2,1)} %param.24) | copy-start | bytes 3076
Sparse Core Ops, SparseCore 0:
  254.4 49.2 reduce-scatter.1

commit v7 on v6

--- a/solution.py
+++ b/solution.py
@@ -1693,7 +1693,7 @@
         gate_rows = lax.all_gather(own_gate, "seq")
         rest_rows = lax.all_gather(lax.psum_scatter(wig, "head", scatter_dimension=0, tiled=True), "seq")
         tiny_all = lax.all_gather(lax.psum(sm, "head"), "seq")
-    strips = min(8, shard // 16)
+    strips = min(4, shard // 16)
 
     def strip(total, size):
         return pl.BlockSpec((total // strips, size), lambda j: (j, 0))

time: 463 us -> 461 us (level)
  no operation moved by 1% of the time
where the time goes in v7:
time: 461 us; the launch traced here: 452 us
  Pallas kernels  420 us (91%)
  between operations  15.2 us (3%)
  local copies, waits for them, and re-layouts  10.1 us (2%)
    pallas_call x1, Pallas kernels, local(): pl.pallas_call(functools.partial(gather_kernel, heads=heads, wide=wide),...  157 us
    pallas_call x1, Pallas kernels, local(): pl.pallas_call(grads_kernel, in_specs=[hbm] * 6 + [vmem], out_specs=[hbm]...  120 us
    pallas_call x1, Pallas kernels, local(): pl.pallas_call(functools.partial(mid_kernel, ring=ring), in_specs=[hbm] *...  82.6 us
    pallas_call x1, Pallas kernels, local(): pl.pallas_call(functools.partial(back_kernel, heads=heads, wide=wide, rin...  46.5 us
    pallas_call x1, Pallas kernels, local(): pl.pallas_call(functools.partial(finish_kernel, heads=heads, wide=wide),...  14.6 us
  transfers between devices with their start and end apart: 1, of which 1 were waited for; matrix products, arithmetic and copies ran while one was open for 0% of the time, Pallas kernels for 10%

profile of v7, /device:TPU:0, one launch (start us, length us, event | category | flops | bytes accessed | tf_op | source)
XLA Modules:
  0.0 452.3 jit_solution(14912339091748539636)
XLA Ops:
  7.2 0.0 reduce-scatter.2.cloned.1.call-start
  7.2 1.4 broadcast_in_dim.31.gain_ref
  8.6 1.5 copy.30.dtw_ref
  10.1 1.3 broadcast_in_dim.25.cbi_ref
  11.4 1.3 broadcast_in_dim.26.ggn_ref
  13.3 1.3 maximum_bitcast_fusion.hds_ref
  14.6 156.5 %gather_scan.1 = (bf16[2048,2048]{1,0:T(8,128)(2,1)}, bf16[2048,2048]{1,0:T(8,128)(2,1)}, bf16[2048,2432]{1,0:T(8,128)(2,1)}, bf16[1024,2048]{1,0:T(8,128)(2,1)}...) custom-call(bf16[512,2048]{1,0:T(8,128)(2,1)} %bitcast.26, ...), custom_call_target="tpu_custom_call" | custom-call | flops 28991029248 | bytes 36700160 | tf_op jit(solution)/shard_map/gather_scan/pallas_call | solution.py:1447
  171.1 0.6 broadcast_in_dim.28.mask_ref
  171.7 82.6 %mid.1 = (bf16[512,2048]{1,0:T(8,128)(2,1)}, bf16[2,64,2048]{2,1,0:T(8,128)(2,1)}, bf16[2048,1024]{1,0:T(8,128)(2,1)}, bf16[2048,1024]{1,0:T(8,128)(2,1)}, bf16[2048,1024]{1,0:T(8,128)(2,1)}) custom-call(bf16[2048,1024]{1,0:T(8,128)(2,1)} %get-tuple-element.48.gg_ref, bf16[1024,2048]{1,0:T(8,128)(2,1)} %get-tuple-element.49.wo_ref, ...), custom_call_target="tpu_custom_call" | custom-call | flops 25769803776 | bytes 58720256 | tf_op jit(solution)/shard_map/mid/pallas_call | solution.py:1563
  254.3 0.0 reduce-scatter.2.cloned.1.call-update
  254.3 46.5 %scan_back.1 = (bf16[2048,1408]{1,0:T(8,128)(2,1)}, f32[8,1280]{1,0:T(8,128)}, bf16[4,2,64,2048]{3,2,1,0:T(8,128)(2,1)}) custom-call(bf16[2048,1280]{1,0:T(8,128)(2,1)} %get-tuple-element.52.act_ref, f32[2048,128]{1,0:T(8,128)} %get-tuple-element.53.aux_ref, bf16[2048,1024]{1,0:T(8,128)(2,1)} %get-tuple-element.60.dy_ref, ...), custom_call_target="tpu_custom_call" | custom-call | flops 12884901888 | bytes 50331648 | tf_op jit(solution)/shard_map/scan_back/pallas_call | solution.py:1611
  300.8 2.9 reduce-scatter.2.cloned.1.call-done.gate_ref
  303.7 120.0 %weight_grads.1 = (bf16[512,2048]{1,0:T(8,128)(2,1)}, bf16[4,256,1024]{2,1,0:T(8,128)(2,1)}, bf16[4,256,1408]{2,1,0:T(8,128)(2,1)}, bf16[8,64,2048]{2,1,0:T(8,128)(2,1)}) custom-call(bf16[2048,1024]{1,0:T(8,128)(2,1)} %get-tuple-element.59.dpg_ref, bf16[2048,1408]{1,0:T(8,128)(2,1)} %get-tuple-element.67.dp_ref, bf16[2048,2432]{1,0:T(8,128)(2,1)} %get-tuple-element.68.w_ref, ...), custom_call_target="tpu_custom_call" | custom-call | flops 40802189312 | bytes 39845888 | tf_op jit(solution)/shard_map/weight_grads/pallas_call | solution.py:1643
  423.7 1.0 bitcast_convert_fusion
  424.8 0.1 copy.36
  424.9 0.1 reshape.66
  425.0 0.1 slice_reduce_fusion.1
  425.1 0.1 fusion
  425.2 0.6 slice.46
  425.8 0.6 slice_reduce_fusion.2
  426.4 0.1 reshape_squeeze.3
  426.5 0.1 reduce_sum.19
  426.6 0.1 stack.12
  426.7 0.1 stack.10
  426.8 0.1 stack.11
  426.9 0.1 constant_dynamic-slice_fusion
  426.9 0.5 slice_bitcast_fusion
  427.5 0.0 copy-start
  427.5 14.6 %finish.1 = (f32[256,8448]{1,0:T(8,128)}, f32[256,64]{1,0:T(8,128)}, f32[1,256]{1,0:T(1,128)}, f32[512,2048]{1,0:T(8,128)}, f32[1,512]{1,0:T(1,128)}, /*index=5*/bf16[512,2048]{1,0:T(8,128)(2,1)}, f32[512,2048]{1,0:T(8,128)}) custom-call(bf16[4,256,1024]{2,1,0:T(8,128)(2,1)} %get-tuple-element.72.gate_ref, bf16[4,256,1408]{2,1,0:T(8,128)(2,1)} %get-tuple-element.73.rest_ref, ...), custom_call_target="tpu_custom_call" | custom-call | flops 12976128 | bytes 34603008 | tf_op jit(solution)/shard_map/finish/pallas_call | solution.py:1704
  442.1 1.6 copy.34
  443.7 0.0 copy-done
  443.7 1.3 convert_divide_fusion
  (5 shorter events, 0.1 us)
Async XLA Ops:
  7.2 296.5 %reduce-scatter.2.cloned.1.call-start = ((), (), s32[]{:S(2)}) async-start(), calls=%async_computation.1 | async-start | bytes 4718592 | tf_op jit(solution)/shard_map/reduce_scatter | solution.py:1608
  427.5 16.2 %copy-start = (bf16[512]{0:T(512)(128)(2,1)S(1)}, bf16[512]{0:T(512)(128)(2,1)}, u32[]{:S(2)}) copy-start(bf16[512]{0:T(512)(128)(2,1)} %param.24) | copy-start | bytes 3076
Sparse Core Ops, SparseCore 0:
  254.4 49.2 reduce-scatter.1
